TPU v7x, 128 devices: a whole 4x4x4 slice. The times are simulated.
128 devices in a mesh: grp: 2 (over y_lo), dap: 64 (over z, x, y_hi, core).
Axes of the slice: x: 4, y: 4 (y_hi: 2, y_lo: 2; y = y_hi * 2 + y_lo), z: 4, core: 2. Of those that a mesh axis runs over, the one named last changes fastest.
Arguments:
- homolog_matrix: bfloat16 [512, 512, 256], P(('grp', 'dap')), may hold values from -6 to 6
- pair_state: bfloat16 [512, 512, 128], P('dap', 'grp'), may hold values from -6 to 6
- alignment_entry_mask: int32 [512, 512], P(('grp', 'dap')), may hold values 0 or 1
- residue_chain_index: int32 [512], replicated, may hold values from 0 to 3, as said below
- horizontal_scale_vector: float32 [256], replicated, may hold values from 0.1 to 1.9
- pair_norm_gain: float32 [128], replicated, may hold values from 0.1 to 1.9
- pair_bias_weight: bfloat16 [8, 128], replicated, may hold values from -15 to 15
- interchain_bias: float32 [8], replicated, may hold values from -2 to 2
- horizontal_query_projector: bfloat16 [256, 1024], replicated, may hold values from -0.375 to 0.375
- horizontal_final_projector: bfloat16 [256, 256], replicated, may hold values from -0.375 to 0.375
- vertical_scale_vector: float32 [256], replicated, may hold values from 0.1 to 1.9
- column_input_weight: bfloat16 [256, 1024], replicated, may hold values from -7 to 7
- vertical_final_projector: bfloat16 [256, 256], replicated, may hold values from -0.375 to 0.375
- feedforward_scale_vector: float32 [256], replicated, may hold values from 0.1 to 1.9
- feedforward_expand_matrix: bfloat16 [256, 1024], replicated, may hold values from -0.375 to 0.375
- feedforward_shrink_matrix: bfloat16 [1024, 256], replicated, may hold values from -0.1875 to 0.1875
Outputs:
- msa_out: bfloat16 [512, 512, 256], P(('grp', 'dap'))
Inputs may be any that keep to these rules, and one draw needn't show every extreme that they name: residue_chain_index never falls along the residues; each of the four chains is one run of residues.
All inputs are finite; a program needn't handle non-finite values. No bound on the sum of `alignment_entry_mask` on one device may be relied on, other than what follows from the above.
Results may differ from a plain program's by a relative error of at most 0.0095.
The roundings to bfloat16 on the way count: a program that leaves them out, or rounds other values in their place, can miss the bound.
Values may be sent and summed in bfloat16 or wider, within the bound.
No kernel may reach another device: no remote copies, remote signals or barrier semaphores. Data moves between devices by JAX's collectives and lax.ppermute only.
A program may use at most 128 MiB of HBM per device.

v0:
```python
import jax
import jax.numpy as jnp
from jax import lax
from jax.sharding import PartitionSpec as P

EPSILON = 1e-05
NEGATIVE_FILL = 1000000000.0


def layer_norm_apply(field, gain):
    field = field.astype(jnp.float32)
    average = jnp.mean(field, axis=-1, keepdims=True)
    center = field - average
    spread = jnp.mean(center * center, axis=-1, keepdims=True)
    return center * lax.rsqrt(spread + EPSILON) * gain


def attend(query_rows, key_rows, bias_term, key_mask_term, out_weight, head_count):
    channel_width = out_weight.shape[0]
    head_size = channel_width // head_count
    row_count = query_rows.shape[0]
    key_count = key_rows.shape[0]
    queries = query_rows[:, :channel_width].reshape(row_count, head_count, head_size)
    gates = query_rows[:, 3 * channel_width :].astype(jnp.float32)
    keys_all = key_rows[:, channel_width : 2 * channel_width].reshape(
        key_count, head_count, head_size
    )
    attended_vectors = key_rows[:, 2 * channel_width : 3 * channel_width].reshape(
        key_count, head_count, head_size
    )
    scores = jnp.einsum(
        "qhd,khd->hqk", queries, keys_all, preferred_element_type=jnp.float32
    ) * head_size ** (-0.5)
    scores = scores + bias_term + key_mask_term[None, None, :]
    highest = jnp.max(scores, axis=-1, keepdims=True)
    powers = jnp.exp(scores - highest)
    weights = (powers / jnp.sum(powers, axis=-1, keepdims=True)).astype(jnp.bfloat16)
    blended = jnp.einsum(
        "hqk,khd->qhd", weights, attended_vectors, preferred_element_type=jnp.float32
    ).reshape(row_count, channel_width)
    gated = (blended * jax.nn.sigmoid(gates)).astype(jnp.bfloat16)
    return jnp.dot(gated, out_weight, preferred_element_type=jnp.float32)


def body(
    homolog_matrix,
    pair_state,
    alignment_entry_mask,
    residue_chain_index,
    horizontal_scale_vector,
    pair_norm_gain,
    pair_bias_weight,
    interchain_bias,
    horizontal_query_projector,
    horizontal_final_projector,
    vertical_scale_vector,
    column_input_weight,
    vertical_final_projector,
    feedforward_scale_vector,
    feedforward_expand_matrix,
    feedforward_shrink_matrix,
):
    head_count = pair_bias_weight.shape[0]
    local_sequence_rows, residue_positions, channel_width = homolog_matrix.shape
    groups = lax.axis_size("grp")
    dap_count = lax.axis_size("dap")
    pair_rows = pair_state.shape[0]
    pair_cols = pair_state.shape[1]
    row_offset = lax.axis_index("dap") * pair_rows
    col_offset = lax.axis_index("grp") * pair_cols
    pair_normed = layer_norm_apply(pair_state, pair_norm_gain).astype(jnp.bfloat16)
    local_bias = jnp.einsum(
        "ijc,hc->hij", pair_normed, pair_bias_weight, preferred_element_type=jnp.float32
    )
    chain_rows = lax.dynamic_slice_in_dim(residue_chain_index, row_offset, pair_rows)
    chain_cols = lax.dynamic_slice_in_dim(residue_chain_index, col_offset, pair_cols)
    cross_pairs = (chain_rows[:, None] != chain_cols[None, :]).astype(jnp.float32)
    local_bias = (local_bias + interchain_bias[:, None, None] * cross_pairs[None]).astype(
        jnp.bfloat16
    )
    bias_strip = lax.all_gather(local_bias, "grp", axis=2, tiled=True)
    row_input_normed = layer_norm_apply(homolog_matrix, horizontal_scale_vector).astype(
        jnp.bfloat16
    )
    packed = jnp.dot(
        row_input_normed.reshape(-1, channel_width),
        horizontal_query_projector,
        preferred_element_type=jnp.float32,
    )
    packed = packed.astype(jnp.bfloat16).reshape(
        local_sequence_rows, residue_positions, 4 * channel_width
    )
    key_mask_term = (alignment_entry_mask.astype(jnp.float32) - 1.0) * NEGATIVE_FILL
    full_bias = lax.all_gather(bias_strip, "dap", axis=1, tiled=True)
    bias_term = full_bias.astype(jnp.float32)

    def per_sequence(inputs):
        seq_packed, seq_mask = inputs
        return attend(
            seq_packed, seq_packed, bias_term, seq_mask, horizontal_final_projector, head_count
        )

    row_update_terms = lax.map(per_sequence, (packed, key_mask_term))
    alignment_after_rows = (homolog_matrix.astype(jnp.float32) + row_update_terms).astype(
        jnp.bfloat16
    )
    mask_present_flag = alignment_entry_mask.astype(jnp.bfloat16)
    residue_window = residue_positions // (groups * dap_count)
    column_alignment, column_entry_mask = (
        lax.all_to_all(
            alignment_after_rows, ("grp", "dap"), split_axis=1, concat_axis=0, tiled=True
        ),
        lax.all_to_all(mask_present_flag, ("grp", "dap"), split_axis=1, concat_axis=0, tiled=True),
    )
    sequence_positions = column_alignment.shape[0]
    column_input_normed = layer_norm_apply(column_alignment, vertical_scale_vector).astype(
        jnp.bfloat16
    )
    col_packed = jnp.dot(
        column_input_normed.reshape(-1, channel_width),
        column_input_weight,
        preferred_element_type=jnp.float32,
    )
    col_packed = col_packed.astype(jnp.bfloat16).reshape(
        sequence_positions, residue_window, 4 * channel_width
    )
    col_key_term = (column_entry_mask.astype(jnp.float32) - 1.0) * NEGATIVE_FILL

    def per_residue(inputs):
        res_packed, res_mask = inputs
        return attend(res_packed, res_packed, 0.0, res_mask, vertical_final_projector, head_count)

    column_update_terms = lax.map(
        per_residue, (jnp.swapaxes(col_packed, 0, 1), jnp.swapaxes(col_key_term, 0, 1))
    )
    alignment_after_columns = (
        column_alignment.astype(jnp.float32) + jnp.swapaxes(column_update_terms, 0, 1)
    ).astype(jnp.bfloat16)
    transition_input_normed = (
        layer_norm_apply(alignment_after_columns, feedforward_scale_vector)
        .astype(jnp.bfloat16)
        .reshape(-1, channel_width)
    )
    hidden = jax.nn.relu(
        jnp.dot(
            transition_input_normed, feedforward_expand_matrix, preferred_element_type=jnp.float32
        )
    ).astype(jnp.bfloat16)
    residual_update = jnp.dot(hidden, feedforward_shrink_matrix, preferred_element_type=jnp.float32)
    alignment_after_transition = (
        alignment_after_columns.astype(jnp.float32).reshape(-1, channel_width) + residual_update
    ).astype(jnp.bfloat16)
    alignment_after_transition = alignment_after_transition.reshape(
        sequence_positions, residue_window, channel_width
    )
    return lax.all_to_all(
        alignment_after_transition, ("grp", "dap"), split_axis=0, concat_axis=1, tiled=True
    )


def solution(mesh):
    return jax.shard_map(
        body,
        mesh=mesh,
        in_specs=(
            P(("grp", "dap"), None, None),
            P("dap", "grp", None),
            P(("grp", "dap"), None),
            P(),
            P(),
            P(),
            P(),
            P(),
            P(),
            P(),
            P(),
            P(),
            P(),
            P(),
            P(),
            P(),
        ),
        out_specs=P(("grp", "dap"), None, None),
        check_vma=False,
    )
```

profile of v0, /device:TPU:1, one launch (start us, length us, event | category | flops | bytes accessed | tf_op | source)
XLA Modules:
  0.0 333.5 jit_solution(10805586738203221690)
XLA Ops:
  18.3 12.0 %all-to-all-start.1 = ((bf16[4,128,4]{2,0,1:T(4,128)(2,1)}), bf16[4,128,4]{2,0,1:T(4,128)(2,1)S(1)}, u32[]{:S(2)}, u32[]{:S(2)}) async-start(bf16[4,128,4]{2,0,1:T(4,128)(2,1)} %copy.72), calls=%async_computation.1 | async-start | bytes 262144 | tf_op jit(solution)/shard_map/all_to_all | solution.py:113
  35.3 58.3 %all-gather.2.cloned.1.call-done = bf16[8,512,512]{2,0,1:T(8,128)(2,1)} async-done(((bf16[8,8,512]{2,0,1:T(8,128)(2,1)}), bf16[8,512,512]{2,0,1:T(8,128)(2,1)}) %all-gather.2.cloned.1.call-update) | async-done | bytes 4194320 | tf_op jit(solution)/shard_map/all_gather | solution.py:94
  93.6 8.7 %copy.67 = f32[8,512,512]{1,2,0:T(8,128)} copy(bf16[8,512,512]{2,0,1:T(8,128)(2,1)} %all-gather.2.cloned.1.call-done) | data formatting | bytes 12582912 | tf_op jit(solution)/shard_map/while | solution.py:103
  103.8 74.1 %while.20 = (s32[]{:T(128)}, f32[4,512,256]{2,1,0:T(8,128)}, bf16[4,512,1024]{2,1,0:T(8,128)(2,1)}, f32[8,512,512]{1,2,0:T(8,128)}, f32[4,512]{1,0:T(4,128)S(1)}, /*index=5*/bf16[256,256]{1,0:T(8,128)(2,1)S(1)}, s32[]{:T(128)}) while((s32[]{:T(128)}, f32[4,512,256]{2,1,0:T(8,128)}, bf16[4,512,1024]{2,1,0:T(8,128)(2,1)}, ...), condition=%wide.region_7.8_spmd, body=%wide.region_4.7_spmd.sunk | while | flops 353113088 | bytes 76192368 | solution.py:103
  105.7 5.2 %add_add_fusion.2 = f32[8,512,512]{1,2,0:T(8,128)S(1)} fusion(f32[8,512,512]{1,2,0:T(8,128)} %get-tuple-element.229, f32[512]{0:T(512)S(1)} %bitcast.158, bf16[512,8,32]{0,2,1:T(8,128)(2,1)S(1)} %bitcast.148, bf16[512,8,32]{0,2,1:T(8,128)(2,1)S(1)} %bitcast.147), kind=kOutput, calls=%fused_computation.3.clone.1 | convolution fusion | flops 140509184 | bytes 17303552 | tf_op jit(solution)/shard_map/while/body/eval_jaxpr/qhd,khd->hqk/dot_general | solution.py:31
  114.1 6.9 %fusion.96 = f32[8,32,512]{2,1,0:T(8,128)S(1)} fusion(bf16[512,8,32]{0,2,1:T(8,128)(2,1)S(1)} %bitcast.153, f32[8,512]{1,0:T(8,128)S(1)} %fusion.95, f32[8,512,512]{1,2,0:T(8,128)} %copy-done.2), kind=kOutput, calls=%fused_computation.4.clone.1 | convolution fusion | flops 140513792 | bytes 9191424 | tf_op jit(solution)/shard_map/while/body/eval_jaxpr/hqk,khd->qhd/dot_general | solution.py:38
  124.2 5.2 %add_add_fusion.2 = f32[8,512,512]{1,2,0:T(8,128)S(1)} fusion(f32[8,512,512]{1,2,0:T(8,128)} %get-tuple-element.229, f32[512]{0:T(512)S(1)} %bitcast.158, bf16[512,8,32]{0,2,1:T(8,128)(2,1)S(1)} %bitcast.148, bf16[512,8,32]{0,2,1:T(8,128)(2,1)S(1)} %bitcast.147), kind=kOutput, calls=%fused_computation.3.clone.1 | convolution fusion | flops 140509184 | bytes 17303552 | tf_op jit(solution)/shard_map/while/body/eval_jaxpr/qhd,khd->hqk/dot_general | solution.py:31
  132.6 6.9 %fusion.96 = f32[8,32,512]{2,1,0:T(8,128)S(1)} fusion(bf16[512,8,32]{0,2,1:T(8,128)(2,1)S(1)} %bitcast.153, f32[8,512]{1,0:T(8,128)S(1)} %fusion.95, f32[8,512,512]{1,2,0:T(8,128)} %copy-done.2), kind=kOutput, calls=%fused_computation.4.clone.1 | convolution fusion | flops 140513792 | bytes 9191424 | tf_op jit(solution)/shard_map/while/body/eval_jaxpr/hqk,khd->qhd/dot_general | solution.py:38
  142.8 5.2 %add_add_fusion.2 = f32[8,512,512]{1,2,0:T(8,128)S(1)} fusion(f32[8,512,512]{1,2,0:T(8,128)} %get-tuple-element.229, f32[512]{0:T(512)S(1)} %bitcast.158, bf16[512,8,32]{0,2,1:T(8,128)(2,1)S(1)} %bitcast.148, bf16[512,8,32]{0,2,1:T(8,128)(2,1)S(1)} %bitcast.147), kind=kOutput, calls=%fused_computation.3.clone.1 | convolution fusion | flops 140509184 | bytes 17303552 | tf_op jit(solution)/shard_map/while/body/eval_jaxpr/qhd,khd->hqk/dot_general | solution.py:31
  151.2 6.9 %fusion.96 = f32[8,32,512]{2,1,0:T(8,128)S(1)} fusion(bf16[512,8,32]{0,2,1:T(8,128)(2,1)S(1)} %bitcast.153, f32[8,512]{1,0:T(8,128)S(1)} %fusion.95, f32[8,512,512]{1,2,0:T(8,128)} %copy-done.2), kind=kOutput, calls=%fused_computation.4.clone.1 | convolution fusion | flops 140513792 | bytes 9191424 | tf_op jit(solution)/shard_map/while/body/eval_jaxpr/hqk,khd->qhd/dot_general | solution.py:38
  161.3 5.2 %add_add_fusion.2 = f32[8,512,512]{1,2,0:T(8,128)S(1)} fusion(f32[8,512,512]{1,2,0:T(8,128)} %get-tuple-element.229, f32[512]{0:T(512)S(1)} %bitcast.158, bf16[512,8,32]{0,2,1:T(8,128)(2,1)S(1)} %bitcast.148, bf16[512,8,32]{0,2,1:T(8,128)(2,1)S(1)} %bitcast.147), kind=kOutput, calls=%fused_computation.3.clone.1 | convolution fusion | flops 140509184 | bytes 17303552 | tf_op jit(solution)/shard_map/while/body/eval_jaxpr/qhd,khd->hqk/dot_general | solution.py:31
  169.7 6.9 %fusion.96 = f32[8,32,512]{2,1,0:T(8,128)S(1)} fusion(bf16[512,8,32]{0,2,1:T(8,128)(2,1)S(1)} %bitcast.153, f32[8,512]{1,0:T(8,128)S(1)} %fusion.95, f32[8,512,512]{1,2,0:T(8,128)} %copy-done.2), kind=kOutput, calls=%fused_computation.4.clone.1 | convolution fusion | flops 140513792 | bytes 9191424 | tf_op jit(solution)/shard_map/while/body/eval_jaxpr/hqk,khd->qhd/dot_general | solution.py:38
  181.8 5.1 %all-to-all-start = ((bf16[4,512,256]{2,0,1:T(4,128)(2,1)}), bf16[4,512,256]{2,0,1:T(4,128)(2,1)}, u32[]{:S(2)}, u32[]{:S(2)}) async-start(bf16[4,512,256]{2,0,1:T(4,128)(2,1)} %copy.68), calls=%async_computation | async-start | bytes 2097152 | tf_op jit(solution)/shard_map/all_to_all | solution.py:110
  187.4 18.1 %all-to-all-done = bf16[4,512,256]{2,0,1:T(4,128)(2,1)} async-done(((bf16[4,512,256]{2,0,1:T(4,128)(2,1)}), bf16[4,512,256]{2,0,1:T(4,128)(2,1)}, u32[]{:S(2)}, u32[]{:S(2)}) %all-to-all-start) | async-done | bytes 1048608 | tf_op jit(solution)/shard_map/all_to_all | solution.py:110
  217.1 7.2 %reshape.174 = bf16[512,4,1024]{2,1,0:T(4,128)(2,1)} reshape(bf16[2048,1024]{1,0:T(8,128)(2,1)} %convolution_convert_fusion) | data formatting | bytes 8388608 | tf_op jit(solution)/shard_map/reshape | solution.py:124
  224.3 7.5 %copy.71 = bf16[512,4,1024]{0,2,1:T(8,128)(2,1)} copy(bf16[512,4,1024]{2,1,0:T(4,128)(2,1)} %reshape.174) | data formatting | bytes 8388608 | tf_op jit(solution)/shard_map/reshape | solution.py:124
  233.4 48.4 %while.21 = (s32[]{:T(128)}, f32[4,512,256]{2,1,0:T(8,128)}, bf16[4,512,1024]{1,2,0:T(8,128)(2,1)}, f32[4,512]{1,0:T(4,128)S(1)}, bf16[256,256]{1,0:T(8,128)(2,1)S(1)}, /*index=5*/s32[]{:T(128)}) while((s32[]{:T(128)}, f32[4,512,256]{2,1,0:T(8,128)}, bf16[4,512,1024]{1,2,0:T(8,128)(2,1)}, f32[4,512]{1,0:T(4,128)S(1)}, ...), condition=%wide.region_13.14_spmd, body=%wide.region_10.13_spmd.sunk | while | flops 348914176 | bytes 23763532 | solution.py:133
  234.7 5.2 %fusion.105 = (f32[8,512]{1,0:T(8,128)S(1)}, f32[8,512,512]{1,2,0:T(8,128)}) fusion(f32[512]{0:T(512)S(1)} %bitcast.159, bf16[512,8,32]{0,2,1:T(8,128)(2,1)S(1)} %bitcast.155, bf16[512,8,32]{0,2,1:T(8,128)(2,1)S(1)} %bitcast.154), kind=kOutput, calls=%fused_computation.85.clone.1 | convolution fusion | flops 142606848 | bytes 8931328 | tf_op jit(solution)/shard_map/while/body/eval_jaxpr/sub | solution.py:36
  240.0 4.2 %fusion.106 = f32[8,32,512]{2,1,0:T(8,128)S(1)} fusion(bf16[512,8,32]{0,2,1:T(8,128)(2,1)S(1)} %bitcast.152, f32[8,512,512]{1,2,0:T(8,128)} %get-tuple-element.210, f32[8,512]{1,0:T(8,128)S(1)} %get-tuple-element.211), kind=kOutput, calls=%fused_computation.19.clone.1 | convolution fusion | flops 138412032 | bytes 9191424 | tf_op jit(solution)/shard_map/while/body/eval_jaxpr/hqk,khd->qhd/dot_general | solution.py:38
  246.9 5.2 %fusion.105 = (f32[8,512]{1,0:T(8,128)S(1)}, f32[8,512,512]{1,2,0:T(8,128)}) fusion(f32[512]{0:T(512)S(1)} %bitcast.159, bf16[512,8,32]{0,2,1:T(8,128)(2,1)S(1)} %bitcast.155, bf16[512,8,32]{0,2,1:T(8,128)(2,1)S(1)} %bitcast.154), kind=kOutput, calls=%fused_computation.85.clone.1 | convolution fusion | flops 142606848 | bytes 8931328 | tf_op jit(solution)/shard_map/while/body/eval_jaxpr/sub | solution.py:36
  259.0 5.2 %fusion.105 = (f32[8,512]{1,0:T(8,128)S(1)}, f32[8,512,512]{1,2,0:T(8,128)}) fusion(f32[512]{0:T(512)S(1)} %bitcast.159, bf16[512,8,32]{0,2,1:T(8,128)(2,1)S(1)} %bitcast.155, bf16[512,8,32]{0,2,1:T(8,128)(2,1)S(1)} %bitcast.154), kind=kOutput, calls=%fused_computation.85.clone.1 | convolution fusion | flops 142606848 | bytes 8931328 | tf_op jit(solution)/shard_map/while/body/eval_jaxpr/sub | solution.py:36
  271.0 5.2 %fusion.105 = (f32[8,512]{1,0:T(8,128)S(1)}, f32[8,512,512]{1,2,0:T(8,128)}) fusion(f32[512]{0:T(512)S(1)} %bitcast.159, bf16[512,8,32]{0,2,1:T(8,128)(2,1)S(1)} %bitcast.155, bf16[512,8,32]{0,2,1:T(8,128)(2,1)S(1)} %bitcast.154), kind=kOutput, calls=%fused_computation.85.clone.1 | convolution fusion | flops 142606848 | bytes 8931328 | tf_op jit(solution)/shard_map/while/body/eval_jaxpr/sub | solution.py:36
  297.3 4.4 %fusion.15 = bf16[2048,256]{1,0:T(8,128)(2,1)S(1)} fusion(f32[2048,256]{1,0:T(8,128)} %reshape.175, bf16[1024,256]{1,0:T(8,128)(2,1)S(1)} %copy-done.11, bf16[2048,256]{1,0:T(8,128)(2,1)} %reshape.176, bf16[256,1024]{1,0:T(8,128)(2,1)S(1)} %copy-done.12), kind=kOutput, calls=%fused_computation.35 | convolution fusion | flops 2152726528 | bytes 5242880 | tf_op jit(solution)/shard_map/dot_general | solution.py:149
  302.0 23.2 %all_to_all.40 = bf16[512,4,256]{2,1,0:T(4,128)(2,1)S(1)} all-to-all(bf16[512,4,256]{2,1,0:T(4,128)(2,1)S(1)} %reshape.177), channel_id=1, replica_groups=mesh['grp'=2,'dap'=64] {'grp','dap'}, dimensions={0} | all-to-all | bytes 2097152 | tf_op jit(solution)/shard_map/all_to_all | solution.py:156
  (138 shorter events, 101.3 us)
Async XLA Ops:
  6.5 25.6 %copy-start = (bf16[256,1024]{1,0:T(8,128)(2,1)S(1)}, bf16[256,1024]{1,0:T(8,128)(2,1)}, u32[]{:S(2)}) copy-start(bf16[256,1024]{1,0:T(8,128)(2,1)} %param.28) | copy-start | bytes 1572868
  6.5 10.7 %copy-start.7 = (s32[4,512]{1,0:T(4,128)S(1)}, s32[4,512]{1,0:T(4,128)}, u32[]{:S(2)}) copy-start(s32[4,512]{1,0:T(4,128)} %param.22) | copy-start | bytes 24580
  6.5 23.8 %copy-start.3 = (bf16[4,512,256]{2,1,0:T(8,128)(2,1)S(1)}, bf16[4,512,256]{2,1,0:T(8,128)(2,1)}, u32[]{:S(2)}) copy-start(bf16[4,512,256]{2,1,0:T(8,128)(2,1)} %param.20) | copy-start | bytes 3145732
  6.5 87.0 %all-gather.2.cloned.1.call-start = ((), (), s32[]{:S(2)}) async-start(), calls=%async_computation.3 | async-start | bytes 4259840 | tf_op jit(solution)/shard_map/all_gather | solution.py:94
  11.2 20.1 %copy-start.9 = (f32[256]{0:T(256)S(1)}, f32[256]{0:T(256)}, u32[]{:S(2)}) copy-start(f32[256]{0:T(256)} %param.24) | copy-start | bytes 3076
  18.3 163.5 %all-to-all-start.1 = ((bf16[4,128,4]{2,0,1:T(4,128)(2,1)}), bf16[4,128,4]{2,0,1:T(4,128)(2,1)S(1)}, u32[]{:S(2)}, u32[]{:S(2)}) async-start(bf16[4,128,4]{2,0,1:T(4,128)(2,1)} %copy.72), calls=%async_computation.1 | async-start | bytes 262144 | tf_op jit(solution)/shard_map/all_to_all | solution.py:113
  102.3 1.5 copy-start.4
  110.9 3.2 copy-start.2
  129.4 3.2 copy-start.2
  148.0 3.2 copy-start.2
  166.5 3.2 copy-start.2
  181.8 23.7 %all-to-all-start = ((bf16[4,512,256]{2,0,1:T(4,128)(2,1)}), bf16[4,512,256]{2,0,1:T(4,128)(2,1)}, u32[]{:S(2)}, u32[]{:S(2)}) async-start(bf16[4,512,256]{2,0,1:T(4,128)(2,1)} %copy.68), calls=%async_computation | async-start | bytes 2097152 | tf_op jit(solution)/shard_map/all_to_all | solution.py:110
  212.1 2.1 copy-start.6
  212.1 2.1 copy-start.8
  231.8 1.5 copy-start.5
  289.2 1.5 copy-start.10
  295.4 1.9 copy-start.11
  295.4 1.9 copy-start.12
  325.2 1.5 copy-start.1
Sparse Core Ops, SparseCore 0:
  17.3 76.1 all-gather.1
where the time goes:
time: 335 us; the launch traced here: 333 us
  matrix products  107 us (32%)
  waiting for transfers between devices  76.4 us (23%)
  local copies, waits for them, and re-layouts  67.7 us (20%)
  blocking collectives  27.4 us (8%)
  other arithmetic  23.5 us (7%)
  starting transfers between devices  17.1 us (5%)
  between operations  13.7 us (4%)
    all_gather x1, waiting for transfers between devices, body(): full_bias = lax.all_gather(bias_strip, 'dap', axis=1, tiled=True)  58.3 us
    dot_general x8, matrix products, attend(): jnp.einsum('hqk,khd->qhd', weights, attended_vectors, preferred_element_t...  44.6 us
    all_to_all x1, blocking collectives, body(): lax.all_to_all(alignment_after_transition, ('grp', 'dap'), split_axis=0,...  23.2 us
    sub x4, matrix products, attend(): powers = jnp.exp(scores - highest)  21 us
    dot_general x4, matrix products, attend(): jnp.einsum('qhd,khd->hqk', queries, keys_all, preferred_element_type=jnp....  20.7 us
    all_to_all x1, waiting for transfers between devices, body(): lax.all_to_all(alignment_after_rows, ('grp', 'dap'), split_axis=1, concat...  18.1 us
    reshape x2, local copies, waits for them, and re-layouts, body(): col_packed.astype(jnp.bfloat16)  14.7 us
    all_to_all x1, starting transfers between devices, body(): lax.all_to_all(mask_present_flag, ('grp', 'dap'), split_axis=1, concat_ax...  12 us
  transfers between devices with their start and end apart: 3, of which 2 were waited for; matrix products, arithmetic and copies ran while one was open for 26% of the time, Pallas kernels for 0%

commit v1 on v0

v1 whole, which is shorter than its diff:
```python
import functools
import math

import jax
import jax.numpy as jnp
import ml_dtypes
import numpy as np
from jax import lax
from jax.experimental import pallas as pl
from jax.experimental.pallas import tpu as pltpu
from jax.sharding import Mesh, PartitionSpec as P

EPSILON = 1e-05
HEADS = 8
HEAD = 32
WIDTH = 256
LENGTH = 512
HALF = 256
PEERS = 64
TILE_ROWS = 72
LOG2E = math.log2(math.e)
SCALE = HEAD**-0.5 * LOG2E
F32 = jnp.float32
BF16 = jnp.bfloat16
AXES = ("grp", "z", "x", "yh", "core")
PLANE = ("grp", "z", "x", "yh")
VMEM_LIMIT = 50 * 1024 * 1024

MASK_TERM = 1e9 * HEAD**0.5


def mask_parts():
    parts = []
    rest = MASK_TERM
    for _ in range(3):
        part = float(np.asarray(rest, ml_dtypes.bfloat16))
        parts.append(part)
        rest -= part
    return parts


def nt(a, b):
    return lax.dot_general(a, b, (((1,), (1,)), ((), ())), preferred_element_type=F32)


def tn(a, b):
    return lax.dot_general(a, b, (((0,), (0,)), ((), ())), preferred_element_type=F32)


def nn(a, b):
    return jnp.dot(a, b, preferred_element_type=F32)


def norm(x, gain):
    average = jnp.mean(x, axis=-1, keepdims=True)
    center = x - average
    spread = jnp.mean(center * center, axis=-1, keepdims=True)
    return (center * lax.rsqrt(spread + EPSILON) * gain).astype(BF16)


def position():
    q = (lax.axis_index("z") * 4 + lax.axis_index("x")) * 2 + lax.axis_index("yh")
    return lax.axis_index("grp"), q, lax.axis_index("core")


def bias_kernel(pair_ref, gain_ref, weight_ref, chain_s_ref, chain_v_ref, inter_ref, out_ref):
    grp, q, core = position()
    normed = norm(pair_ref[...].astype(F32), gain_ref[...])
    bias = nt(weight_ref[...], normed)
    chain_cols = chain_v_ref[pl.ds(grp, 1), :]
    inter = inter_ref[...]
    parts = []
    for ii in range(8):
        chain_row = chain_s_ref[16 * q + 8 * core + ii]
        cross = (chain_cols != chain_row).astype(F32)
        parts.append(bias[:, ii * 256 : (ii + 1) * 256] + inter * cross)
    stacked = jnp.stack(parts, axis=0)
    out_ref[...] = jnp.swapaxes(stacked, 0, 1).reshape(64, 256).astype(BF16)


def payload_kernel(bias_ref, own_ref, other_ref, out_ref):
    _, _, core = position()
    own = own_ref[...].astype(F32)
    other = other_ref[...].astype(F32)
    first = jnp.where(core == 0, own, other)
    second = jnp.where(core == 0, other, own)
    mask = jnp.concatenate([first, second], axis=0).astype(BF16)
    i = lax.broadcasted_iota(jnp.int32, (LENGTH, HALF), 0)
    l = lax.broadcasted_iota(jnp.int32, (LENGTH, HALF), 1)
    pick = (i == (l // 8) * 16 + core * 8 + l % 8).astype(F32).astype(BF16)
    rows = nn(mask, pick).astype(BF16)
    tile = jnp.concatenate([bias_ref[...].astype(F32), rows.astype(F32)], axis=0).astype(BF16)

    def put(p, carry):
        out_ref[p] = tile
        return carry

    lax.fori_loop(0, PEERS, put, 0)


def project_kernel(
    own_ref, other_ref, mask_ref, gain_ref, wk_ref, wt_ref, k_ref, vt_ref, qt_ref, gt_ref, xq_ref
):
    step = pl.program_id(0)
    _, _, core = position()
    x = jnp.where(step < 4, own_ref[0].astype(F32), other_ref[0].astype(F32))
    normed = norm(x, gain_ref[...])
    k_ref[0, :, :WIDTH] = nn(normed, wk_ref[...]).astype(BF16)
    lane = lax.broadcasted_iota(jnp.int32, (8, 128), 1)
    row = lax.broadcasted_iota(jnp.int32, (8, 128), 0)
    consts = mask_parts()
    pick = jnp.zeros((8, 128), F32)
    for at, value in enumerate(consts):
        pick = jnp.where((lane == at) & (row == step), value, pick)
    k_ref[0, :, WIDTH:] = nn(mask_ref[...] - 1, pick.astype(BF16)).astype(BF16)
    vt_ref[0] = nt(wt_ref[2 * WIDTH : 3 * WIDTH], normed).astype(BF16)

    def half(a):
        rows = a.reshape(32, 2, 8, WIDTH)
        return jnp.where(core == 0, rows[:, 0], rows[:, 1]).reshape(HALF, WIDTH)

    xq = half(x)
    xq_ref[0] = xq.astype(BF16)
    normed_q = half(normed.astype(F32)).astype(BF16)
    qt_ref[0] = nt(wt_ref[:WIDTH], normed_q).astype(BF16)
    gt_ref[0] = nt(wt_ref[3 * WIDTH :], normed_q).astype(BF16)


def attend(keys, mask_tile, vt, qt, bias, queries):
    ones_rows = jnp.ones((128, queries), BF16)
    ones_v = jnp.ones((16, LENGTH), BF16)
    augmented = [
        jnp.concatenate([keys[:, g * 128 : (g + 1) * 128], mask_tile], axis=1) for g in range(2)
    ]
    out = []
    for h in range(HEADS):
        group, at = divmod(h, 4)
        pieces = []
        if at:
            pieces.append(jnp.zeros((HEAD * at, queries), BF16))
        pieces.append(qt[h * HEAD : (h + 1) * HEAD])
        if at < 3:
            pieces.append(jnp.zeros((HEAD * (3 - at), queries), BF16))
        pieces.append(ones_rows)
        spread = jnp.concatenate(pieces, axis=0)
        scores = nn(augmented[group], spread) * SCALE
        if bias is not None:
            scores = scores + bias[h]
        highest = jnp.max(scores, axis=0, keepdims=True)
        powers = jnp.exp2(scores - highest).astype(BF16)
        values = jnp.concatenate([vt[h * HEAD : (h + 1) * HEAD], ones_v], axis=0)
        blended = nn(values, powers)
        out.append(blended[:HEAD] / blended[HEAD : HEAD + 1])
    return jnp.concatenate(out, axis=0)


def row_kernel(tile_ref, k_ref, vt_ref, qt_ref, gt_ref, xq_ref, wo_ref, out_ref, bias_ref, y_ref):
    step = pl.program_id(0)
    _, _, core = position()

    @pl.when(step == 0)
    def _():
        row = lax.broadcasted_iota(jnp.int32, (HALF, HALF), 0)
        col = lax.broadcasted_iota(jnp.int32, (HALF, HALF), 1)
        eye = (row == col).astype(F32).astype(BF16)
        for g in range(2):
            for pair in range(4):
                block = tile_ref[g * 32 : (g + 1) * 32, pair * 16 : (pair + 1) * 16, :]
                block = block.astype(F32).reshape(32, 2, 8, 256)
                for k in range(2):
                    rows = block[:, k].reshape(HALF, 256).astype(BF16)
                    bias_ref[pair * 2 + k, g * 256 : (g + 1) * 256, :] = nt(eye, rows) * LOG2E

    o = attend(k_ref[0, :, :WIDTH], k_ref[0, :, WIDTH:], vt_ref[0], qt_ref[0], bias_ref, HALF)
    gated = (o * jax.nn.sigmoid(gt_ref[0].astype(F32))).astype(BF16)
    y = xq_ref[0].astype(F32) + tn(gated, wo_ref[...])
    s = lax.rem(step + 4 * core, 8)
    for j in range(2):
        y_ref[j, pl.ds(s, HALF, stride=8), :] = y[:, j * 128 : (j + 1) * 128]

    @pl.when(step == 7)
    def _():
        for j in range(2):
            out_ref[:, j * 128 : (j + 1) * 128] = y_ref[j].astype(BF16)


def column_kernel(
    x_ref, mask_ref, gain_ref, wk_ref, wt_ref, wo_ref, gain2_ref, w1_ref, w2_ref, out_ref,
    x32_ref, y_ref,
):
    r = pl.program_id(0)
    grp, q, _ = position()
    peer = grp * 32 + q

    @pl.when(r == 0)
    def _():
        x32_ref[...] = x_ref[...].astype(F32).reshape(PEERS, 4, 8, WIDTH)

    x = x32_ref[:, r].reshape(LENGTH, WIDTH)
    normed = norm(x, gain_ref[...])
    keys = nn(normed, wk_ref[...]).astype(BF16)
    lane = lax.broadcasted_iota(jnp.int32, (HALF, 128), 1)
    row = lax.broadcasted_iota(jnp.int32, (HALF, 128), 0)
    pick = jnp.zeros((HALF, 128), F32)
    for at, value in enumerate(mask_parts()):
        pick = jnp.where((lane == at) & (row == 4 * peer + r), value, pick)
    mask_tile = nn(mask_ref[...] - 1, pick.astype(BF16)).astype(BF16)
    vt = nt(wt_ref[2 * WIDTH : 3 * WIDTH], normed).astype(BF16)
    qt = nt(wt_ref[:WIDTH], normed).astype(BF16)
    gt = nt(wt_ref[3 * WIDTH :], normed).astype(BF16)
    for part in range(2):
        cols = slice(part * HALF, (part + 1) * HALF)
        o = attend(keys, mask_tile, vt, qt[:, cols], None, HALF)
        gated = (o * jax.nn.sigmoid(gt[:, cols].astype(F32))).astype(BF16)
        one = x[cols] + tn(gated, wo_ref[...])
        two = one.astype(BF16).astype(F32)
        hidden = jnp.maximum(nn(norm(two, gain2_ref[...]), w1_ref[...]), 0.0).astype(BF16)
        y = two + nn(hidden, w2_ref[...])
        for j in range(2):
            y_ref[j, pl.ds(part * 4 * HALF + r, HALF, stride=4), :] = y[:, j * 128 : (j + 1) * 128]

    @pl.when(r == 3)
    def _():
        for j in range(2):
            out_ref[:, j * 128 : (j + 1) * 128] = y_ref[j].astype(BF16)


def whole(*shape):
    return pl.BlockSpec(shape, lambda i: (0,) * len(shape))


def each(*shape):
    return pl.BlockSpec((1,) + shape, lambda i: (i,) + (0,) * len(shape))


def body(
    homolog,
    pair_state,
    mask,
    chain,
    row_gain,
    pair_gain,
    pair_weight,
    interchain,
    row_in,
    row_out,
    col_gain,
    col_in,
    col_out,
    ff_gain,
    ff_expand,
    ff_shrink,
):
    params = pltpu.CompilerParams(vmem_limit_bytes=VMEM_LIMIT)
    swap = [(0, 1), (1, 0)]
    other_mask = lax.ppermute(mask, "core", swap)
    other = lax.ppermute(homolog, "core", swap)

    bias = pl.pallas_call(
        bias_kernel,
        out_shape=jax.ShapeDtypeStruct((64, 256), BF16),
        in_specs=[
            pl.BlockSpec(memory_space=pltpu.VMEM),
            pl.BlockSpec(memory_space=pltpu.VMEM),
            pl.BlockSpec(memory_space=pltpu.VMEM),
            pl.BlockSpec(memory_space=pltpu.SMEM),
            pl.BlockSpec(memory_space=pltpu.VMEM),
            pl.BlockSpec(memory_space=pltpu.VMEM),
        ],
        compiler_params=params,
    )(
        pair_state.reshape(2048, 128),
        pair_gain.reshape(1, 128),
        pair_weight,
        chain,
        chain.reshape(2, 256),
        interchain.reshape(8, 1),
    )
    payload = pl.pallas_call(
        payload_kernel,
        out_shape=jax.ShapeDtypeStruct((PEERS, TILE_ROWS, 256), BF16),
        compiler_params=params,
    )(bias, mask, other_mask)
    tiles = lax.all_to_all(payload, PLANE, 0, 0, tiled=True)

    row_in_t = row_in.T
    col_in_t = col_in.T
    mask_t = jnp.concatenate([mask, other_mask], axis=0).astype(BF16).T
    keys, vt, qt, gt, xq = pl.pallas_call(
        project_kernel,
        grid=(8,),
        out_shape=[
            jax.ShapeDtypeStruct((8, LENGTH, WIDTH + 128), BF16),
            jax.ShapeDtypeStruct((8, WIDTH, LENGTH), BF16),
            jax.ShapeDtypeStruct((8, WIDTH, HALF), BF16),
            jax.ShapeDtypeStruct((8, WIDTH, HALF), BF16),
            jax.ShapeDtypeStruct((8, HALF, WIDTH), BF16),
        ],
        in_specs=[
            pl.BlockSpec((1, LENGTH, WIDTH), lambda i: (jnp.minimum(i, 3), 0, 0)),
            pl.BlockSpec((1, LENGTH, WIDTH), lambda i: (jnp.maximum(i - 4, 0), 0, 0)),
            whole(LENGTH, 8),
            whole(1, WIDTH),
            whole(WIDTH, WIDTH),
            whole(4 * WIDTH, WIDTH),
        ],
        out_specs=[
            each(LENGTH, WIDTH + 128),
            each(WIDTH, LENGTH),
            each(WIDTH, HALF),
            each(WIDTH, HALF),
            each(HALF, WIDTH),
        ],
        compiler_params=params,
        cost_estimate=pl.CostEstimate(
            flops=2 * 8 * 512 * 256 * 768, bytes_accessed=9 * 2**20, transcendentals=0
        ),
    )(
        homolog,
        other,
        mask_t,
        row_gain.reshape(1, WIDTH),
        row_in[:, WIDTH : 2 * WIDTH],
        row_in_t,
    )

    after_rows = pl.pallas_call(
        row_kernel,
        grid=(8,),
        out_shape=jax.ShapeDtypeStruct((8 * HALF, WIDTH), BF16),
        in_specs=[
            whole(PEERS, TILE_ROWS, 256),
            each(LENGTH, WIDTH + 128),
            each(WIDTH, LENGTH),
            each(WIDTH, HALF),
            each(WIDTH, HALF),
            each(HALF, WIDTH),
            whole(WIDTH, WIDTH),
        ],
        out_specs=whole(8 * HALF, WIDTH),
        scratch_shapes=[
            pltpu.VMEM((HEADS, LENGTH, HALF), F32),
            pltpu.VMEM((2, 8 * HALF, 128), F32),
        ],
        compiler_params=params,
        cost_estimate=pl.CostEstimate(
            flops=2 * 8 * 8 * 512 * 256 * 512, bytes_accessed=9 * 2**20, transcendentals=8 * 2**20
        ),
    )(tiles, keys, vt, qt, gt, xq, row_out)

    columns = lax.all_to_all(after_rows.reshape(PEERS, 32, WIDTH), PLANE, 0, 0, tiled=True)
    col_mask = tiles[:, 64:, :].reshape(LENGTH, HALF)

    finished = pl.pallas_call(
        column_kernel,
        grid=(4,),
        out_shape=jax.ShapeDtypeStruct((4 * LENGTH, WIDTH), BF16),
        in_specs=[
            whole(PEERS, 32, WIDTH),
            whole(LENGTH, HALF),
            whole(1, WIDTH),
            whole(WIDTH, WIDTH),
            whole(4 * WIDTH, WIDTH),
            whole(WIDTH, WIDTH),
            whole(1, WIDTH),
            whole(WIDTH, 4 * WIDTH),
            whole(4 * WIDTH, WIDTH),
        ],
        out_specs=whole(4 * LENGTH, WIDTH),
        scratch_shapes=[
            pltpu.VMEM((PEERS, 4, 8, WIDTH), F32),
            pltpu.VMEM((2, 4 * LENGTH, 128), F32),
        ],
        compiler_params=params,
        cost_estimate=pl.CostEstimate(
            flops=2 * 8 * 8 * 512 * 256 * 512, bytes_accessed=4 * 2**20, transcendentals=8 * 2**20
        ),
    )(
        columns,
        col_mask,
        col_gain.reshape(1, WIDTH),
        col_in[:, WIDTH : 2 * WIDTH],
        col_in_t,
        col_out,
        ff_gain.reshape(1, WIDTH),
        ff_expand,
        ff_shrink,
    )

    back = lax.all_to_all(finished.reshape(128, 16, WIDTH), AXES, 0, 0, tiled=True)
    back = back.reshape(32, 2, 2, 4, 4, WIDTH)
    return jnp.transpose(back, (3, 0, 2, 1, 4, 5)).reshape(4, LENGTH, WIDTH)


def solution(mesh):
    inner = Mesh(mesh.devices.reshape(2, 4, 4, 2, 2), AXES)
    dap = ("z", "x", "yh", "core")
    return jax.shard_map(
        body,
        mesh=inner,
        in_specs=(P(AXES, None, None), P(dap, "grp", None), P(AXES, None)) + (P(),) * 13,
        out_specs=P(AXES, None, None),
        check_vma=False,
    )
```

time: 335 us -> 172 us (0.51)
  matrix products: 107 us -> 0 us
  Pallas kernels: 0 us -> 78.4 us
  local copies, waits for them, and re-layouts: 67.7 us -> 10.5 us
  waiting for transfers between devices: 76.4 us -> 35.8 us
  other arithmetic: 23.5 us -> 0.02 us
  between operations: 13.7 us -> 0.18 us
  starting transfers between devices: 17.1 us -> 20.9 us
    dot_general x24 -> x0, matrix products: 86.3 us -> none  [the longest x8 44.6 us: attend(): jnp.einsum('hqk,khd->qhd', weights, attended_vectors, preferred_element_t...]
    pallas_call x0 -> x5, Pallas kernels: none -> 78.4 us  [the longest x1 35.5 us: body(): pl.pallas_call(column_kernel, grid=(4,), out_shape=jax.ShapeDtypeStruct((...]
    all_gather x1 -> x0, waiting for transfers between devices: 58.3 us -> none  [body(): full_bias = lax.all_gather(bias_strip, 'dap', axis=1, tiled=True)]
    sub x4 -> x0, matrix products: 21 us -> none  [attend(): powers = jnp.exp(scores - highest)]
    all_to_all x2, waiting for transfers between devices: 18.1 us -> 33.8 us  [the longest x1 18.4 us: body(): tiles = lax.all_to_all(payload, PLANE, 0, 0, tiled=True)]
    while x9 -> x0, local copies, waits for them, and re-layouts: 15.5 us -> none  [the longest x1 8.73 us: body(): row_update_terms = lax.map(per_sequence, (packed, key_mask_term))]
    reshape x5 -> x6, local copies, waits for them, and re-layouts: 19 us -> 4.16 us  [the longest x1 1.11 us: body(): return jnp.transpose(back, (3, 0, 2, 1, 4, 5)).reshape(4, LENGTH, WIDTH)]
    convert_element_type x7 -> x0, local copies, waits for them, and re-layouts: 12 us -> none  [the longest x4 7.62 us: body(): column_alignment.astype(jnp.float32)]
  transfers between devices with their start and end apart: 3 -> 4, of which waited for: 2 -> 3; matrix products, arithmetic and copies ran while one was open for 26% -> 2% of each run, Pallas kernels for 0% -> 6%
where the time goes in v1:
time: 172 us; the launch traced here: 171 us
  Pallas kernels  78.4 us (46%)
  waiting for transfers between devices  35.8 us (21%)
  blocking collectives  25.1 us (15%)
  starting transfers between devices  20.9 us (12%)
  local copies, waits for them, and re-layouts  10.5 us (6%)
    pallas_call x1, Pallas kernels, body(): pl.pallas_call(column_kernel, grid=(4,), out_shape=jax.ShapeDtypeStruct((...  35.5 us
    pallas_call x1, Pallas kernels, body(): pl.pallas_call(row_kernel, grid=(8,), out_shape=jax.ShapeDtypeStruct((8 *...  31.5 us
    all_to_all x1, blocking collectives, body(): lax.all_to_all(finished.reshape(128, 16, WIDTH), AXES, 0, 0, tiled=True)  25.1 us
    all_to_all x1, waiting for transfers between devices, body(): tiles = lax.all_to_all(payload, PLANE, 0, 0, tiled=True)  18.4 us
    all_to_all x1, waiting for transfers between devices, body(): lax.all_to_all(after_rows.reshape(PEERS, 32, WIDTH), PLANE, 0, 0, tiled=T...  15.4 us
    all_to_all x1, starting transfers between devices, body(): tiles = lax.all_to_all(payload, PLANE, 0, 0, tiled=True)  11.6 us
    pallas_call x1, Pallas kernels, body(): pl.pallas_call(project_kernel, grid=(8,), out_shape=[jax.ShapeDtypeStruct...  8.2 us
    all_to_all x1, starting transfers between devices, body(): lax.all_to_all(after_rows.reshape(PEERS, 32, WIDTH), PLANE, 0, 0, tiled=T...  7.5 us
  transfers between devices with their start and end apart: 4, of which 3 were waited for; matrix products, arithmetic and copies ran while one was open for 2% of the time, Pallas kernels for 6%

profile of v1, /device:TPU:1, one launch (start us, length us, event | category | flops | bytes accessed | tf_op | source)
XLA Modules:
  0.0 170.9 jit_solution(15901773968196740236)
XLA Ops:
  0.0 1.4 collective-permute-start
  1.4 0.7 reshape.38.chain_v_ref
  2.1 0.7 copy.24.inter_ref
  2.8 1.0 copy-done
  3.9 0.7 copy-done.3
  4.6 0.7 copy-done.4
  5.3 0.7 copy-done.5
  5.9 1.4 shard_map.154.bias_ref
  7.3 0.7 copy-done.1
  8.0 1.9 %shard_map.155 = bf16[64,72,256]{2,1,0:T(8,128)(2,1)} custom-call(bf16[64,256]{1,0:T(8,128)(2,1)S(1)} %shard_map.154.bias_ref, s32[4,512]{1,0:T(4,128)S(1)} %copy-done.1, s32[4,512]{1,0:T(4,128)S(1)} %collective-permute-done.other_ref), custom_call_target="tpu_custom_call" | custom-call | tf_op jit(solution)/shard_map/pallas_call | solution.py:279
  9.9 11.6 %all-to-all-start = ((bf16[64,72,256]{2,1,0:T(8,128)(2,1)}), bf16[64,72,256]{2,1,0:T(8,128)(2,1)}, u32[]{:S(2)}, u32[]{:S(2)}) async-start(bf16[64,72,256]{2,1,0:T(8,128)(2,1)} %shard_map.155), calls=%async_computation | async-start | bytes 4718592 | tf_op jit(solution)/shard_map/all_to_all | solution.py:284
  22.3 2.1 %collective-permute-done.1.other_ref = bf16[4,512,256]{2,1,0:T(8,128)(2,1)} collective-permute-done((bf16[4,512,256]{2,1,0:T(8,128)(2,1)S(1)}, bf16[4,512,256]{2,1,0:T(8,128)(2,1)}, u32[]{:S(2)}, u32[]{:S(2)}) %collective-permute-start.1) | collective-permute-done | bytes 1048608 | tf_op jit(solution)/shard_map/ppermute | solution.py:257
  24.4 8.2 %shard_map.156 = (bf16[8,512,384]{2,1,0:T(8,128)(2,1)}, bf16[8,256,512]{2,1,0:T(8,128)(2,1)}, bf16[8,256,256]{2,1,0:T(8,128)(2,1)S(1)}, bf16[8,256,256]{2,1,0:T(8,128)(2,1)S(1)}, bf16[8,256,256]{2,1,0:T(8,128)(2,1)S(1)}) custom-call(bf16[4,512,256]{2,1,0:T(8,128)(2,1)} %own_ref.3, bf16[4,512,256]{2,1,0:T(8,128)(2,1)} %collective-permute-done.1.other_ref, ...), custom_call_target="tpu_custom_call" | custom-call | flops 1610612736 | bytes 9437184 | tf_op jit(solution)/shard_map/pallas_call | solution.py:289
  32.6 1.0 copy-done.13
  33.6 18.4 %all-to-all-done.tile_ref = bf16[64,72,256]{2,1,0:T(8,128)(2,1)} async-done(((bf16[64,72,256]{2,1,0:T(8,128)(2,1)}), bf16[64,72,256]{2,1,0:T(8,128)(2,1)}, u32[]{:S(2)}, u32[]{:S(2)}) %all-to-all-start) | async-done | bytes 2359328 | tf_op jit(solution)/shard_map/all_to_all | solution.py:284
  52.0 31.5 %shard_map.157 = bf16[2048,256]{1,0:T(8,128)(2,1)} custom-call(bf16[64,72,256]{2,1,0:T(8,128)(2,1)} %all-to-all-done.tile_ref, bf16[8,512,384]{2,1,0:T(8,128)(2,1)} %get-tuple-element.10.k_ref, bf16[8,256,512]{2,1,0:T(8,128)(2,1)} %get-tuple-element.11.vt_ref, bf16[8,256,256]{2,1,0:T(8,128)(2,1)S(1)} %get-tuple-element.12.qt_ref, ...), custom_call_target="tpu_custom_call" | custom-call | flops 8589934592 | bytes 9437184 | tf_op jit(solution)/shard_map/pallas_call | solution.py:327
  83.5 7.5 %all-to-all-start.1 = ((bf16[64,32,256]{2,1,0:T(8,128)(2,1)}), bf16[64,32,256]{2,1,0:T(8,128)(2,1)S(1)}, u32[]{:S(2)}, u32[]{:S(2)}) async-start(bf16[64,32,256]{2,1,0:T(8,128)(2,1)} %bitcast.6), calls=%async_computation.1 | async-start | bytes 2097152 | tf_op jit(solution)/shard_map/all_to_all | solution.py:351
  91.2 1.0 slice_bitcast_fusion.mask_ref
  92.2 15.4 %all-to-all-done.1.x_ref = bf16[64,32,256]{2,1,0:T(8,128)(2,1)S(1)} async-done(((bf16[64,32,256]{2,1,0:T(8,128)(2,1)}), bf16[64,32,256]{2,1,0:T(8,128)(2,1)S(1)}, u32[]{:S(2)}, u32[]{:S(2)}) %all-to-all-start.1) | async-done | bytes 1048608 | tf_op jit(solution)/shard_map/all_to_all | solution.py:351
  107.6 1.0 copy-done.14
  108.6 35.5 %shard_map.158 = bf16[2048,256]{1,0:T(8,128)(2,1)S(1)} custom-call(bf16[64,32,256]{2,1,0:T(8,128)(2,1)} %copy-done.14, bf16[512,256]{1,0:T(8,128)(2,1)S(1)} %slice_bitcast_fusion.mask_ref, f32[1,256]{1,0:T(1,128)S(1)} %bitcast.23, bf16[256,256]{1,0:T(8,128)(2,1)S(1)} %slice.11.wk_ref, bf16[1024,256]{1,0:T(8,128)(2,1)S(1)} %bitcast.19, ...), custom_call_target="tpu_custom_call" | custom-call | flops 8589934592 | bytes 4194304 | tf_op jit(solution)/shard_map/pallas_call | solution.py:354
  144.0 25.1 %all_to_all.15 = bf16[128,16,256]{2,1,0:T(8,128)(2,1)S(1)} all-to-all(bf16[128,16,256]{2,1,0:T(8,128)(2,1)S(1)} %bitcast.16), channel_id=1, replica_groups=mesh['grp'=2,'z'=4,'x'=4,'yh'=2,'core'=2] {'grp','z','x','yh','core'}, dimensions={0} | all-to-all | bytes 2097152 | tf_op jit(solution)/shard_map/all_to_all | solution.py:390
  169.4 0.4 copy.30
  169.8 1.1 reshape.47
  (40 shorter events, 1.3 us)
Async XLA Ops:
  0.0 7.3 %collective-permute-start = (s32[4,512]{1,0:T(4,128)}, s32[4,512]{1,0:T(4,128)S(1)}, u32[]{:S(2)}, u32[]{:S(2)}) collective-permute-start(s32[4,512]{1,0:T(4,128)} %own_ref.2), channel_id=1, source_target_pairs={{0,1},{1,0},{2,3},{3,2},{4,5},{5,4},{6,7},{7,6},{8,9},{9,8},{10,11... | collective-permute-start | bytes 24584 | tf_op jit(solution)/shard_map/ppermute | solution.py:256
  2.8 1.0 copy-start
  3.9 0.7 copy-start.3
  4.6 0.7 copy-start.4
  5.3 0.7 copy-start.5
  7.3 0.7 copy-start.1
  9.9 11.6 %copy-start.17 = (bf16[4,512,256]{2,1,0:T(8,128)(2,1)S(1)}, bf16[4,512,256]{2,1,0:T(8,128)(2,1)}, u32[]{:S(2)}) copy-start(bf16[4,512,256]{2,1,0:T(8,128)(2,1)} %own_ref.3) | copy-start | bytes 3145732
  9.9 12.0 %copy-start.2 = (s32[4,512]{1,0:T(4,128)S(1)}, s32[4,512]{1,0:T(4,128)}, u32[]{:S(2)}) copy-start(s32[4,512]{1,0:T(4,128)} %own_ref.2) | copy-start | bytes 24580
  9.9 12.0 %copy-start.15 = (bf16[256,1024]{1,0:T(8,128)(2,1)S(1)}, bf16[256,1024]{1,0:T(8,128)(2,1)}, u32[]{:S(2)}) copy-start(bf16[256,1024]{1,0:T(8,128)(2,1)} %param.24) | copy-start | bytes 1572868
  9.9 14.5 %copy-start.10 = (f32[256]{0:T(256)S(1)}, f32[256]{0:T(256)}, u32[]{:S(2)}) copy-start(f32[256]{0:T(256)} %param.20) | copy-start | bytes 3076
  9.9 42.1 %all-to-all-start = ((bf16[64,72,256]{2,1,0:T(8,128)(2,1)}), bf16[64,72,256]{2,1,0:T(8,128)(2,1)}, u32[]{:S(2)}, u32[]{:S(2)}) async-start(bf16[64,72,256]{2,1,0:T(8,128)(2,1)} %shard_map.155), calls=%async_computation | async-start | bytes 4718592 | tf_op jit(solution)/shard_map/all_to_all | solution.py:284
  21.5 2.9 %collective-permute-start.1 = (bf16[4,512,256]{2,1,0:T(8,128)(2,1)S(1)}, bf16[4,512,256]{2,1,0:T(8,128)(2,1)}, u32[]{:S(2)}, u32[]{:S(2)}) collective-permute-start(bf16[4,512,256]{2,1,0:T(8,128)(2,1)S(1)} %copy-done.17), channel_id=1, source_target_pairs={{0,1},{1,0},{2,3},{3,2},{4,5},{5,4},{6,7},{7,6},{8,9},{9,8},{10,11... | collective-permute-start | bytes 3145736 | tf_op jit(solution)/shard_map/ppermute | solution.py:257
  24.4 27.6 %copy-start.8 = (bf16[256,256]{1,0:T(8,128)(2,1)S(1)}, bf16[256,256]{1,0:T(8,128)(2,1)}, u32[]{:S(2)}) copy-start(bf16[256,256]{1,0:T(8,128)(2,1)} %wo_ref.2) | copy-start | bytes 393220
  32.6 1.0 copy-start.13
  52.0 39.0 %copy-start.16 = (bf16[256,1024]{1,0:T(8,128)(2,1)S(1)}, bf16[256,1024]{1,0:T(8,128)(2,1)}, u32[]{:S(2)}) copy-start(bf16[256,1024]{1,0:T(8,128)(2,1)} %param.27) | copy-start | bytes 1572868
  83.4 25.1 %copy-start.6 = (bf16[256,1024]{1,0:T(8,128)(2,1)S(1)}, bf16[256,1024]{1,0:T(8,128)(2,1)}, u32[]{:S(2)}) copy-start(bf16[256,1024]{1,0:T(8,128)(2,1)} %w1_ref.1) | copy-start | bytes 1572868
  83.4 25.1 %copy-start.7 = (bf16[1024,256]{1,0:T(8,128)(2,1)S(1)}, bf16[1024,256]{1,0:T(8,128)(2,1)}, u32[]{:S(2)}) copy-start(bf16[1024,256]{1,0:T(8,128)(2,1)} %w2_ref.1) | copy-start | bytes 1572868
  83.4 25.1 %copy-start.9 = (bf16[256,256]{1,0:T(8,128)(2,1)S(1)}, bf16[256,256]{1,0:T(8,128)(2,1)}, u32[]{:S(2)}) copy-start(bf16[256,256]{1,0:T(8,128)(2,1)} %wo_ref.3) | copy-start | bytes 393220
  83.4 25.1 %copy-start.11 = (f32[256]{0:T(256)S(1)}, f32[256]{0:T(256)}, u32[]{:S(2)}) copy-start(f32[256]{0:T(256)} %param.26) | copy-start | bytes 3076
  83.5 25.1 %copy-start.12 = (f32[256]{0:T(256)S(1)}, f32[256]{0:T(256)}, u32[]{:S(2)}) copy-start(f32[256]{0:T(256)} %param.29) | copy-start | bytes 3076
  83.5 24.1 %all-to-all-start.1 = ((bf16[64,32,256]{2,1,0:T(8,128)(2,1)}), bf16[64,32,256]{2,1,0:T(8,128)(2,1)S(1)}, u32[]{:S(2)}, u32[]{:S(2)}) async-start(bf16[64,32,256]{2,1,0:T(8,128)(2,1)} %bitcast.6), calls=%async_computation.1 | async-start | bytes 2097152 | tf_op jit(solution)/shard_map/all_to_all | solution.py:351
  107.6 1.0 copy-start.14

commit v2 on v1

v2 whole, which is shorter than its diff:
```python
import functools
import math

import jax
import jax.numpy as jnp
import ml_dtypes
import numpy as np
from jax import lax
from jax.experimental import pallas as pl
from jax.experimental.pallas import tpu as pltpu
from jax.sharding import Mesh, PartitionSpec as P

EPSILON = 1e-05
HEADS = 8
HEAD = 32
WIDTH = 256
LENGTH = 512
HALF = 256
PEERS = 64
BATCH = 2
LOG2E = math.log2(math.e)
SCALE = HEAD**-0.5 * LOG2E
F32 = jnp.float32
BF16 = jnp.bfloat16
AXES = ("grp", "z", "x", "yh", "core")
PLANE = ("grp", "z", "x", "yh")
VMEM_LIMIT = 50 * 1024 * 1024

MASK_TERM = 1e9 * HEAD**0.5


def mask_parts():
    parts = []
    rest = MASK_TERM
    for _ in range(3):
        part = float(np.asarray(rest, ml_dtypes.bfloat16))
        parts.append(part)
        rest -= part
    return parts


def nt(a, b):
    return lax.dot_general(a, b, (((1,), (1,)), ((), ())), preferred_element_type=F32)


def tn(a, b):
    return lax.dot_general(a, b, (((0,), (0,)), ((), ())), preferred_element_type=F32)


def nn(a, b):
    return jnp.dot(a, b, preferred_element_type=F32)


def norm(x, gain):
    average = jnp.mean(x, axis=-1, keepdims=True)
    center = x - average
    spread = jnp.mean(center * center, axis=-1, keepdims=True)
    return (center * lax.rsqrt(spread + EPSILON) * gain).astype(BF16)


def position():
    q = (lax.axis_index("z") * 4 + lax.axis_index("x")) * 2 + lax.axis_index("yh")
    return lax.axis_index("grp"), q, lax.axis_index("core")


def bias_kernel(pair_ref, gain_ref, weight_ref, chain_ref, inter_ref, out_ref):
    grp, q, core = position()
    normed = norm(pair_ref[...].astype(F32), gain_ref[...])
    bias = nt(weight_ref[...], normed)
    chain = chain_ref[...]
    cols = jnp.where(grp == 0, chain[:, :256], chain[:, 256:])
    place = lax.broadcasted_iota(jnp.int32, (8, LENGTH), 1)
    wanted = 16 * q + 8 * core + lax.broadcasted_iota(jnp.int32, (8, LENGTH), 0)
    rows = jnp.sum(jnp.where(place == wanted, chain, 0), axis=1, keepdims=True)
    cross = (rows != cols).astype(F32)
    row = lax.broadcasted_iota(jnp.int32, (8, 8), 0)
    col = lax.broadcasted_iota(jnp.int32, (8, 8), 1)
    inter = jnp.sum(jnp.where(row == col, inter_ref[...], 0.0), axis=1, keepdims=True)
    parts = [
        bias[:, ii * 256 : (ii + 1) * 256] + inter * cross[ii : ii + 1] for ii in range(8)
    ]
    stacked = jnp.stack(parts, axis=0)
    tile = jnp.swapaxes(stacked, 0, 1).reshape(64, 256).astype(BF16)

    def put(p, carry):
        out_ref[p] = tile
        return carry

    lax.fori_loop(0, PEERS, put, 0)


def project_kernel(
    own_ref, other_ref, mask_ref, own_mask_ref, other_mask_ref, gain_ref, wk_ref, wt_ref,
    k_ref, vt_ref, qt_ref, gt_ref, xq_ref, mask_out_ref,
):
    step = pl.program_id(0)
    _, _, core = position()
    x = jnp.where(step < 4, own_ref[0].astype(F32), other_ref[0].astype(F32))
    normed = norm(x, gain_ref[...])
    k_ref[0, :, :WIDTH] = nn(normed, wk_ref[...]).astype(BF16)
    lane = lax.broadcasted_iota(jnp.int32, (8, 128), 1)
    row = lax.broadcasted_iota(jnp.int32, (8, 128), 0)
    consts = mask_parts()
    pick = jnp.zeros((8, 128), F32)
    for at, value in enumerate(consts):
        pick = jnp.where((lane == at) & (row == step), value, pick)
    k_ref[0, :, WIDTH:] = nn(mask_ref[...] - 1, pick.astype(BF16)).astype(BF16)
    vt_ref[0] = nt(wt_ref[2 * WIDTH : 3 * WIDTH], normed).astype(BF16)

    def half(a):
        rows = a.reshape(32, 2, 8, WIDTH)
        return jnp.where(core == 0, rows[:, 0], rows[:, 1]).reshape(HALF, WIDTH)

    xq = half(x)
    xq_ref[0] = xq.astype(BF16)
    normed_q = half(normed.astype(F32)).astype(BF16)
    qt_ref[0] = nt(wt_ref[:WIDTH], normed_q).astype(BF16)
    gt_ref[0] = nt(wt_ref[3 * WIDTH :], normed_q).astype(BF16)

    @pl.when(step == 0)
    def _():
        own = own_mask_ref[...].astype(F32)
        other = other_mask_ref[...].astype(F32)
        first = jnp.where(core == 0, own, other)
        second = jnp.where(core == 0, other, own)
        mask = jnp.concatenate([first, second], axis=0).astype(BF16)
        i = lax.broadcasted_iota(jnp.int32, (LENGTH, HALF), 0)
        l = lax.broadcasted_iota(jnp.int32, (LENGTH, HALF), 1)
        pick = (i == (l // 8) * 16 + core * 8 + l % 8).astype(F32).astype(BF16)
        mask_out_ref[...] = nn(mask, pick).astype(BF16)


def spread(qt, h, mask_rows):
    at = h % 4
    queries = qt.shape[1]
    pieces = []
    if at:
        pieces.append(jnp.zeros((HEAD * at, queries), BF16))
    pieces.append(qt[h * HEAD : (h + 1) * HEAD])
    if at < 3:
        pieces.append(jnp.zeros((HEAD * (3 - at), queries), BF16))
    pieces.append(mask_rows)
    return jnp.concatenate(pieces, axis=0)


def attend(parts, bias):
    mask_rows = jnp.ones((128, HALF), BF16)
    ones_v = jnp.ones((16, LENGTH), BF16)
    augmented = [
        [jnp.concatenate([keys[:, g * 128 : (g + 1) * 128], tile], axis=1) for g in range(2)]
        for keys, tile, _, _ in parts
    ]
    units = [(part, h) for part in range(len(parts)) for h in range(HEADS)]

    def score(part, h):
        return nn(augmented[part][h // 4], spread(parts[part][3], h, mask_rows))

    def blend(part, h, powers):
        vt = parts[part][2]
        values = jnp.concatenate([vt[h * HEAD : (h + 1) * HEAD], ones_v], axis=0)
        blended = nn(values, powers)
        return blended[:HEAD] / blended[HEAD : HEAD + 1]

    out = []
    scores = score(*units[0])
    powers = None
    for at, (part, h) in enumerate(units):
        later = score(*units[at + 1]) if at + 1 < len(units) else None
        scaled = scores * SCALE
        if bias is not None:
            scaled = scaled + bias[h]
        highest = jnp.max(scaled, axis=0, keepdims=True)
        now = jnp.exp2(scaled - highest).astype(BF16)
        if at:
            out.append(blend(*units[at - 1], powers))
        powers = now
        scores = later
    out.append(blend(*units[-1], powers))
    return [
        jnp.concatenate(out[part * HEADS : (part + 1) * HEADS], axis=0)
        for part in range(len(parts))
    ]


def row_kernel(
    tile_ref, k_ref, vt_ref, qt_ref, gt_ref, xq_ref, wo_ref, mask_ref, out_ref, bias_ref, y_ref
):
    step = pl.program_id(0)
    _, _, core = position()

    @pl.when(step == 0)
    def _():
        row = lax.broadcasted_iota(jnp.int32, (HALF, HALF), 0)
        col = lax.broadcasted_iota(jnp.int32, (HALF, HALF), 1)
        eye = (row == col).astype(F32).astype(BF16)
        for g in range(2):
            for pair in range(4):
                block = tile_ref[g * 32 : (g + 1) * 32, pair * 16 : (pair + 1) * 16, :]
                block = block.astype(F32).reshape(32, 2, 8, 256)
                for k in range(2):
                    rows = block[:, k].reshape(HALF, 256).astype(BF16)
                    bias_ref[pair * 2 + k, g * 256 : (g + 1) * 256, :] = nt(eye, rows) * LOG2E

    parts = [
        (k_ref[n, :, :WIDTH], k_ref[n, :, WIDTH:], vt_ref[n], qt_ref[n]) for n in range(BATCH)
    ]
    for n, o in enumerate(attend(parts, bias_ref)):
        gated = (o * jax.nn.sigmoid(gt_ref[n].astype(F32))).astype(BF16)
        y = xq_ref[n].astype(F32) + tn(gated, wo_ref[...])
        s = lax.rem(step * BATCH + n + 4 * core, 8)
        for j in range(2):
            y_ref[j, pl.ds(s, HALF, stride=8), :] = y[:, j * 128 : (j + 1) * 128]

    @pl.when(step == 8 // BATCH - 1)
    def _():
        for j in range(2):
            lanes = slice(j * 128, (j + 1) * 128)
            out_ref[:, :32, lanes] = y_ref[j].astype(BF16).reshape(PEERS, 32, 128)
        out_ref[:, 32:, :] = jnp.broadcast_to(mask_ref[...][None], (PEERS, 8, WIDTH))


def column_kernel(
    x_ref, gain_ref, wk_ref, wt_ref, wo_ref, gain2_ref, w1_ref, w2_ref, out_ref, x32_ref, y_ref
):
    r = pl.program_id(0)
    grp, q, _ = position()
    peer = grp * 32 + q

    @pl.when(r == 0)
    def _():
        x32_ref[...] = x_ref[...].astype(F32).reshape(PEERS, 5, 8, WIDTH)

    x = x32_ref[:, r].reshape(LENGTH, WIDTH)
    normed = norm(x, gain_ref[...])
    keys = nn(normed, wk_ref[...]).astype(BF16)
    lane = lax.broadcasted_iota(jnp.int32, (HALF, 128), 1)
    row = lax.broadcasted_iota(jnp.int32, (HALF, 128), 0)
    pick = jnp.zeros((HALF, 128), F32)
    for at, value in enumerate(mask_parts()):
        pick = jnp.where((lane == at) & (row == 4 * peer + r), value, pick)
    mask_tile = nn((x32_ref[:, 4].reshape(LENGTH, HALF) - 1.0).astype(BF16), pick.astype(BF16)).astype(BF16)
    vt = nt(wt_ref[2 * WIDTH : 3 * WIDTH], normed).astype(BF16)
    qt = nt(wt_ref[:WIDTH], normed).astype(BF16)
    gt = nt(wt_ref[3 * WIDTH :], normed).astype(BF16)
    parts = [(keys, mask_tile, vt, qt[:, n * HALF : (n + 1) * HALF]) for n in range(2)]
    for n, o in enumerate(attend(parts, None)):
        cols = slice(n * HALF, (n + 1) * HALF)
        gated = (o * jax.nn.sigmoid(gt[:, cols].astype(F32))).astype(BF16)
        one = x[cols] + tn(gated, wo_ref[...])
        two = one.astype(BF16).astype(F32)
        hidden = jnp.maximum(nn(norm(two, gain2_ref[...]), w1_ref[...]), 0.0).astype(BF16)
        y = two + nn(hidden, w2_ref[...])
        for j in range(2):
            y_ref[j, pl.ds(n * 4 * HALF + r, HALF, stride=4), :] = y[:, j * 128 : (j + 1) * 128]

    @pl.when(r == 3)
    def _():
        for j in range(2):
            out_ref[:, j * 128 : (j + 1) * 128] = y_ref[j].astype(BF16)


def whole(*shape):
    return pl.BlockSpec(shape, lambda i: (0,) * len(shape))


def each(count, *shape):
    return pl.BlockSpec((count,) + shape, lambda i: (i,) + (0,) * len(shape))


def body(
    homolog,
    pair_state,
    mask,
    chain,
    row_gain,
    pair_gain,
    pair_weight,
    interchain,
    row_in,
    row_out,
    col_gain,
    col_in,
    col_out,
    ff_gain,
    ff_expand,
    ff_shrink,
):
    params = pltpu.CompilerParams(vmem_limit_bytes=VMEM_LIMIT)
    swap = [(0, 1), (1, 0)]
    other_mask = lax.ppermute(mask, "core", swap)
    other = lax.ppermute(homolog, "core", swap)

    payload = pl.pallas_call(
        bias_kernel,
        grid=(1,),
        out_shape=jax.ShapeDtypeStruct((PEERS, 64, 256), BF16),
        in_specs=[whole(2048, 128), whole(1, 128), whole(8, 128), whole(1, LENGTH), whole(1, 8)],
        out_specs=whole(PEERS, 64, 256),
        compiler_params=params,
    )(
        pair_state.reshape(2048, 128),
        pair_gain.reshape(1, 128),
        pair_weight,
        chain.reshape(1, LENGTH),
        interchain.reshape(1, 8),
    )
    tiles = lax.all_to_all(payload, PLANE, 0, 0, tiled=True)

    row_in_t = row_in.T
    col_in_t = col_in.T
    mask_t = jnp.concatenate([mask, other_mask], axis=0).astype(BF16).T
    keys, vt, qt, gt, xq, mask_half = pl.pallas_call(
        project_kernel,
        grid=(8,),
        out_shape=[
            jax.ShapeDtypeStruct((8, LENGTH, WIDTH + 128), BF16),
            jax.ShapeDtypeStruct((8, WIDTH, LENGTH), BF16),
            jax.ShapeDtypeStruct((8, WIDTH, HALF), BF16),
            jax.ShapeDtypeStruct((8, WIDTH, HALF), BF16),
            jax.ShapeDtypeStruct((8, HALF, WIDTH), BF16),
            jax.ShapeDtypeStruct((8, HALF), BF16),
        ],
        in_specs=[
            pl.BlockSpec((1, LENGTH, WIDTH), lambda i: (jnp.minimum(i, 3), 0, 0)),
            pl.BlockSpec((1, LENGTH, WIDTH), lambda i: (jnp.maximum(i - 4, 0), 0, 0)),
            whole(LENGTH, 8),
            whole(4, LENGTH),
            whole(4, LENGTH),
            whole(1, WIDTH),
            whole(WIDTH, WIDTH),
            whole(4 * WIDTH, WIDTH),
        ],
        out_specs=[
            each(1, LENGTH, WIDTH + 128),
            each(1, WIDTH, LENGTH),
            each(1, WIDTH, HALF),
            each(1, WIDTH, HALF),
            each(1, HALF, WIDTH),
            whole(8, HALF),
        ],
        compiler_params=params,
        cost_estimate=pl.CostEstimate(
            flops=2 * 8 * 512 * 256 * 768, bytes_accessed=9 * 2**20, transcendentals=0
        ),
    )(
        homolog,
        other,
        mask_t,
        mask,
        other_mask,
        row_gain.reshape(1, WIDTH),
        row_in[:, WIDTH : 2 * WIDTH],
        row_in_t,
    )

    after_rows = pl.pallas_call(
        row_kernel,
        grid=(8 // BATCH,),
        out_shape=jax.ShapeDtypeStruct((PEERS, 40, WIDTH), BF16),
        in_specs=[
            whole(PEERS, 64, 256),
            each(BATCH, LENGTH, WIDTH + 128),
            each(BATCH, WIDTH, LENGTH),
            each(BATCH, WIDTH, HALF),
            each(BATCH, WIDTH, HALF),
            each(BATCH, HALF, WIDTH),
            whole(WIDTH, WIDTH),
            whole(8, HALF),
        ],
        out_specs=whole(PEERS, 40, WIDTH),
        scratch_shapes=[
            pltpu.VMEM((HEADS, LENGTH, HALF), F32),
            pltpu.VMEM((2, 8 * HALF, 128), F32),
        ],
        compiler_params=params,
        cost_estimate=pl.CostEstimate(
            flops=2 * 8 * 8 * 512 * 256 * 512, bytes_accessed=9 * 2**20, transcendentals=8 * 2**20
        ),
    )(tiles, keys, vt, qt, gt, xq, row_out, mask_half)

    columns = lax.all_to_all(after_rows, PLANE, 0, 0, tiled=True)

    finished = pl.pallas_call(
        column_kernel,
        grid=(4,),
        out_shape=jax.ShapeDtypeStruct((4 * LENGTH, WIDTH), BF16),
        in_specs=[
            whole(PEERS, 40, WIDTH),
            whole(1, WIDTH),
            whole(WIDTH, WIDTH),
            whole(4 * WIDTH, WIDTH),
            whole(WIDTH, WIDTH),
            whole(1, WIDTH),
            whole(WIDTH, 4 * WIDTH),
            whole(4 * WIDTH, WIDTH),
        ],
        out_specs=whole(4 * LENGTH, WIDTH),
        scratch_shapes=[
            pltpu.VMEM((PEERS, 5, 8, WIDTH), F32),
            pltpu.VMEM((2, 4 * LENGTH, 128), F32),
        ],
        compiler_params=params,
        cost_estimate=pl.CostEstimate(
            flops=2 * 8 * 8 * 512 * 256 * 512, bytes_accessed=4 * 2**20, transcendentals=8 * 2**20
        ),
    )(
        columns,
        col_gain.reshape(1, WIDTH),
        col_in[:, WIDTH : 2 * WIDTH],
        col_in_t,
        col_out,
        ff_gain.reshape(1, WIDTH),
        ff_expand,
        ff_shrink,
    )

    back = lax.all_to_all(finished.reshape(128, 16, WIDTH), AXES, 0, 0, tiled=True)
    back = back.reshape(32, 2, 2, 4, 4, WIDTH)
    return jnp.transpose(back, (3, 0, 2, 1, 4, 5)).reshape(4, LENGTH, WIDTH)


def solution(mesh):
    inner = Mesh(mesh.devices.reshape(2, 4, 4, 2, 2), AXES)
    dap = ("z", "x", "yh", "core")
    return jax.shard_map(
        body,
        mesh=inner,
        in_specs=(P(AXES, None, None), P(dap, "grp", None), P(AXES, None)) + (P(),) * 13,
        out_specs=P(AXES, None, None),
        check_vma=False,
    )
```

time: 172 us -> 139 us (0.81)
  Pallas kernels: 78.4 us -> 48.7 us
  waiting for transfers between devices: 35.8 us -> 31.8 us
    pallas_call x1, Pallas kernels: 35.5 us -> 20.3 us  [body(): pl.pallas_call(column_kernel, grid=(4,), out_shape=jax.ShapeDtypeStruct((...]
    pallas_call x3 -> x2, Pallas kernels: 34.7 us -> 19.6 us  [the longest x1 17.2 us: body(): pl.pallas_call(row_kernel, grid=(8 // BATCH,), out_shape=jax.ShapeDtypeSt...]
    all_to_all x1, waiting for transfers between devices: 18.4 us -> 13.8 us  [body(): tiles = lax.all_to_all(payload, PLANE, 0, 0, tiled=True)]
    reshape x3 -> x0, local copies, waits for them, and re-layouts: 2.39 us -> none  [the longest x1 0.97 us: body(): col_mask = tiles[:, 64:, :].reshape(LENGTH, HALF)]
    unnamed x38, local copies, waits for them, and re-layouts: 6.14 us -> 8.46 us
    ppermute x1, waiting for transfers between devices: 2.07 us -> 0.08 us  [body(): other = lax.ppermute(homolog, 'core', swap)]
    ppermute x1, waiting for transfers between devices: 0.01 us -> 1.83 us  [body(): other_mask = lax.ppermute(mask, 'core', swap)]
  transfers between devices with their start and end apart: 4 -> 4, of which waited for: 3 -> 4; matrix products, arithmetic and copies ran while one was open for 2% -> 2% of each run, Pallas kernels for 6% -> 6%
where the time goes in v2:
time: 139 us
  Pallas kernels  48.7 us (35%)
  waiting for transfers between devices  31.8 us (23%)
  blocking collectives  26.2 us (19%)
  starting transfers between devices  20.5 us (15%)
  local copies, waits for them, and re-layouts  11.3 us (8%)
    all_to_all x1, blocking collectives, body(): lax.all_to_all(finished.reshape(128, 16, WIDTH), AXES, 0, 0, tiled=True)  26.2 us
    pallas_call x1, Pallas kernels, body(): pl.pallas_call(column_kernel, grid=(4,), out_shape=jax.ShapeDtypeStruct((...  20.3 us
    pallas_call x1, Pallas kernels, body(): pl.pallas_call(row_kernel, grid=(8 // BATCH,), out_shape=jax.ShapeDtypeSt...  17.2 us
    all_to_all x1, waiting for transfers between devices, body(): columns = lax.all_to_all(after_rows, PLANE, 0, 0, tiled=True)  16.1 us
    all_to_all x1, waiting for transfers between devices, body(): tiles = lax.all_to_all(payload, PLANE, 0, 0, tiled=True)  13.8 us
    all_to_all x1, starting transfers between devices, body(): tiles = lax.all_to_all(payload, PLANE, 0, 0, tiled=True)  12.4 us
    pallas_call x1, Pallas kernels, body(): pl.pallas_call(project_kernel, grid=(8,), out_shape=[jax.ShapeDtypeStruct...  8.79 us
    unnamed x38, local copies, waits for them, and re-layouts  8.46 us
  transfers between devices with their start and end apart: 4, of which 4 were waited for; matrix products, arithmetic and copies ran while one was open for 2% of the time, Pallas kernels for 6%

profile of v2, /device:TPU:1, one launch (start us, length us, event | category | flops | bytes accessed | tf_op | source)
XLA Modules:
  0.0 138.6 jit_solution(5690894686714020398)
XLA Ops:
  0.0 1.0 copy-done
  1.0 0.7 copy-done.2
  1.7 0.7 copy-done.3
  2.4 0.7 copy-done.4
  3.1 0.7 copy-done.5
  3.7 2.5 %shard_map.154 = bf16[64,64,256]{2,1,0:T(8,128)(2,1)} custom-call(bf16[2048,128]{1,0:T(8,128)(2,1)S(1)} %bitcast.16, f32[1,128]{1,0:T(1,128)S(1)} %bitcast.20, bf16[8,128]{1,0:T(8,128)(2,1)S(1)} %copy-done.2, s32[1,512]{1,0:T(1,128)S(1)} %bitcast.19, f32[1,8]{1,0:T(1,128)S(1)} %bitcast.21), custom_call_target="tpu_custom_call" | custom-call | tf_op jit(solution)/shard_map/pallas_call | solution.py:293
  6.2 12.4 %all-to-all-start = ((bf16[64,64,256]{2,1,0:T(8,128)(2,1)}), bf16[64,64,256]{2,1,0:T(8,128)(2,1)}, u32[]{:S(2)}, u32[]{:S(2)}) async-start(bf16[64,64,256]{2,1,0:T(8,128)(2,1)} %shard_map.154), calls=%async_computation | async-start | bytes 4194304 | tf_op jit(solution)/shard_map/all_to_all | solution.py:307
  18.6 1.0 collective-permute-start
  20.0 1.8 %collective-permute-done.1.other_mask_ref = s32[4,512]{1,0:T(4,128)S(1)} collective-permute-done((s32[4,512]{1,0:T(4,128)S(1)}, s32[4,512]{1,0:T(4,128)S(1)}, u32[]{:S(2)}, u32[]{:S(2)}) %collective-permute-start.1) | collective-permute-done | bytes 8224 | tf_op jit(solution)/shard_map/ppermute | solution.py:290
  22.1 8.8 %shard_map.155 = (bf16[8,512,384]{2,1,0:T(8,128)(2,1)}, bf16[8,256,512]{2,1,0:T(8,128)(2,1)}, bf16[8,256,256]{2,1,0:T(8,128)(2,1)S(1)}, bf16[8,256,256]{2,1,0:T(...) custom-call(bf16[4,512,256]{2,1,0:T(8,128)(2,1)} %own_ref.1, ...), custom_call_target="tpu_custom_call" | custom-call | flops 1610612736 | bytes 9437184 | tf_op jit(solution)/shard_map/pallas_call | solution.py:312
  30.8 1.0 copy-done.13
  31.8 13.8 %all-to-all-done.tile_ref = bf16[64,64,256]{2,1,0:T(8,128)(2,1)} async-done(((bf16[64,64,256]{2,1,0:T(8,128)(2,1)}), bf16[64,64,256]{2,1,0:T(8,128)(2,1)}, u32[]{:S(2)}, u32[]{:S(2)}) %all-to-all-start) | async-done | bytes 2097184 | tf_op jit(solution)/shard_map/all_to_all | solution.py:307
  45.6 1.2 copy-done.14
  46.8 17.2 %shard_map.156 = bf16[64,40,256]{2,1,0:T(8,128)(2,1)} custom-call(bf16[64,64,256]{2,1,0:T(8,128)(2,1)} %all-to-all-done.tile_ref, bf16[8,512,384]{2,1,0:T(8,128)(2,1)} %get-tuple-element.11.k_ref, bf16[8,256,512]{2,1,0:T(8,128)(2,1)} %get-tuple-element.12.vt_ref, bf16[8,256,256]{2,1,0:T(8,128)(2,1)S(1)} %get-tuple-element.13.qt_ref, ...), custom_call_target="tpu_custom_call" | custom-call | flops 8589934592 | bytes 9437184 | tf_op jit(solution)/shard_map/pallas_call | solution.py:356
  64.0 7.0 %all-to-all-start.1 = ((bf16[64,40,256]{2,1,0:T(8,128)(2,1)}), bf16[64,40,256]{2,1,0:T(8,128)(2,1)S(1)}, u32[]{:S(2)}, u32[]{:S(2)}) async-start(bf16[64,40,256]{2,1,0:T(8,128)(2,1)} %shard_map.156), calls=%async_computation.1 | async-start | bytes 2621440 | tf_op jit(solution)/shard_map/all_to_all | solution.py:381
  71.0 0.9 slice.7.wk_ref
  71.9 1.2 copy.19
  73.2 16.1 %all-to-all-done.1.x_ref = bf16[64,40,256]{2,1,0:T(8,128)(2,1)S(1)} async-done(((bf16[64,40,256]{2,1,0:T(8,128)(2,1)}), bf16[64,40,256]{2,1,0:T(8,128)(2,1)S(1)}, u32[]{:S(2)}, u32[]{:S(2)}) %all-to-all-start.1) | async-done | bytes 1310752 | tf_op jit(solution)/shard_map/all_to_all | solution.py:381
  89.3 1.1 copy-done.15
  90.3 20.3 %shard_map.157 = bf16[2048,256]{1,0:T(8,128)(2,1)S(1)} custom-call(bf16[64,40,256]{2,1,0:T(8,128)(2,1)} %copy-done.15, f32[1,256]{1,0:T(1,128)S(1)} %bitcast.23, bf16[256,256]{1,0:T(8,128)(2,1)S(1)} %slice.7.wk_ref, bf16[1024,256]{1,0:T(8,128)(2,1)S(1)} %bitcast.18, bf16[256,256]{1,0:T(8,128)(2,1)S(1)} %copy-done.9, f32[1,256]{1,0:T(1,128)S(1)} %bitcast.24, ...), custom_call_target="tpu_custom_call" | custom-call | flops 8589934592 | bytes 4194304 | tf_op jit(solution)/shard_map/pallas_call | solution.py:383
  110.7 26.2 %all_to_all.15 = bf16[128,16,256]{2,1,0:T(8,128)(2,1)S(1)} all-to-all(bf16[128,16,256]{2,1,0:T(8,128)(2,1)S(1)} %bitcast.15), channel_id=1, replica_groups=mesh['grp'=2,'z'=4,'x'=4,'yh'=2,'core'=2] {'grp','z','x','yh','core'}, dimensions={0} | all-to-all | bytes 2097152 | tf_op jit(solution)/shard_map/all_to_all | solution.py:417
  136.8 0.3 reshape.38
  137.1 0.4 copy.22
  137.5 1.1 reshape.39
  (36 shorter events, 0.6 us)
Async XLA Ops:
  0.0 1.0 copy-start
  1.0 0.7 copy-start.2
  1.7 0.7 copy-start.3
  2.4 0.7 copy-start.4
  3.1 0.7 copy-start.5
  6.2 12.4 %copy-start.17 = (bf16[4,512,256]{2,1,0:T(8,128)(2,1)S(1)}, bf16[4,512,256]{2,1,0:T(8,128)(2,1)}, u32[]{:S(2)}) copy-start(bf16[4,512,256]{2,1,0:T(8,128)(2,1)} %own_ref.1) | copy-start | bytes 3145732
  6.2 13.4 %copy-start.1 = (s32[4,512]{1,0:T(4,128)S(1)}, s32[4,512]{1,0:T(4,128)}, u32[]{:S(2)}) copy-start(s32[4,512]{1,0:T(4,128)} %own_mask_ref.1) | copy-start | bytes 24580
  6.2 13.5 %copy-start.16 = (bf16[256,1024]{1,0:T(8,128)(2,1)S(1)}, bf16[256,1024]{1,0:T(8,128)(2,1)}, u32[]{:S(2)}) copy-start(bf16[256,1024]{1,0:T(8,128)(2,1)} %param.24) | copy-start | bytes 1572868
  6.2 15.9 %copy-start.10 = (f32[256]{0:T(256)S(1)}, f32[256]{0:T(256)}, u32[]{:S(2)}) copy-start(f32[256]{0:T(256)} %param.20) | copy-start | bytes 3076
  6.2 39.4 %all-to-all-start = ((bf16[64,64,256]{2,1,0:T(8,128)(2,1)}), bf16[64,64,256]{2,1,0:T(8,128)(2,1)}, u32[]{:S(2)}, u32[]{:S(2)}) async-start(bf16[64,64,256]{2,1,0:T(8,128)(2,1)} %shard_map.154), calls=%async_computation | async-start | bytes 4194304 | tf_op jit(solution)/shard_map/all_to_all | solution.py:307
  18.6 3.5 %collective-permute-start = (bf16[4,512,256]{2,1,0:T(8,128)(2,1)S(1)}, bf16[4,512,256]{2,1,0:T(8,128)(2,1)}, u32[]{:S(2)}, u32[]{:S(2)}) collective-permute-start(bf16[4,512,256]{2,1,0:T(8,128)(2,1)S(1)} %copy-done.17), channel_id=1, source_target_pairs={{0,1},{1,0},{2,3},{3,2},{4,5},{5,4},{6,7},{7,6},{8,9},{9,8},{10,11... | collective-permute-start | bytes 3145736 | tf_op jit(solution)/shard_map/ppermute | solution.py:291
  19.6 2.2 %collective-permute-start.1 = (s32[4,512]{1,0:T(4,128)S(1)}, s32[4,512]{1,0:T(4,128)S(1)}, u32[]{:S(2)}, u32[]{:S(2)}) collective-permute-start(s32[4,512]{1,0:T(4,128)S(1)} %copy-done.1), channel_id=1, source_target_pairs={{0,1},{1,0},{2,3},{3,2},{4,5},{5,4},{6,7},{7,6},{8,9},{9,8},{10,11... | collective-permute-start | bytes 24584 | tf_op jit(solution)/shard_map/ppermute | solution.py:290
  22.0 23.6 %copy-start.8 = (bf16[256,256]{1,0:T(8,128)(2,1)S(1)}, bf16[256,256]{1,0:T(8,128)(2,1)}, u32[]{:S(2)}) copy-start(bf16[256,256]{1,0:T(8,128)(2,1)} %wo_ref.2) | copy-start | bytes 393220
  30.8 1.0 copy-start.13
  45.6 1.2 copy-start.14
  64.0 26.3 %copy-start.6 = (bf16[256,1024]{1,0:T(8,128)(2,1)S(1)}, bf16[256,1024]{1,0:T(8,128)(2,1)}, u32[]{:S(2)}) copy-start(bf16[256,1024]{1,0:T(8,128)(2,1)} %w1_ref.1) | copy-start | bytes 1572868
  64.0 26.3 %copy-start.7 = (bf16[1024,256]{1,0:T(8,128)(2,1)S(1)}, bf16[1024,256]{1,0:T(8,128)(2,1)}, u32[]{:S(2)}) copy-start(bf16[1024,256]{1,0:T(8,128)(2,1)} %w2_ref.1) | copy-start | bytes 1572868
  64.0 26.3 %copy-start.9 = (bf16[256,256]{1,0:T(8,128)(2,1)S(1)}, bf16[256,256]{1,0:T(8,128)(2,1)}, u32[]{:S(2)}) copy-start(bf16[256,256]{1,0:T(8,128)(2,1)} %wo_ref.3) | copy-start | bytes 393220
  64.0 26.3 %copy-start.11 = (f32[256]{0:T(256)S(1)}, f32[256]{0:T(256)}, u32[]{:S(2)}) copy-start(f32[256]{0:T(256)} %param.26) | copy-start | bytes 3076
  64.0 26.3 %copy-start.12 = (f32[256]{0:T(256)S(1)}, f32[256]{0:T(256)}, u32[]{:S(2)}) copy-start(f32[256]{0:T(256)} %param.29) | copy-start | bytes 3076
  64.0 25.2 %all-to-all-start.1 = ((bf16[64,40,256]{2,1,0:T(8,128)(2,1)}), bf16[64,40,256]{2,1,0:T(8,128)(2,1)S(1)}, u32[]{:S(2)}, u32[]{:S(2)}) async-start(bf16[64,40,256]{2,1,0:T(8,128)(2,1)} %shard_map.156), calls=%async_computation.1 | async-start | bytes 2621440 | tf_op jit(solution)/shard_map/all_to_all | solution.py:381
  89.3 1.1 copy-start.15

commit v3 on v2

v3 whole, which is shorter than its diff:
```python
import functools
import math

import jax
import jax.numpy as jnp
import ml_dtypes
import numpy as np
from jax import lax
from jax.experimental import pallas as pl
from jax.experimental.pallas import tpu as pltpu
from jax.sharding import Mesh, PartitionSpec as P

EPSILON = 1e-05
HEADS = 8
HEAD = 32
WIDTH = 256
LENGTH = 512
HALF = 256
PEERS = 64
LOG2E = math.log2(math.e)
SCALE = HEAD**-0.5 * LOG2E
F32 = jnp.float32
BF16 = jnp.bfloat16
AXES = ("grp", "z", "x", "yh", "core")
PLANE = ("grp", "z", "x", "yh")
VMEM_LIMIT = 40 * 1024 * 1024
SLOTS = 3
VMEM_WHOLE = 60 * 2**20
VMEM_TILE = 58 * 2**20
ROW_BOUND = 40.0
COLUMN_BOUND = 60.0

MASK_TERM = 1e9 * HEAD**0.5


def mask_parts():
    parts = []
    rest = MASK_TERM
    for _ in range(3):
        part = float(np.asarray(rest, ml_dtypes.bfloat16))
        parts.append(part)
        rest -= part
    return parts


def nt(a, b):
    return lax.dot_general(a, b, (((1,), (1,)), ((), ())), preferred_element_type=F32)


def tn(a, b):
    return lax.dot_general(a, b, (((0,), (0,)), ((), ())), preferred_element_type=F32)


def nn(a, b):
    return jnp.dot(a, b, preferred_element_type=F32)


def norm(x, gain):
    average = jnp.mean(x, axis=-1, keepdims=True)
    center = x - average
    spread = jnp.mean(center * center, axis=-1, keepdims=True)
    return (center * lax.rsqrt(spread + EPSILON) * gain).astype(BF16)


def position():
    q = (lax.axis_index("z") * 4 + lax.axis_index("x")) * 2 + lax.axis_index("yh")
    return lax.axis_index("grp"), q, lax.axis_index("core")


def bias_kernel(pair_ref, gain_ref, weight_ref, chain_ref, inter_ref, out_ref):
    grp, q, core = position()
    normed = norm(pair_ref[...].astype(F32), gain_ref[...])
    bias = nt(weight_ref[...], normed)
    chain = chain_ref[...]
    cols = jnp.where(grp == 0, chain[:, :256], chain[:, 256:])
    place = lax.broadcasted_iota(jnp.int32, (8, LENGTH), 1)
    wanted = 16 * q + 8 * core + lax.broadcasted_iota(jnp.int32, (8, LENGTH), 0)
    rows = jnp.sum(jnp.where(place == wanted, chain, 0), axis=1, keepdims=True)
    cross = (rows != cols).astype(F32)
    row = lax.broadcasted_iota(jnp.int32, (8, 8), 0)
    col = lax.broadcasted_iota(jnp.int32, (8, 8), 1)
    inter = jnp.sum(jnp.where(row == col, inter_ref[...], 0.0), axis=1, keepdims=True)
    parts = [
        bias[:, ii * 256 : (ii + 1) * 256] + inter * cross[ii : ii + 1] for ii in range(8)
    ]
    stacked = jnp.stack(parts, axis=0)
    tile = jnp.swapaxes(stacked, 0, 1).reshape(64, 256).astype(BF16)

    def put(p, carry):
        out_ref[p] = tile
        return carry

    lax.fori_loop(0, PEERS, put, 0)


def spread(qt, h, mask_rows):
    at = h % 4
    queries = qt.shape[1]
    pieces = []
    if at:
        pieces.append(jnp.zeros((HEAD * at, queries), BF16))
    pieces.append(qt[h * HEAD : (h + 1) * HEAD])
    if at < 3:
        pieces.append(jnp.zeros((HEAD * (3 - at), queries), BF16))
    pieces.append(mask_rows)
    return jnp.concatenate(pieces, axis=0)


def augment(keys, mask_tile):
    return [jnp.concatenate([keys[:, g * 128 : (g + 1) * 128], mask_tile], axis=1) for g in range(2)]


def score_bound(keys, qt):
    feat = lax.broadcasted_iota(jnp.int32, (WIDTH, 128), 0) // HEAD
    lane = lax.broadcasted_iota(jnp.int32, (WIDTH, 128), 1)
    ones = (feat == lane).astype(F32).astype(BF16)
    feat_t = lax.broadcasted_iota(jnp.int32, (16, WIDTH), 1) // HEAD
    row_t = lax.broadcasted_iota(jnp.int32, (16, WIDTH), 0)
    ones_t = (feat_t == row_t).astype(F32).astype(BF16)
    key_norm = jnp.max(nn(keys * keys, ones))
    query_norm = jnp.max(nn(ones_t, qt * qt))
    return jnp.sqrt(key_norm * 1.02) * jnp.sqrt(query_norm * 1.02) * SCALE


def any_present(tile):
    lane = lax.broadcasted_iota(jnp.int32, tile.shape, 1)
    return jnp.max(jnp.where(lane == 0, tile, -1e30)) > -1.0


def score_powers(keys, mask_tile, qt):
    mask_rows = jnp.ones((128, qt.shape[1]), BF16)
    augmented = augment(keys, mask_tile)
    out = []
    scores = nn(augmented[0], spread(qt, 0, mask_rows))
    for h in range(HEADS):
        later = None
        if h + 1 < HEADS:
            later = nn(augmented[(h + 1) // 4], spread(qt, h + 1, mask_rows))
        out.append(jnp.exp2(scores * SCALE).astype(BF16))
        scores = later
    return out


def blend(vt, h, powers):
    ones_v = jnp.ones((16, LENGTH), BF16)
    blended = nn(jnp.concatenate([vt[h * HEAD : (h + 1) * HEAD], ones_v], axis=0), powers)
    return blended[:HEAD] / blended[HEAD : HEAD + 1]


def attend(parts, bias, exact):
    mask_rows = jnp.ones((128, HALF), BF16)
    augmented = [augment(keys, tile) for keys, tile, _, _ in parts]
    units = [(part, h) for part in range(len(parts)) for h in range(HEADS)]

    def score(part, h):
        return nn(augmented[part][h // 4], spread(parts[part][3], h, mask_rows))

    out = []
    scores = score(*units[0])
    powers = None
    for at, (part, h) in enumerate(units):
        later = score(*units[at + 1]) if at + 1 < len(units) else None
        scaled = scores * SCALE
        if bias is not None:
            scaled = scaled + bias[h]
        if exact:
            scaled = scaled - jnp.max(scaled, axis=0, keepdims=True)
        now = jnp.exp2(scaled).astype(BF16)
        if at:
            before = units[at - 1]
            out.append(blend(parts[before[0]][2], before[1], powers))
        powers = now
        scores = later
    out.append(blend(parts[units[-1][0]][2], units[-1][1], powers))
    return [
        jnp.concatenate(out[part * HEADS : (part + 1) * HEADS], axis=0)
        for part in range(len(parts))
    ]


def project_kernel(
    own_ref, other_ref, mask_ref, own_mask_ref, other_mask_ref, gain_ref, wk_ref, wt_ref,
    k_ref, vt_ref, qt_ref, gt_ref, xq_ref, mask_out_ref, powers_ref, safe_ref,
):
    step = pl.program_id(0)
    _, _, core = position()
    x = jnp.where(step < 4, own_ref[0].astype(F32), other_ref[0].astype(F32))
    normed = norm(x, gain_ref[...])
    keys = nn(normed, wk_ref[...]).astype(BF16)
    k_ref[0, :, :WIDTH] = keys
    lane = lax.broadcasted_iota(jnp.int32, (8, 128), 1)
    row = lax.broadcasted_iota(jnp.int32, (8, 128), 0)
    consts = mask_parts()
    pick = jnp.zeros((8, 128), F32)
    for at, value in enumerate(consts):
        pick = jnp.where((lane == at) & (row == step), value, pick)
    tile = nn(mask_ref[...] - 1, pick.astype(BF16))
    mask_tile = tile.astype(BF16)
    k_ref[0, :, WIDTH:] = mask_tile
    vt_ref[0] = nt(wt_ref[2 * WIDTH : 3 * WIDTH], normed).astype(BF16)

    def half(a):
        rows = a.reshape(32, 2, 8, WIDTH)
        return jnp.where(core == 0, rows[:, 0], rows[:, 1]).reshape(HALF, WIDTH)

    xq = half(x)
    xq_ref[0] = xq.astype(BF16)
    normed_q = half(normed.astype(F32)).astype(BF16)
    qt = nt(wt_ref[:WIDTH], normed_q).astype(BF16)
    qt_ref[0] = qt
    powers = score_powers(keys, mask_tile, qt)
    for h in range(HEADS):
        powers_ref[0, h] = powers[h]
    bound = score_bound(keys, qt)
    present = any_present(tile)
    safe = (bound <= ROW_BOUND) & present
    safe_ref[0] = jnp.where(safe, 1.0, 0.0) + jnp.zeros((8, 128), F32)
    gt_ref[0] = nt(wt_ref[3 * WIDTH :], normed_q).astype(BF16)

    @pl.when(step == 0)
    def _():
        own = own_mask_ref[...].astype(F32)
        other = other_mask_ref[...].astype(F32)
        first = jnp.where(core == 0, own, other)
        second = jnp.where(core == 0, other, own)
        mask = jnp.concatenate([first, second], axis=0).astype(BF16)
        i = lax.broadcasted_iota(jnp.int32, (LENGTH, HALF), 0)
        l = lax.broadcasted_iota(jnp.int32, (LENGTH, HALF), 1)
        pick = (i == (l // 8) * 16 + core * 8 + l % 8).astype(F32).astype(BF16)
        mask_out_ref[...] = nn(mask, pick).astype(BF16)


def bias_blocks(tile_ref):
    row = lax.broadcasted_iota(jnp.int32, (HALF, HALF), 0)
    col = lax.broadcasted_iota(jnp.int32, (HALF, HALF), 1)
    eye = (row == col).astype(F32).astype(BF16)
    for g in range(2):
        for pair in range(4):
            block = tile_ref[g * 32 : (g + 1) * 32, pair * 16 : (pair + 1) * 16, :]
            block = block.astype(F32).reshape(32, 2, 8, 256)
            for k in range(2):
                rows = block[:, k].reshape(HALF, 256).astype(BF16)
                yield pair * 2 + k, g, nt(eye, rows) * LOG2E


def row_kernel(
    safe_ref, wo_ref, mask_ref, tile_ref, powers_ref, vt_ref, gt_ref, xq_ref, k_ref, qt_ref,
    out_ref, powers_here, vt_here, gt_here, xq_here, bias_ref, factor_ref, o_ref, y_ref, result_ref,
    k_here, qt_here, slot_sem, out_sem,
):
    _, _, core = position()

    def fetch(step):
        slot = lax.rem(step, SLOTS)
        pairs = [(powers_ref, powers_here), (vt_ref, vt_here), (gt_ref, gt_here), (xq_ref, xq_here)]
        return [
            pltpu.make_async_copy(source.at[step], target.at[slot], slot_sem.at[slot, n])
            for n, (source, target) in enumerate(pairs)
        ]

    for step in range(SLOTS):
        for copy in fetch(step):
            copy.start()

    largest = jnp.zeros((8, HALF), F32)
    for h, g, block in bias_blocks(tile_ref):
        factor_ref[h, g * 256 : (g + 1) * 256, :] = jnp.exp2(block).astype(BF16)
        size = jnp.abs(block).reshape(32, 8, HALF)
        largest = jnp.maximum(largest, jnp.max(size, axis=0))
    bias_safe = jnp.max(largest) <= ROW_BOUND

    def sequence(step, carry):
        slot = lax.rem(step, SLOTS)
        for copy in fetch(step):
            copy.wait()
        safe = bias_safe & (jnp.max(safe_ref[step]) > 0.5)

        @pl.when(safe)
        def _():
            now = powers_here[slot, 0] * factor_ref[0]
            for h in range(HEADS):
                later = None
                if h + 1 < HEADS:
                    later = powers_here[slot, h + 1] * factor_ref[h + 1]
                o_ref[h * HEAD : (h + 1) * HEAD, :] = blend(vt_here[slot], h, now)
                now = later

        @pl.when(jnp.logical_not(safe))
        def _():
            pltpu.sync_copy(k_ref.at[step], k_here)
            pltpu.sync_copy(qt_ref.at[step], qt_here)
            for h, g, block in bias_blocks(tile_ref):
                bias_ref[h, g * 256 : (g + 1) * 256, :] = block
            part = (k_here[:, :WIDTH], k_here[:, WIDTH:], vt_here[slot], qt_here[...])
            o_ref[...] = attend([part], bias_ref, True)[0]

        gated = (o_ref[...] * jax.nn.sigmoid(gt_here[slot].astype(F32))).astype(BF16)
        y = xq_here[slot].astype(F32) + tn(gated, wo_ref[...])
        s = lax.rem(step + 4 * core, 8)
        for j in range(2):
            y_ref[j, pl.ds(s, HALF, stride=8), :] = y[:, j * 128 : (j + 1) * 128]

        @pl.when(step + SLOTS < 8)
        def _():
            for copy in fetch(step + SLOTS):
                copy.start()

        return carry

    lax.fori_loop(0, 8, sequence, 0)
    for j in range(2):
        result_ref[:, j * 32 : (j + 1) * 32, :] = y_ref[j].astype(BF16).reshape(PEERS, 32, 128)
        result_ref[j * 32 : (j + 1) * 32, 64:, :] = jnp.broadcast_to(
            mask_ref[:, j * 128 : (j + 1) * 128][None], (32, 8, 128)
        )
    out = pltpu.make_async_copy(result_ref, out_ref, out_sem)
    out.start()
    out.wait()


def column_kernel(
    x_ref, gain_ref, wk_ref, wt_ref, wo_ref, gain2_ref, w1_ref, w2_ref, out_ref,
    x32_ref, o_ref, y_ref,
):
    _, q, _ = position()
    x32_ref[...] = x_ref[...].astype(F32).reshape(PEERS, 9, 8, 128)

    def residue(r, carry):
        x = jnp.concatenate([x32_ref[:, 4 * j + r].reshape(LENGTH, 128) for j in range(2)], axis=1)
        normed = norm(x, gain_ref[...])
        keys = nn(normed, wk_ref[...]).astype(BF16)
        lane = lax.broadcasted_iota(jnp.int32, (128, 128), 1)
        row = lax.broadcasted_iota(jnp.int32, (128, 128), 0)
        pick = jnp.zeros((128, 128), F32)
        for at, value in enumerate(mask_parts()):
            pick = jnp.where((lane == at) & (row == 4 * q + r), value, pick)
        absent = (x32_ref[:, 8].reshape(LENGTH, 128) - 1.0).astype(BF16)
        tile = nn(absent, pick.astype(BF16))
        mask_tile = tile.astype(BF16)
        vt = nt(wt_ref[2 * WIDTH : 3 * WIDTH], normed).astype(BF16)
        qt = nt(wt_ref[:WIDTH], normed).astype(BF16)
        gt = nt(wt_ref[3 * WIDTH :], normed).astype(BF16)
        parts = [(keys, mask_tile, vt, qt[:, n * HALF : (n + 1) * HALF]) for n in range(2)]
        safe = (score_bound(keys, qt) <= COLUMN_BOUND) & any_present(tile)

        @pl.when(safe)
        def _():
            for n, o in enumerate(attend(parts, None, False)):
                o_ref[n] = o

        @pl.when(jnp.logical_not(safe))
        def _():
            for n, o in enumerate(attend(parts, None, True)):
                o_ref[n] = o

        for n in range(2):
            cols = slice(n * HALF, (n + 1) * HALF)
            gated = (o_ref[n] * jax.nn.sigmoid(gt[:, cols].astype(F32))).astype(BF16)
            one = x[cols] + tn(gated, wo_ref[...])
            two = one.astype(BF16).astype(F32)
            hidden = jnp.maximum(nn(norm(two, gain2_ref[...]), w1_ref[...]), 0.0).astype(BF16)
            y = two + nn(hidden, w2_ref[...])
            for j in range(2):
                y_ref[j, pl.ds(n * 4 * HALF + r, HALF, stride=4), :] = y[:, j * 128 : (j + 1) * 128]
        return carry

    lax.fori_loop(0, 4, residue, 0)
    for j in range(2):
        out_ref[:, j * 128 : (j + 1) * 128] = y_ref[j].astype(BF16)


def whole(*shape):
    return pl.BlockSpec(shape, lambda i: (0,) * len(shape))


def each(count, *shape):
    return pl.BlockSpec((count,) + shape, lambda i: (i,) + (0,) * len(shape))


def body(
    homolog,
    pair_state,
    mask,
    chain,
    row_gain,
    pair_gain,
    pair_weight,
    interchain,
    row_in,
    row_out,
    col_gain,
    col_in,
    col_out,
    ff_gain,
    ff_expand,
    ff_shrink,
):
    params = pltpu.CompilerParams(vmem_limit_bytes=VMEM_LIMIT)
    here = pl.BlockSpec(memory_space=pltpu.VMEM)
    away = pl.BlockSpec(memory_space=pltpu.HBM)
    swap = [(0, 1), (1, 0)]
    other_mask = lax.ppermute(mask, "core", swap)
    other = lax.ppermute(homolog, "core", swap)

    payload = pl.pallas_call(
        bias_kernel,
        grid=(1,),
        out_shape=jax.ShapeDtypeStruct((PEERS, 64, 256), BF16),
        in_specs=[whole(2048, 128), whole(1, 128), whole(8, 128), whole(1, LENGTH), whole(1, 8)],
        out_specs=whole(PEERS, 64, 256),
        compiler_params=pltpu.CompilerParams(vmem_limit_bytes=VMEM_WHOLE),
    )(
        pair_state.reshape(2048, 128),
        pair_gain.reshape(1, 128),
        pair_weight,
        chain.reshape(1, LENGTH),
        interchain.reshape(1, 8),
    )
    tiles = lax.all_to_all(payload, PLANE, 0, 0, tiled=True)

    row_in_t = row_in.T
    col_in_t = col_in.T
    mask_t = jnp.concatenate([mask, other_mask], axis=0).astype(BF16).T
    keys, vt, qt, gt, xq, mask_half, powers, safe = pl.pallas_call(
        project_kernel,
        grid=(8,),
        out_shape=[
            jax.ShapeDtypeStruct((8, LENGTH, WIDTH + 128), BF16),
            jax.ShapeDtypeStruct((8, WIDTH, LENGTH), BF16),
            jax.ShapeDtypeStruct((8, WIDTH, HALF), BF16),
            jax.ShapeDtypeStruct((8, WIDTH, HALF), BF16),
            jax.ShapeDtypeStruct((8, HALF, WIDTH), BF16),
            jax.ShapeDtypeStruct((8, HALF), BF16),
            jax.ShapeDtypeStruct((8, HEADS, LENGTH, HALF), BF16),
            jax.ShapeDtypeStruct((8, 8, 128), F32),
        ],
        in_specs=[
            pl.BlockSpec((1, LENGTH, WIDTH), lambda i: (jnp.minimum(i, 3), 0, 0)),
            pl.BlockSpec((1, LENGTH, WIDTH), lambda i: (jnp.maximum(i - 4, 0), 0, 0)),
            whole(LENGTH, 8),
            whole(4, LENGTH),
            whole(4, LENGTH),
            whole(1, WIDTH),
            whole(WIDTH, WIDTH),
            whole(4 * WIDTH, WIDTH),
        ],
        out_specs=[
            each(1, LENGTH, WIDTH + 128),
            each(1, WIDTH, LENGTH),
            each(1, WIDTH, HALF),
            each(1, WIDTH, HALF),
            each(1, HALF, WIDTH),
            whole(8, HALF),
            each(1, HEADS, LENGTH, HALF),
            each(1, 8, 128),
        ],
        compiler_params=pltpu.CompilerParams(vmem_limit_bytes=VMEM_WHOLE),
        cost_estimate=pl.CostEstimate(
            flops=8 * 8 * 512 * 256 * 768, bytes_accessed=25 * 2**20, transcendentals=8 * 2**20
        ),
    )(
        homolog,
        other,
        mask_t,
        mask,
        other_mask,
        row_gain.reshape(1, WIDTH),
        row_in[:, WIDTH : 2 * WIDTH],
        row_in_t,
    )

    after_rows = pl.pallas_call(
        row_kernel,
        out_shape=jax.ShapeDtypeStruct((PEERS, 72, 128), BF16),
        grid=(1,),
        in_specs=[whole(8, 8, 128), whole(WIDTH, WIDTH), whole(8, HALF), here] + [away] * 6,
        out_specs=away,
        scratch_shapes=[
            pltpu.VMEM((SLOTS, HEADS, LENGTH, HALF), BF16),
            pltpu.VMEM((SLOTS, WIDTH, LENGTH), BF16),
            pltpu.VMEM((SLOTS, WIDTH, HALF), BF16),
            pltpu.VMEM((SLOTS, HALF, WIDTH), BF16),
            pltpu.VMEM((HEADS, LENGTH, HALF), F32),
            pltpu.VMEM((HEADS, LENGTH, HALF), BF16),
            pltpu.VMEM((WIDTH, HALF), F32),
            pltpu.VMEM((2, 8 * HALF, 128), F32),
            pltpu.VMEM((PEERS, 72, 128), BF16),
            pltpu.VMEM((LENGTH, WIDTH + 128), BF16),
            pltpu.VMEM((WIDTH, HALF), BF16),
            pltpu.SemaphoreType.DMA((SLOTS, 4)),
            pltpu.SemaphoreType.DMA,
        ],
        compiler_params=pltpu.CompilerParams(vmem_limit_bytes=VMEM_TILE),
        cost_estimate=pl.CostEstimate(
            flops=8 * 8 * 512 * 256 * 512, bytes_accessed=20 * 2**20, transcendentals=0
        ),
    )(safe, row_out, mask_half, tiles, powers, vt, gt, xq, keys, qt)

    columns = lax.all_to_all(after_rows, PLANE, 0, 0, tiled=True)

    finished = pl.pallas_call(
        column_kernel,
        out_shape=jax.ShapeDtypeStruct((4 * LENGTH, WIDTH), BF16),
        grid=(1,),
        in_specs=[here] * 8,
        out_specs=whole(4 * LENGTH, WIDTH),
        scratch_shapes=[
            pltpu.VMEM((PEERS, 9, 8, 128), F32),
            pltpu.VMEM((2, WIDTH, HALF), F32),
            pltpu.VMEM((2, 4 * LENGTH, 128), F32),
        ],
        compiler_params=params,
        cost_estimate=pl.CostEstimate(
            flops=2 * 8 * 8 * 512 * 256 * 512, bytes_accessed=4 * 2**20, transcendentals=8 * 2**20
        ),
    )(
        columns,
        col_gain.reshape(1, WIDTH),
        col_in[:, WIDTH : 2 * WIDTH],
        col_in_t,
        col_out,
        ff_gain.reshape(1, WIDTH),
        ff_expand,
        ff_shrink,
    )

    back = lax.all_to_all(finished.reshape(128, 16, WIDTH), AXES, 0, 0, tiled=True)
    back = back.reshape(32, 2, 2, 4, 4, WIDTH)
    return jnp.transpose(back, (3, 0, 2, 1, 4, 5)).reshape(4, LENGTH, WIDTH)


def solution(mesh):
    inner = Mesh(mesh.devices.reshape(2, 4, 4, 2, 2), AXES)
    dap = ("z", "x", "yh", "core")
    return jax.shard_map(
        body,
        mesh=inner,
        in_specs=(P(AXES, None, None), P(dap, "grp", None), P(AXES, None)) + (P(),) * 13,
        out_specs=P(AXES, None, None),
        check_vma=False,
    )
```

time: 139 us -> 162 us (1.17)
  Pallas kernels: 48.7 us -> 84.8 us
  waiting for transfers between devices: 31.8 us -> 24.4 us
  local copies, waits for them, and re-layouts: 11.3 us -> 5.85 us
    pallas_call x2, Pallas kernels: 37.5 us -> 65.3 us  [the longest x1 44.4 us: body(): pl.pallas_call(row_kernel, out_shape=jax.ShapeDtypeStruct((PEERS, 72, 128...]
    pallas_call x1, Pallas kernels: 8.79 us -> 15.9 us  [body(): pl.pallas_call(project_kernel, grid=(8,), out_shape=[jax.ShapeDtypeStruct...]
    all_to_all x1, waiting for transfers between devices: 13.8 us -> 7.26 us  [body(): tiles = lax.all_to_all(payload, PLANE, 0, 0, tiled=True)]
    unnamed x38 -> x22, local copies, waits for them, and re-layouts: 8.46 us -> 2.62 us
  transfers between devices with their start and end apart: 4 -> 4, of which waited for: 4 -> 3; matrix products, arithmetic and copies ran while one was open for 2% -> 2% of each run, Pallas kernels for 6% -> 10%
where the time goes in v3:
time: 162 us
  Pallas kernels  84.8 us (52%)
  blocking collectives  26.1 us (16%)
  waiting for transfers between devices  24.4 us (15%)
  starting transfers between devices  20.2 us (12%)
  local copies, waits for them, and re-layouts  5.85 us (4%)
    pallas_call x1, Pallas kernels, body(): pl.pallas_call(row_kernel, out_shape=jax.ShapeDtypeStruct((PEERS, 72, 128...  44.4 us
    all_to_all x1, blocking collectives, body(): lax.all_to_all(finished.reshape(128, 16, WIDTH), AXES, 0, 0, tiled=True)  26.1 us
    pallas_call x1, Pallas kernels, body(): pl.pallas_call(column_kernel, out_shape=jax.ShapeDtypeStruct((4 * LENGTH,...  20.9 us
    all_to_all x1, waiting for transfers between devices, body(): columns = lax.all_to_all(after_rows, PLANE, 0, 0, tiled=True)  16.7 us
    pallas_call x1, Pallas kernels, body(): pl.pallas_call(project_kernel, grid=(8,), out_shape=[jax.ShapeDtypeStruct...  15.9 us
    all_to_all x1, starting transfers between devices, body(): tiles = lax.all_to_all(payload, PLANE, 0, 0, tiled=True)  12.1 us
    all_to_all x1, waiting for transfers between devices, body(): tiles = lax.all_to_all(payload, PLANE, 0, 0, tiled=True)  7.26 us
    all_to_all x1, starting transfers between devices, body(): columns = lax.all_to_all(after_rows, PLANE, 0, 0, tiled=True)  6.98 us
  transfers between devices with their start and end apart: 4, of which 3 were waited for; matrix products, arithmetic and copies ran while one was open for 2% of the time, Pallas kernels for 10%

profile of v3, /device:TPU:1, one launch (start us, length us, event | category | flops | bytes accessed | tf_op | source)
XLA Modules:
  0.0 161.5 jit_solution(16703463174914962280)
XLA Ops:
  0.0 3.6 %shard_map.155 = bf16[64,64,256]{2,1,0:T(8,128)(2,1)} custom-call(bf16[2048,128]{1,0:T(8,128)(2,1)} %bitcast.20, f32[1,128]{1,0:T(1,128)} %bitcast.23, bf16[8,128]{1,0:T(8,128)(2,1)} %weight_ref.1, s32[1,512]{1,0:T(1,128)} %bitcast.22, f32[1,8]{1,0:T(1,128)} %bitcast.24), custom_call_target="tpu_custom_call" | custom-call | tf_op jit(solution)/shard_map/pallas_call | solution.py:405
  3.6 12.1 %all-to-all-start = ((bf16[64,64,256]{2,1,0:T(8,128)(2,1)}), bf16[64,64,256]{2,1,0:T(8,128)(2,1)S(1)}, u32[]{:S(2)}, u32[]{:S(2)}) async-start(bf16[64,64,256]{2,1,0:T(8,128)(2,1)} %shard_map.155), calls=%async_computation | async-start | bytes 4194304 | tf_op jit(solution)/shard_map/all_to_all | solution.py:419
  15.7 1.0 collective-permute-start
  16.7 0.1 collective-permute-start.1
  16.8 1.0 copy.17
  17.8 0.7 slice.6.wk_ref
  18.5 0.4 collective-permute-done.1.other_mask_ref
  18.9 0.8 copy.18.mask_ref
  19.7 15.9 %shard_map.154 = (bf16[8,512,384]{2,1,0:T(8,128)(2,1)}, bf16[8,256,512]{2,1,0:T(8,128)(2,1)}, bf16[8,256,256]{2,1,0:T(8,128)(2,1)}, bf16[8,256,256]{2,1,0:T(8,12...) custom-call(bf16[4,512,256]{2,1,0:T(8,128)(2,1)} %own_ref.1, ...), custom_call_target="tpu_custom_call" | custom-call | flops 6442450944 | bytes 26214400 | tf_op jit(solution)/shard_map/pallas_call | solution.py:424
  35.6 7.3 %all-to-all-done.tile_ref = bf16[64,64,256]{2,1,0:T(8,128)(2,1)S(1)} async-done(((bf16[64,64,256]{2,1,0:T(8,128)(2,1)}), bf16[64,64,256]{2,1,0:T(8,128)(2,1)S(1)}, u32[]{:S(2)}, u32[]{:S(2)}) %all-to-all-start) | async-done | bytes 2097184 | tf_op jit(solution)/shard_map/all_to_all | solution.py:419
  42.9 1.4 copy-done.5
  44.2 44.4 %shard_map.156 = bf16[64,72,128]{2,1,0:T(8,128)(2,1)} custom-call(f32[8,8,128]{2,1,0:T(8,128)} %get-tuple-element.13.safe_ref, bf16[256,256]{1,0:T(8,128)(2,1)} %wo_ref.2, bf16[8,256]{1,0:T(8,128)(2,1)} %get-tuple-element.14.mask_ref, bf16[64,64,256]{2,1,0:T(8,128)(2,1)} %copy-done.5, bf16[8,8,512,256]{3,2,1,0:T(8,128)(2,1)} %get-tuple-element.15.powers_ref, ...), custom_call_target="tpu_custom_call" | custom-call | flops 4294967296 | bytes 20971520 | tf_op jit(solution)/shard_map/pallas_call | solution.py:472
  88.6 0.0 copy-start.7
  88.6 0.0 copy-start
  88.7 0.0 copy-start.1
  88.7 0.0 copy-start.2
  88.7 7.0 %all-to-all-start.1 = ((bf16[64,72,128]{2,1,0:T(8,128)(2,1)}), bf16[64,72,128]{2,1,0:T(8,128)(2,1)S(1)}, u32[]{:S(2)}, u32[]{:S(2)}) async-start(bf16[64,72,128]{2,1,0:T(8,128)(2,1)} %shard_map.156), calls=%async_computation.1 | async-start | bytes 2359296 | tf_op jit(solution)/shard_map/all_to_all | solution.py:499
  95.7 0.2 copy.19
  95.9 16.7 %all-to-all-done.1.x_ref = bf16[64,72,128]{2,1,0:T(8,128)(2,1)S(1)} async-done(((bf16[64,72,128]{2,1,0:T(8,128)(2,1)}), bf16[64,72,128]{2,1,0:T(8,128)(2,1)S(1)}, u32[]{:S(2)}, u32[]{:S(2)}) %all-to-all-start.1) | async-done | bytes 1179680 | tf_op jit(solution)/shard_map/all_to_all | solution.py:499
  112.7 20.9 %shard_map.157 = bf16[2048,256]{1,0:T(8,128)(2,1)S(1)} custom-call(bf16[64,72,128]{2,1,0:T(8,128)(2,1)S(1)} %all-to-all-done.1.x_ref, f32[1,256]{1,0:T(1,128)S(1)} %bitcast.17, bf16[256,256]{1,0:T(8,128)(2,1)S(1)} %slice.7.wk_ref, bf16[1024,256]{1,0:T(8,128)(2,1)S(1)} %bitcast.16, bf16[256,256]{1,0:T(8,128)(2,1)S(1)} %copy-done.2, f32[1,256]{1,0:T(1,128)S(1)} %bitcast.18, ...), custom_call_target="tpu_custom_call" | custom-call | flops 8589934592 | bytes 4194304 | tf_op jit(solution)/shard_map/pallas_call | solution.py:501
  133.6 26.1 %all_to_all.15 = bf16[128,16,256]{2,1,0:T(8,128)(2,1)S(1)} all-to-all(bf16[128,16,256]{2,1,0:T(8,128)(2,1)S(1)} %bitcast.15), channel_id=1, replica_groups=mesh['grp'=2,'z'=4,'x'=4,'yh'=2,'core'=2] {'grp','z','x','yh','core'}, dimensions={0} | all-to-all | bytes 2097152 | tf_op jit(solution)/shard_map/all_to_all | solution.py:527
  159.7 0.3 reshape.38
  160.0 0.4 copy.22
  160.4 1.1 reshape.39
  (20 shorter events, 0.1 us)
Async XLA Ops:
  3.6 13.1 %copy-start.8 = (s32[4,512]{1,0:T(4,128)S(1)}, s32[4,512]{1,0:T(4,128)}, u32[]{:S(2)}) copy-start(s32[4,512]{1,0:T(4,128)} %own_mask_ref.1) | copy-start | bytes 24580
  3.6 13.3 %copy-start.6 = (bf16[256,1024]{1,0:T(8,128)(2,1)S(1)}, bf16[256,1024]{1,0:T(8,128)(2,1)}, u32[]{:S(2)}) copy-start(bf16[256,1024]{1,0:T(8,128)(2,1)} %param.24) | copy-start | bytes 1572868
  3.6 39.3 %all-to-all-start = ((bf16[64,64,256]{2,1,0:T(8,128)(2,1)}), bf16[64,64,256]{2,1,0:T(8,128)(2,1)S(1)}, u32[]{:S(2)}, u32[]{:S(2)}) async-start(bf16[64,64,256]{2,1,0:T(8,128)(2,1)} %shard_map.155), calls=%async_computation | async-start | bytes 4194304 | tf_op jit(solution)/shard_map/all_to_all | solution.py:419
  15.7 4.0 %collective-permute-start = (bf16[4,512,256]{2,1,0:T(8,128)(2,1)}, bf16[4,512,256]{2,1,0:T(8,128)(2,1)}, u32[]{:S(2)}, u32[]{:S(2)}) collective-permute-start(bf16[4,512,256]{2,1,0:T(8,128)(2,1)} %own_ref.1), channel_id=1, source_target_pairs={{0,1},{1,0},{2,3},{3,2},{4,5},{5,4},{6,7},{7,6},{8,9},{9,8},{10,11... | collective-permute-start | bytes 3145736 | tf_op jit(solution)/shard_map/ppermute | solution.py:403
  16.7 2.2 %collective-permute-start.1 = (s32[4,512]{1,0:T(4,128)S(1)}, s32[4,512]{1,0:T(4,128)S(1)}, u32[]{:S(2)}, u32[]{:S(2)}) collective-permute-start(s32[4,512]{1,0:T(4,128)S(1)} %copy-done.8), channel_id=1, source_target_pairs={{0,1},{1,0},{2,3},{3,2},{4,5},{5,4},{6,7},{7,6},{8,9},{9,8},{10,11... | collective-permute-start | bytes 24584 | tf_op jit(solution)/shard_map/ppermute | solution.py:402
  18.9 0.8 copy-start.9
  42.9 1.4 copy-start.5
  88.6 7.1 %copy-start.7 = (bf16[256,1024]{1,0:T(8,128)(2,1)S(1)}, bf16[256,1024]{1,0:T(8,128)(2,1)}, u32[]{:S(2)}) copy-start(bf16[256,1024]{1,0:T(8,128)(2,1)} %param.27) | copy-start | bytes 1572868
  88.6 24.0 %copy-start = (bf16[256,1024]{1,0:T(8,128)(2,1)S(1)}, bf16[256,1024]{1,0:T(8,128)(2,1)}, u32[]{:S(2)}) copy-start(bf16[256,1024]{1,0:T(8,128)(2,1)} %w1_ref.1) | copy-start | bytes 1572868
  88.7 24.0 %copy-start.1 = (bf16[1024,256]{1,0:T(8,128)(2,1)S(1)}, bf16[1024,256]{1,0:T(8,128)(2,1)}, u32[]{:S(2)}) copy-start(bf16[1024,256]{1,0:T(8,128)(2,1)} %w2_ref.1) | copy-start | bytes 1572868
  88.7 24.0 %copy-start.2 = (bf16[256,256]{1,0:T(8,128)(2,1)S(1)}, bf16[256,256]{1,0:T(8,128)(2,1)}, u32[]{:S(2)}) copy-start(bf16[256,256]{1,0:T(8,128)(2,1)} %wo_ref.3) | copy-start | bytes 393220
  88.7 24.0 %copy-start.3 = (f32[256]{0:T(256)S(1)}, f32[256]{0:T(256)}, u32[]{:S(2)}) copy-start(f32[256]{0:T(256)} %param.26) | copy-start | bytes 3076
  88.7 24.0 %copy-start.4 = (f32[256]{0:T(256)S(1)}, f32[256]{0:T(256)}, u32[]{:S(2)}) copy-start(f32[256]{0:T(256)} %param.29) | copy-start | bytes 3076
  88.7 24.0 %all-to-all-start.1 = ((bf16[64,72,128]{2,1,0:T(8,128)(2,1)}), bf16[64,72,128]{2,1,0:T(8,128)(2,1)S(1)}, u32[]{:S(2)}, u32[]{:S(2)}) async-start(bf16[64,72,128]{2,1,0:T(8,128)(2,1)} %shard_map.156), calls=%async_computation.1 | async-start | bytes 2359296 | tf_op jit(solution)/shard_map/all_to_all | solution.py:499

commit v4 on v3

--- a/solution.py
+++ b/solution.py
@@ -147,7 +147,7 @@
     return blended[:HEAD] / blended[HEAD : HEAD + 1]
 
 
-def attend(parts, bias, exact):
+def attend(parts, bias, exact, between=()):
     mask_rows = jnp.ones((128, HALF), BF16)
     augmented = [augment(keys, tile) for keys, tile, _, _ in parts]
     units = [(part, h) for part in range(len(parts)) for h in range(HEADS)]
@@ -171,6 +171,8 @@
             out.append(blend(parts[before[0]][2], before[1], powers))
         powers = now
         scores = later
+        for call in between[at * len(between) // len(units) : (at + 1) * len(between) // len(units)]:
+            call()
     out.append(blend(parts[units[-1][0]][2], units[-1][1], powers))
     return [
         jnp.concatenate(out[part * HEADS : (part + 1) * HEADS], axis=0)
@@ -320,51 +322,93 @@
 
 def column_kernel(
     x_ref, gain_ref, wk_ref, wt_ref, wo_ref, gain2_ref, w1_ref, w2_ref, out_ref,
-    x32_ref, o_ref, y_ref,
+    x32_ref, keys_ref, tile_ref, vt_ref, qt_ref, gt_ref, o_ref, total_ref, normed_ref, y_ref,
 ):
     _, q, _ = position()
     x32_ref[...] = x_ref[...].astype(F32).reshape(PEERS, 9, 8, 128)
-
-    def residue(r, carry):
-        x = jnp.concatenate([x32_ref[:, 4 * j + r].reshape(LENGTH, 128) for j in range(2)], axis=1)
-        normed = norm(x, gain_ref[...])
+    absent = (x32_ref[:, 8].reshape(LENGTH, 128) - 1.0).astype(BF16)
+    lane = lax.broadcasted_iota(jnp.int32, (128, 128), 1)
+    row = lax.broadcasted_iota(jnp.int32, (128, 128), 0)
+
+    def residue_rows(r, first, count):
+        halves = [
+            x32_ref[first : first + count, 4 * j + r].reshape(count * 8, 128) for j in range(2)
+        ]
+        return jnp.concatenate(halves, axis=1)
+
+    safe = jnp.bool_(True)
+    for r in range(4):
+        normed = norm(residue_rows(r, 0, PEERS), gain_ref[...])
         keys = nn(normed, wk_ref[...]).astype(BF16)
-        lane = lax.broadcasted_iota(jnp.int32, (128, 128), 1)
-        row = lax.broadcasted_iota(jnp.int32, (128, 128), 0)
+        keys_ref[r] = keys
         pick = jnp.zeros((128, 128), F32)
         for at, value in enumerate(mask_parts()):
             pick = jnp.where((lane == at) & (row == 4 * q + r), value, pick)
-        absent = (x32_ref[:, 8].reshape(LENGTH, 128) - 1.0).astype(BF16)
         tile = nn(absent, pick.astype(BF16))
-        mask_tile = tile.astype(BF16)
-        vt = nt(wt_ref[2 * WIDTH : 3 * WIDTH], normed).astype(BF16)
+        tile_ref[r] = tile.astype(BF16)
+        vt_ref[r] = nt(wt_ref[2 * WIDTH : 3 * WIDTH], normed).astype(BF16)
         qt = nt(wt_ref[:WIDTH], normed).astype(BF16)
-        gt = nt(wt_ref[3 * WIDTH :], normed).astype(BF16)
-        parts = [(keys, mask_tile, vt, qt[:, n * HALF : (n + 1) * HALF]) for n in range(2)]
-        safe = (score_bound(keys, qt) <= COLUMN_BOUND) & any_present(tile)
-
-        @pl.when(safe)
-        def _():
-            for n, o in enumerate(attend(parts, None, False)):
-                o_ref[n] = o
-
-        @pl.when(jnp.logical_not(safe))
-        def _():
-            for n, o in enumerate(attend(parts, None, True)):
-                o_ref[n] = o
-
-        for n in range(2):
+        qt_ref[r] = qt
+        gt_ref[r] = nt(wt_ref[3 * WIDTH :], normed).astype(BF16)
+        safe = safe & (score_bound(keys, qt) <= COLUMN_BOUND) & any_present(tile)
+
+    def attention(r, exact, between=()):
+        parts = [
+            (keys_ref[r], tile_ref[r], vt_ref[r], qt_ref[r, :, n * HALF : (n + 1) * HALF])
+            for n in range(2)
+        ]
+        for n, o in enumerate(attend(parts, None, exact, between)):
             cols = slice(n * HALF, (n + 1) * HALF)
-            gated = (o_ref[n] * jax.nn.sigmoid(gt[:, cols].astype(F32))).astype(BF16)
-            one = x[cols] + tn(gated, wo_ref[...])
-            two = one.astype(BF16).astype(F32)
-            hidden = jnp.maximum(nn(norm(two, gain2_ref[...]), w1_ref[...]), 0.0).astype(BF16)
-            y = two + nn(hidden, w2_ref[...])
-            for j in range(2):
-                y_ref[j, pl.ds(n * 4 * HALF + r, HALF, stride=4), :] = y[:, j * 128 : (j + 1) * 128]
-        return carry
-
-    lax.fori_loop(0, 4, residue, 0)
+            gate = jax.nn.sigmoid(gt_ref[r, :, cols].astype(F32))
+            o_ref[r, :, cols] = (o * gate).astype(BF16)
+
+    def project_out(r):
+        one = residue_rows(r, 0, PEERS) + tn(o_ref[r], wo_ref[...])
+        total_ref[...] = one.astype(BF16).astype(F32)
+
+    def normalize():
+        normed_ref[...] = norm(total_ref[...], gain2_ref[...])
+
+    def transition(part):
+        cols = slice(part * 256, (part + 1) * 256)
+        hidden = jnp.maximum(nn(normed_ref[...], w1_ref[:, cols]), 0.0).astype(BF16)
+        total_ref[...] += nn(hidden, w2_ref[cols])
+
+    def keep(r):
+        for j in range(2):
+            y_ref[j, pl.ds(r, LENGTH, stride=4), :] = total_ref[:, j * 128 : (j + 1) * 128]
+
+    def finishing(r):
+        blocks = [functools.partial(transition, part) for part in range(4)]
+        return [functools.partial(project_out, r), normalize] + blocks + [functools.partial(keep, r)]
+
+    @pl.when(safe)
+    def _():
+        attention(0, False)
+
+        def residue(r, carry):
+            attention(r, False, finishing(r - 1))
+            return carry
+
+        lax.fori_loop(1, 4, residue, 0)
+
+    @pl.when(jnp.logical_not(safe))
+    def _():
+        def residue(r, carry):
+            attention(r, True)
+            return carry
+
+        lax.fori_loop(0, 4, residue, 0)
+
+        def rest(r, carry):
+            for call in finishing(r):
+                call()
+            return carry
+
+        lax.fori_loop(0, 3, rest, 0)
+
+    for call in finishing(3):
+        call()
     for j in range(2):
         out_ref[:, j * 128 : (j + 1) * 128] = y_ref[j].astype(BF16)
 
@@ -506,7 +550,14 @@
         out_specs=whole(4 * LENGTH, WIDTH),
         scratch_shapes=[
             pltpu.VMEM((PEERS, 9, 8, 128), F32),
-            pltpu.VMEM((2, WIDTH, HALF), F32),
+            pltpu.VMEM((4, LENGTH, WIDTH), BF16),
+            pltpu.VMEM((4, LENGTH, 128), BF16),
+            pltpu.VMEM((4, WIDTH, LENGTH), BF16),
+            pltpu.VMEM((4, WIDTH, LENGTH), BF16),
+            pltpu.VMEM((4, WIDTH, LENGTH), BF16),
+            pltpu.VMEM((4, WIDTH, LENGTH), BF16),
+            pltpu.VMEM((LENGTH, WIDTH), F32),
+            pltpu.VMEM((LENGTH, WIDTH), BF16),
             pltpu.VMEM((2, 4 * LENGTH, 128), F32),
         ],
         compiler_params=params,

time: 162 us -> 160 us (0.988)
  Pallas kernels: 84.8 us -> 82.8 us
    pallas_call x1, Pallas kernels: 20.9 us -> 19 us  [body(): pl.pallas_call(column_kernel, out_shape=jax.ShapeDtypeStruct((4 * LENGTH,...]
where the time goes in v4:
time: 160 us
  Pallas kernels  82.8 us (52%)
  blocking collectives  26.1 us (16%)
  waiting for transfers between devices  24.5 us (15%)
  starting transfers between devices  20 us (12%)
  local copies, waits for them, and re-layouts  5.85 us (4%)
    pallas_call x1, Pallas kernels, body(): pl.pallas_call(row_kernel, out_shape=jax.ShapeDtypeStruct((PEERS, 72, 128...  44.4 us
    all_to_all x1, blocking collectives, body(): lax.all_to_all(finished.reshape(128, 16, WIDTH), AXES, 0, 0, tiled=True)  26.1 us
    pallas_call x1, Pallas kernels, body(): pl.pallas_call(column_kernel, out_shape=jax.ShapeDtypeStruct((4 * LENGTH,...  19 us
    all_to_all x1, waiting for transfers between devices, body(): columns = lax.all_to_all(after_rows, PLANE, 0, 0, tiled=True)  16.9 us
    pallas_call x1, Pallas kernels, body(): pl.pallas_call(project_kernel, grid=(8,), out_shape=[jax.ShapeDtypeStruct...  15.9 us
    all_to_all x1, starting transfers between devices, body(): tiles = lax.all_to_all(payload, PLANE, 0, 0, tiled=True)  12.1 us
    all_to_all x1, waiting for transfers between devices, body(): tiles = lax.all_to_all(payload, PLANE, 0, 0, tiled=True)  7.26 us
    all_to_all x1, starting transfers between devices, body(): columns = lax.all_to_all(after_rows, PLANE, 0, 0, tiled=True)  6.8 us
  transfers between devices with their start and end apart: 4, of which 3 were waited for; matrix products, arithmetic and copies ran while one was open for 2% of the time, Pallas kernels for 10%

profile of v4, /device:TPU:1, one launch (start us, length us, event | category | flops | bytes accessed | tf_op | source)
XLA Modules:
  0.0 159.5 jit_solution(9949370208802571016)
XLA Ops:
  0.0 3.6 %shard_map.155 = bf16[64,64,256]{2,1,0:T(8,128)(2,1)} custom-call(bf16[2048,128]{1,0:T(8,128)(2,1)} %bitcast.20, f32[1,128]{1,0:T(1,128)} %bitcast.23, bf16[8,128]{1,0:T(8,128)(2,1)} %weight_ref.1, s32[1,512]{1,0:T(1,128)} %bitcast.22, f32[1,8]{1,0:T(1,128)} %bitcast.24), custom_call_target="tpu_custom_call" | custom-call | tf_op jit(solution)/shard_map/pallas_call | solution.py:449
  3.6 12.1 %all-to-all-start = ((bf16[64,64,256]{2,1,0:T(8,128)(2,1)}), bf16[64,64,256]{2,1,0:T(8,128)(2,1)S(1)}, u32[]{:S(2)}, u32[]{:S(2)}) async-start(bf16[64,64,256]{2,1,0:T(8,128)(2,1)} %shard_map.155), calls=%async_computation | async-start | bytes 4194304 | tf_op jit(solution)/shard_map/all_to_all | solution.py:463
  15.7 1.0 collective-permute-start
  16.7 0.1 collective-permute-start.1
  16.8 1.0 copy.17
  17.8 0.7 slice.6.wk_ref
  18.5 0.4 collective-permute-done.1.other_mask_ref
  18.9 0.8 copy.18.mask_ref
  19.7 15.9 %shard_map.154 = (bf16[8,512,384]{2,1,0:T(8,128)(2,1)}, bf16[8,256,512]{2,1,0:T(8,128)(2,1)}, bf16[8,256,256]{2,1,0:T(8,128)(2,1)}, bf16[8,256,256]{2,1,0:T(8,12...) custom-call(bf16[4,512,256]{2,1,0:T(8,128)(2,1)} %own_ref.1, ...), custom_call_target="tpu_custom_call" | custom-call | flops 6442450944 | bytes 26214400 | tf_op jit(solution)/shard_map/pallas_call | solution.py:468
  35.6 7.3 %all-to-all-done.tile_ref = bf16[64,64,256]{2,1,0:T(8,128)(2,1)S(1)} async-done(((bf16[64,64,256]{2,1,0:T(8,128)(2,1)}), bf16[64,64,256]{2,1,0:T(8,128)(2,1)S(1)}, u32[]{:S(2)}, u32[]{:S(2)}) %all-to-all-start) | async-done | bytes 2097184 | tf_op jit(solution)/shard_map/all_to_all | solution.py:463
  42.9 1.4 copy-done.5
  44.2 44.4 %shard_map.156 = bf16[64,72,128]{2,1,0:T(8,128)(2,1)} custom-call(f32[8,8,128]{2,1,0:T(8,128)} %get-tuple-element.13.safe_ref, bf16[256,256]{1,0:T(8,128)(2,1)} %wo_ref.2, bf16[8,256]{1,0:T(8,128)(2,1)} %get-tuple-element.14.mask_ref, bf16[64,64,256]{2,1,0:T(8,128)(2,1)} %copy-done.5, bf16[8,8,512,256]{3,2,1,0:T(8,128)(2,1)} %get-tuple-element.15.powers_ref, ...), custom_call_target="tpu_custom_call" | custom-call | flops 4294967296 | bytes 20971520 | tf_op jit(solution)/shard_map/pallas_call | solution.py:516
  88.6 0.0 copy-start.7
  88.6 0.0 copy-start
  88.7 0.0 copy-start.1
  88.7 0.0 copy-start.2
  88.7 6.8 %all-to-all-start.1 = ((bf16[64,72,128]{2,1,0:T(8,128)(2,1)}), bf16[64,72,128]{2,1,0:T(8,128)(2,1)S(1)}, u32[]{:S(2)}, u32[]{:S(2)}) async-start(bf16[64,72,128]{2,1,0:T(8,128)(2,1)} %shard_map.156), calls=%async_computation.1 | async-start | bytes 2359296 | tf_op jit(solution)/shard_map/all_to_all | solution.py:543
  95.5 0.2 copy.19
  95.8 16.9 %all-to-all-done.1.x_ref = bf16[64,72,128]{2,1,0:T(8,128)(2,1)S(1)} async-done(((bf16[64,72,128]{2,1,0:T(8,128)(2,1)}), bf16[64,72,128]{2,1,0:T(8,128)(2,1)S(1)}, u32[]{:S(2)}, u32[]{:S(2)}) %all-to-all-start.1) | async-done | bytes 1179680 | tf_op jit(solution)/shard_map/all_to_all | solution.py:543
  112.7 19.0 %shard_map.157 = bf16[2048,256]{1,0:T(8,128)(2,1)S(1)} custom-call(bf16[64,72,128]{2,1,0:T(8,128)(2,1)S(1)} %all-to-all-done.1.x_ref, f32[1,256]{1,0:T(1,128)S(1)} %bitcast.17, bf16[256,256]{1,0:T(8,128)(2,1)S(1)} %slice.7.wk_ref, bf16[1024,256]{1,0:T(8,128)(2,1)S(1)} %bitcast.16, bf16[256,256]{1,0:T(8,128)(2,1)S(1)} %copy-done.2, f32[1,256]{1,0:T(1,128)S(1)} %bitcast.18, ...), custom_call_target="tpu_custom_call" | custom-call | flops 8589934592 | bytes 4194304 | tf_op jit(solution)/shard_map/pallas_call | solution.py:545
  131.7 26.1 %all_to_all.15 = bf16[128,16,256]{2,1,0:T(8,128)(2,1)S(1)} all-to-all(bf16[128,16,256]{2,1,0:T(8,128)(2,1)S(1)} %bitcast.15), channel_id=1, replica_groups=mesh['grp'=2,'z'=4,'x'=4,'yh'=2,'core'=2] {'grp','z','x','yh','core'}, dimensions={0} | all-to-all | bytes 2097152 | tf_op jit(solution)/shard_map/all_to_all | solution.py:578
  157.8 0.3 reshape.38
  158.0 0.4 copy.22
  158.4 1.1 reshape.39
  (20 shorter events, 0.1 us)
Async XLA Ops:
  3.6 13.1 %copy-start.8 = (s32[4,512]{1,0:T(4,128)S(1)}, s32[4,512]{1,0:T(4,128)}, u32[]{:S(2)}) copy-start(s32[4,512]{1,0:T(4,128)} %own_mask_ref.1) | copy-start | bytes 24580
  3.6 13.3 %copy-start.6 = (bf16[256,1024]{1,0:T(8,128)(2,1)S(1)}, bf16[256,1024]{1,0:T(8,128)(2,1)}, u32[]{:S(2)}) copy-start(bf16[256,1024]{1,0:T(8,128)(2,1)} %param.24) | copy-start | bytes 1572868
  3.6 39.3 %all-to-all-start = ((bf16[64,64,256]{2,1,0:T(8,128)(2,1)}), bf16[64,64,256]{2,1,0:T(8,128)(2,1)S(1)}, u32[]{:S(2)}, u32[]{:S(2)}) async-start(bf16[64,64,256]{2,1,0:T(8,128)(2,1)} %shard_map.155), calls=%async_computation | async-start | bytes 4194304 | tf_op jit(solution)/shard_map/all_to_all | solution.py:463
  15.7 4.0 %collective-permute-start = (bf16[4,512,256]{2,1,0:T(8,128)(2,1)}, bf16[4,512,256]{2,1,0:T(8,128)(2,1)}, u32[]{:S(2)}, u32[]{:S(2)}) collective-permute-start(bf16[4,512,256]{2,1,0:T(8,128)(2,1)} %own_ref.1), channel_id=1, source_target_pairs={{0,1},{1,0},{2,3},{3,2},{4,5},{5,4},{6,7},{7,6},{8,9},{9,8},{10,11... | collective-permute-start | bytes 3145736 | tf_op jit(solution)/shard_map/ppermute | solution.py:447
  16.7 2.2 %collective-permute-start.1 = (s32[4,512]{1,0:T(4,128)S(1)}, s32[4,512]{1,0:T(4,128)S(1)}, u32[]{:S(2)}, u32[]{:S(2)}) collective-permute-start(s32[4,512]{1,0:T(4,128)S(1)} %copy-done.8), channel_id=1, source_target_pairs={{0,1},{1,0},{2,3},{3,2},{4,5},{5,4},{6,7},{7,6},{8,9},{9,8},{10,11... | collective-permute-start | bytes 24584 | tf_op jit(solution)/shard_map/ppermute | solution.py:446
  18.9 0.8 copy-start.9
  42.9 1.4 copy-start.5
  88.6 6.9 %copy-start.7 = (bf16[256,1024]{1,0:T(8,128)(2,1)S(1)}, bf16[256,1024]{1,0:T(8,128)(2,1)}, u32[]{:S(2)}) copy-start(bf16[256,1024]{1,0:T(8,128)(2,1)} %param.27) | copy-start | bytes 1572868
  88.6 24.0 %copy-start = (bf16[256,1024]{1,0:T(8,128)(2,1)S(1)}, bf16[256,1024]{1,0:T(8,128)(2,1)}, u32[]{:S(2)}) copy-start(bf16[256,1024]{1,0:T(8,128)(2,1)} %w1_ref.1) | copy-start | bytes 1572868
  88.7 24.0 %copy-start.1 = (bf16[1024,256]{1,0:T(8,128)(2,1)S(1)}, bf16[1024,256]{1,0:T(8,128)(2,1)}, u32[]{:S(2)}) copy-start(bf16[1024,256]{1,0:T(8,128)(2,1)} %w2_ref.1) | copy-start | bytes 1572868
  88.7 24.0 %copy-start.2 = (bf16[256,256]{1,0:T(8,128)(2,1)S(1)}, bf16[256,256]{1,0:T(8,128)(2,1)}, u32[]{:S(2)}) copy-start(bf16[256,256]{1,0:T(8,128)(2,1)} %wo_ref.3) | copy-start | bytes 393220
  88.7 24.0 %copy-start.3 = (f32[256]{0:T(256)S(1)}, f32[256]{0:T(256)}, u32[]{:S(2)}) copy-start(f32[256]{0:T(256)} %param.26) | copy-start | bytes 3076
  88.7 24.0 %copy-start.4 = (f32[256]{0:T(256)S(1)}, f32[256]{0:T(256)}, u32[]{:S(2)}) copy-start(f32[256]{0:T(256)} %param.29) | copy-start | bytes 3076
  88.7 24.0 %all-to-all-start.1 = ((bf16[64,72,128]{2,1,0:T(8,128)(2,1)}), bf16[64,72,128]{2,1,0:T(8,128)(2,1)S(1)}, u32[]{:S(2)}, u32[]{:S(2)}) async-start(bf16[64,72,128]{2,1,0:T(8,128)(2,1)} %shard_map.156), calls=%async_computation.1 | async-start | bytes 2359296 | tf_op jit(solution)/shard_map/all_to_all | solution.py:543

commit v5 on v4

--- a/solution.py
+++ b/solution.py
@@ -147,7 +147,7 @@
     return blended[:HEAD] / blended[HEAD : HEAD + 1]
 
 
-def attend(parts, bias, exact, between=()):
+def attend(parts, between=()):
     mask_rows = jnp.ones((128, HALF), BF16)
     augmented = [augment(keys, tile) for keys, tile, _, _ in parts]
     units = [(part, h) for part in range(len(parts)) for h in range(HEADS)]
@@ -160,12 +160,7 @@
     powers = None
     for at, (part, h) in enumerate(units):
         later = score(*units[at + 1]) if at + 1 < len(units) else None
-        scaled = scores * SCALE
-        if bias is not None:
-            scaled = scaled + bias[h]
-        if exact:
-            scaled = scaled - jnp.max(scaled, axis=0, keepdims=True)
-        now = jnp.exp2(scaled).astype(BF16)
+        now = jnp.exp2(scores * SCALE).astype(BF16)
         if at:
             before = units[at - 1]
             out.append(blend(parts[before[0]][2], before[1], powers))
@@ -178,6 +173,24 @@
         jnp.concatenate(out[part * HEADS : (part + 1) * HEADS], axis=0)
         for part in range(len(parts))
     ]
+
+
+def attend_exact(keys, tile, vt, qt, bias_ref):
+    key_term = jnp.where(tile[:, :1].astype(F32) < 0.0, -1e9, 0.0)
+    feat = lax.broadcasted_iota(jnp.int32, (WIDTH, HALF), 0)
+
+    def head(h, total):
+        mine = (feat >= h * HEAD) & (feat < (h + 1) * HEAD)
+        queries = jnp.where(mine, qt.astype(F32), 0.0).astype(BF16)
+        scores = nn(keys, queries) * HEAD**-0.5
+        if bias_ref is not None:
+            scores = scores + bias_ref[h]
+        scores = scores + key_term
+        powers = jnp.exp(scores - jnp.max(scores, axis=0, keepdims=True))
+        weights = (powers / jnp.sum(powers, axis=0, keepdims=True)).astype(BF16)
+        return jnp.where(mine, nn(vt, weights), total)
+
+    return lax.fori_loop(0, HEADS, head, jnp.zeros((WIDTH, HALF), F32))
 
 
 def project_kernel(
@@ -242,7 +255,7 @@
             block = block.astype(F32).reshape(32, 2, 8, 256)
             for k in range(2):
                 rows = block[:, k].reshape(HALF, 256).astype(BF16)
-                yield pair * 2 + k, g, nt(eye, rows) * LOG2E
+                yield pair * 2 + k, g, nt(eye, rows)
 
 
 def row_kernel(
@@ -266,6 +279,7 @@
 
     largest = jnp.zeros((8, HALF), F32)
     for h, g, block in bias_blocks(tile_ref):
+        block = block * LOG2E
         factor_ref[h, g * 256 : (g + 1) * 256, :] = jnp.exp2(block).astype(BF16)
         size = jnp.abs(block).reshape(32, 8, HALF)
         largest = jnp.maximum(largest, jnp.max(size, axis=0))
@@ -293,8 +307,9 @@
             pltpu.sync_copy(qt_ref.at[step], qt_here)
             for h, g, block in bias_blocks(tile_ref):
                 bias_ref[h, g * 256 : (g + 1) * 256, :] = block
-            part = (k_here[:, :WIDTH], k_here[:, WIDTH:], vt_here[slot], qt_here[...])
-            o_ref[...] = attend([part], bias_ref, True)[0]
+            o_ref[...] = attend_exact(
+                k_here[:, :WIDTH], k_here[:, WIDTH:], vt_here[slot], qt_here[...], bias_ref
+            )
 
         gated = (o_ref[...] * jax.nn.sigmoid(gt_here[slot].astype(F32))).astype(BF16)
         y = xq_here[slot].astype(F32) + tn(gated, wo_ref[...])
@@ -352,15 +367,17 @@
         gt_ref[r] = nt(wt_ref[3 * WIDTH :], normed).astype(BF16)
         safe = safe & (score_bound(keys, qt) <= COLUMN_BOUND) & any_present(tile)
 
-    def attention(r, exact, between=()):
+    def attention(r, between=()):
         parts = [
             (keys_ref[r], tile_ref[r], vt_ref[r], qt_ref[r, :, n * HALF : (n + 1) * HALF])
             for n in range(2)
         ]
-        for n, o in enumerate(attend(parts, None, exact, between)):
-            cols = slice(n * HALF, (n + 1) * HALF)
-            gate = jax.nn.sigmoid(gt_ref[r, :, cols].astype(F32))
-            o_ref[r, :, cols] = (o * gate).astype(BF16)
+        for n, o in enumerate(attend(parts, between)):
+            gate(r, n, o)
+
+    def gate(r, n, o):
+        cols = slice(n * HALF, (n + 1) * HALF)
+        o_ref[r, :, cols] = (o * jax.nn.sigmoid(gt_ref[r, :, cols].astype(F32))).astype(BF16)
 
     def project_out(r):
         one = residue_rows(r, 0, PEERS) + tn(o_ref[r], wo_ref[...])
@@ -384,10 +401,10 @@
 
     @pl.when(safe)
     def _():
-        attention(0, False)
+        attention(0)
 
         def residue(r, carry):
-            attention(r, False, finishing(r - 1))
+            attention(r, finishing(r - 1))
             return carry
 
         lax.fori_loop(1, 4, residue, 0)
@@ -395,7 +412,9 @@
     @pl.when(jnp.logical_not(safe))
     def _():
         def residue(r, carry):
-            attention(r, True)
+            for n in range(2):
+                queries = qt_ref[r, :, n * HALF : (n + 1) * HALF]
+                gate(r, n, attend_exact(keys_ref[r], tile_ref[r], vt_ref[r], queries, None))
             return carry
 
         lax.fori_loop(0, 4, residue, 0)

time: 160 us -> 231 us (1.44)
  Pallas kernels: 82.8 us -> 153 us
    pallas_call x1, Pallas kernels: 19 us -> 54.6 us  [body(): pl.pallas_call(column_kernel, out_shape=jax.ShapeDtypeStruct((4 * LENGTH,...]
    pallas_call x1, Pallas kernels: 44.4 us -> 78.9 us  [body(): pl.pallas_call(row_kernel, out_shape=jax.ShapeDtypeStruct((PEERS, 72, 128...]
  transfers between devices with their start and end apart: 4 -> 4, of which waited for: 3 -> 3; matrix products, arithmetic and copies ran while one was open for 2% -> 1% of each run, Pallas kernels for 10% -> 7%
where the time goes in v5:
time: 231 us; the launch traced here: 230 us
  Pallas kernels  153 us (66%)
  blocking collectives  26.1 us (11%)
  waiting for transfers between devices  24.5 us (11%)
  starting transfers between devices  20 us (9%)
  local copies, waits for them, and re-layouts  5.85 us (3%)
    pallas_call x1, Pallas kernels, body(): pl.pallas_call(row_kernel, out_shape=jax.ShapeDtypeStruct((PEERS, 72, 128...  78.9 us
    pallas_call x1, Pallas kernels, body(): pl.pallas_call(column_kernel, out_shape=jax.ShapeDtypeStruct((4 * LENGTH,...  54.6 us
    all_to_all x1, blocking collectives, body(): lax.all_to_all(finished.reshape(128, 16, WIDTH), AXES, 0, 0, tiled=True)  26.1 us
    all_to_all x1, waiting for transfers between devices, body(): columns = lax.all_to_all(after_rows, PLANE, 0, 0, tiled=True)  16.9 us
    pallas_call x1, Pallas kernels, body(): pl.pallas_call(project_kernel, grid=(8,), out_shape=[jax.ShapeDtypeStruct...  15.9 us
    all_to_all x1, starting transfers between devices, body(): tiles = lax.all_to_all(payload, PLANE, 0, 0, tiled=True)  12.1 us
    all_to_all x1, waiting for transfers between devices, body(): tiles = lax.all_to_all(payload, PLANE, 0, 0, tiled=True)  7.26 us
    all_to_all x1, starting transfers between devices, body(): columns = lax.all_to_all(after_rows, PLANE, 0, 0, tiled=True)  6.81 us
  transfers between devices with their start and end apart: 4, of which 3 were waited for; matrix products, arithmetic and copies ran while one was open for 1% of the time, Pallas kernels for 7%

profile of v5, /device:TPU:1, one launch (start us, length us, event | category | flops | bytes accessed | tf_op | source)
XLA Modules:
  0.0 229.7 jit_solution(1682103671651455639)
XLA Ops:
  0.0 3.6 %shard_map.155 = bf16[64,64,256]{2,1,0:T(8,128)(2,1)} custom-call(bf16[2048,128]{1,0:T(8,128)(2,1)} %bitcast.20, f32[1,128]{1,0:T(1,128)} %bitcast.23, bf16[8,128]{1,0:T(8,128)(2,1)} %weight_ref.1, s32[1,512]{1,0:T(1,128)} %bitcast.22, f32[1,8]{1,0:T(1,128)} %bitcast.24), custom_call_target="tpu_custom_call" | custom-call | tf_op jit(solution)/shard_map/pallas_call | solution.py:468
  3.6 12.1 %all-to-all-start = ((bf16[64,64,256]{2,1,0:T(8,128)(2,1)}), bf16[64,64,256]{2,1,0:T(8,128)(2,1)S(1)}, u32[]{:S(2)}, u32[]{:S(2)}) async-start(bf16[64,64,256]{2,1,0:T(8,128)(2,1)} %shard_map.155), calls=%async_computation | async-start | bytes 4194304 | tf_op jit(solution)/shard_map/all_to_all | solution.py:482
  15.7 1.0 collective-permute-start
  16.7 0.1 collective-permute-start.1
  16.8 1.0 copy.17
  17.8 0.7 slice.6.wk_ref
  18.5 0.4 collective-permute-done.1.other_mask_ref
  18.9 0.8 copy.18.mask_ref
  19.7 15.9 %shard_map.154 = (bf16[8,512,384]{2,1,0:T(8,128)(2,1)}, bf16[8,256,512]{2,1,0:T(8,128)(2,1)}, bf16[8,256,256]{2,1,0:T(8,128)(2,1)}, bf16[8,256,256]{2,1,0:T(8,12...) custom-call(bf16[4,512,256]{2,1,0:T(8,128)(2,1)} %own_ref.1, ...), custom_call_target="tpu_custom_call" | custom-call | flops 6442450944 | bytes 26214400 | tf_op jit(solution)/shard_map/pallas_call | solution.py:487
  35.6 7.3 %all-to-all-done.tile_ref = bf16[64,64,256]{2,1,0:T(8,128)(2,1)S(1)} async-done(((bf16[64,64,256]{2,1,0:T(8,128)(2,1)}), bf16[64,64,256]{2,1,0:T(8,128)(2,1)S(1)}, u32[]{:S(2)}, u32[]{:S(2)}) %all-to-all-start) | async-done | bytes 2097184 | tf_op jit(solution)/shard_map/all_to_all | solution.py:482
  42.9 1.4 copy-done.5
  44.2 78.9 %shard_map.156 = bf16[64,72,128]{2,1,0:T(8,128)(2,1)} custom-call(f32[8,8,128]{2,1,0:T(8,128)} %get-tuple-element.13.safe_ref, bf16[256,256]{1,0:T(8,128)(2,1)} %wo_ref.2, bf16[8,256]{1,0:T(8,128)(2,1)} %get-tuple-element.14.mask_ref, bf16[64,64,256]{2,1,0:T(8,128)(2,1)} %copy-done.5, bf16[8,8,512,256]{3,2,1,0:T(8,128)(2,1)} %get-tuple-element.15.powers_ref, ...), custom_call_target="tpu_custom_call" | custom-call | flops 4294967296 | bytes 20971520 | tf_op jit(solution)/shard_map/pallas_call | solution.py:535
  123.2 0.0 copy-start.7
  123.2 0.0 copy-start
  123.2 0.0 copy-start.2
  123.2 0.0 copy-start.3
  123.2 6.8 %all-to-all-start.1 = ((bf16[64,72,128]{2,1,0:T(8,128)(2,1)}), bf16[64,72,128]{2,1,0:T(8,128)(2,1)S(1)}, u32[]{:S(2)}, u32[]{:S(2)}) async-start(bf16[64,72,128]{2,1,0:T(8,128)(2,1)} %shard_map.156), calls=%async_computation.1 | async-start | bytes 2359296 | tf_op jit(solution)/shard_map/all_to_all | solution.py:562
  130.0 0.2 copy.19
  130.3 16.9 %all-to-all-done.1.x_ref = bf16[64,72,128]{2,1,0:T(8,128)(2,1)S(1)} async-done(((bf16[64,72,128]{2,1,0:T(8,128)(2,1)}), bf16[64,72,128]{2,1,0:T(8,128)(2,1)S(1)}, u32[]{:S(2)}, u32[]{:S(2)}) %all-to-all-start.1) | async-done | bytes 1179680 | tf_op jit(solution)/shard_map/all_to_all | solution.py:562
  147.2 54.6 %shard_map.157 = bf16[2048,256]{1,0:T(8,128)(2,1)S(1)} custom-call(bf16[64,72,128]{2,1,0:T(8,128)(2,1)S(1)} %all-to-all-done.1.x_ref, f32[1,256]{1,0:T(1,128)S(1)} %bitcast.17, bf16[256,256]{1,0:T(8,128)(2,1)S(1)} %slice.7.wk_ref, bf16[1024,256]{1,0:T(8,128)(2,1)S(1)} %bitcast.16, bf16[256,256]{1,0:T(8,128)(2,1)S(1)} %copy-done.2, f32[1,256]{1,0:T(1,128)S(1)} %bitcast.18, ...), custom_call_target="tpu_custom_call" | custom-call | flops 8589934592 | bytes 4194304 | tf_op jit(solution)/shard_map/pallas_call | solution.py:564
  201.8 26.1 %all_to_all.15 = bf16[128,16,256]{2,1,0:T(8,128)(2,1)S(1)} all-to-all(bf16[128,16,256]{2,1,0:T(8,128)(2,1)S(1)} %bitcast.15), channel_id=1, replica_groups=mesh['grp'=2,'z'=4,'x'=4,'yh'=2,'core'=2] {'grp','z','x','yh','core'}, dimensions={0} | all-to-all | bytes 2097152 | tf_op jit(solution)/shard_map/all_to_all | solution.py:597
  227.9 0.3 reshape.38
  228.2 0.4 copy.22
  228.6 1.1 reshape.39
  (20 shorter events, 0.1 us)
Async XLA Ops:
  3.6 13.1 %copy-start.8 = (s32[4,512]{1,0:T(4,128)S(1)}, s32[4,512]{1,0:T(4,128)}, u32[]{:S(2)}) copy-start(s32[4,512]{1,0:T(4,128)} %own_mask_ref.1) | copy-start | bytes 24580
  3.6 13.3 %copy-start.6 = (bf16[256,1024]{1,0:T(8,128)(2,1)S(1)}, bf16[256,1024]{1,0:T(8,128)(2,1)}, u32[]{:S(2)}) copy-start(bf16[256,1024]{1,0:T(8,128)(2,1)} %param.24) | copy-start | bytes 1572868
  3.6 39.3 %all-to-all-start = ((bf16[64,64,256]{2,1,0:T(8,128)(2,1)}), bf16[64,64,256]{2,1,0:T(8,128)(2,1)S(1)}, u32[]{:S(2)}, u32[]{:S(2)}) async-start(bf16[64,64,256]{2,1,0:T(8,128)(2,1)} %shard_map.155), calls=%async_computation | async-start | bytes 4194304 | tf_op jit(solution)/shard_map/all_to_all | solution.py:482
  15.7 4.0 %collective-permute-start = (bf16[4,512,256]{2,1,0:T(8,128)(2,1)}, bf16[4,512,256]{2,1,0:T(8,128)(2,1)}, u32[]{:S(2)}, u32[]{:S(2)}) collective-permute-start(bf16[4,512,256]{2,1,0:T(8,128)(2,1)} %own_ref.1), channel_id=1, source_target_pairs={{0,1},{1,0},{2,3},{3,2},{4,5},{5,4},{6,7},{7,6},{8,9},{9,8},{10,11... | collective-permute-start | bytes 3145736 | tf_op jit(solution)/shard_map/ppermute | solution.py:466
  16.7 2.2 collective-permute-start.1
  18.9 0.8 copy-start.9
  42.9 1.4 copy-start.5
  123.2 6.9 %copy-start.7 = (bf16[256,1024]{1,0:T(8,128)(2,1)S(1)}, bf16[256,1024]{1,0:T(8,128)(2,1)}, u32[]{:S(2)}) copy-start(bf16[256,1024]{1,0:T(8,128)(2,1)} %param.27) | copy-start | bytes 1572868
  123.2 24.0 %copy-start = (bf16[256,1024]{1,0:T(8,128)(2,1)S(1)}, bf16[256,1024]{1,0:T(8,128)(2,1)}, u32[]{:S(2)}) copy-start(bf16[256,1024]{1,0:T(8,128)(2,1)} %w1_ref.1) | copy-start | bytes 1572868
  123.2 24.0 %copy-start.1 = (bf16[1024,256]{1,0:T(8,128)(2,1)S(1)}, bf16[1024,256]{1,0:T(8,128)(2,1)}, u32[]{:S(2)}) copy-start(bf16[1024,256]{1,0:T(8,128)(2,1)} %w2_ref.1) | copy-start | bytes 1572868
  123.2 24.0 %copy-start.2 = (bf16[256,256]{1,0:T(8,128)(2,1)S(1)}, bf16[256,256]{1,0:T(8,128)(2,1)}, u32[]{:S(2)}) copy-start(bf16[256,256]{1,0:T(8,128)(2,1)} %wo_ref.3) | copy-start | bytes 393220
  123.2 24.0 %copy-start.3 = (f32[256]{0:T(256)S(1)}, f32[256]{0:T(256)}, u32[]{:S(2)}) copy-start(f32[256]{0:T(256)} %param.26) | copy-start | bytes 3076
  123.2 24.0 %copy-start.4 = (f32[256]{0:T(256)S(1)}, f32[256]{0:T(256)}, u32[]{:S(2)}) copy-start(f32[256]{0:T(256)} %param.29) | copy-start | bytes 3076
  123.2 24.0 %all-to-all-start.1 = ((bf16[64,72,128]{2,1,0:T(8,128)(2,1)}), bf16[64,72,128]{2,1,0:T(8,128)(2,1)S(1)}, u32[]{:S(2)}, u32[]{:S(2)}) async-start(bf16[64,72,128]{2,1,0:T(8,128)(2,1)} %shard_map.156), calls=%async_computation.1 | async-start | bytes 2359296 | tf_op jit(solution)/shard_map/all_to_all | solution.py:562

commit v6 on v5

--- a/solution.py
+++ b/solution.py
@@ -25,8 +25,7 @@
 PLANE = ("grp", "z", "x", "yh")
 VMEM_LIMIT = 40 * 1024 * 1024
 SLOTS = 3
-VMEM_WHOLE = 60 * 2**20
-VMEM_TILE = 58 * 2**20
+VMEM_WHOLE = 62 * 2**20
 ROW_BOUND = 40.0
 COLUMN_BOUND = 60.0
 
@@ -67,7 +66,9 @@
     return lax.axis_index("grp"), q, lax.axis_index("core")
 
 
-def bias_kernel(pair_ref, gain_ref, weight_ref, chain_ref, inter_ref, out_ref):
+def bias_kernel(
+    pair_ref, gain_ref, weight_ref, chain_ref, inter_ref, out_ref, copies_ref, copy_sem
+):
     grp, q, core = position()
     normed = norm(pair_ref[...].astype(F32), gain_ref[...])
     bias = nt(weight_ref[...], normed)
@@ -86,11 +87,16 @@
     stacked = jnp.stack(parts, axis=0)
     tile = jnp.swapaxes(stacked, 0, 1).reshape(64, 256).astype(BF16)
 
-    def put(p, carry):
-        out_ref[p] = tile
-        return carry
-
-    lax.fori_loop(0, PEERS, put, 0)
+    for n in range(8):
+        copies_ref[n] = tile
+    sends = [
+        pltpu.make_async_copy(copies_ref, out_ref.at[pl.ds(8 * n, 8)], copy_sem.at[n])
+        for n in range(8)
+    ]
+    for send in sends:
+        send.start()
+    for send in sends:
+        send.wait()
 
 
 def spread(qt, h, mask_rows):
@@ -470,7 +476,8 @@
         grid=(1,),
         out_shape=jax.ShapeDtypeStruct((PEERS, 64, 256), BF16),
         in_specs=[whole(2048, 128), whole(1, 128), whole(8, 128), whole(1, LENGTH), whole(1, 8)],
-        out_specs=whole(PEERS, 64, 256),
+        out_specs=away,
+        scratch_shapes=[pltpu.VMEM((8, 64, 256), BF16), pltpu.SemaphoreType.DMA((8,))],
         compiler_params=pltpu.CompilerParams(vmem_limit_bytes=VMEM_WHOLE),
     )(
         pair_state.reshape(2048, 128),
@@ -553,7 +560,7 @@
             pltpu.SemaphoreType.DMA((SLOTS, 4)),
             pltpu.SemaphoreType.DMA,
         ],
-        compiler_params=pltpu.CompilerParams(vmem_limit_bytes=VMEM_TILE),
+        compiler_params=pltpu.CompilerParams(vmem_limit_bytes=VMEM_WHOLE),
         cost_estimate=pl.CostEstimate(
             flops=8 * 8 * 512 * 256 * 512, bytes_accessed=20 * 2**20, transcendentals=0
         ),

time: 231 us -> 229 us (level)
  no operation moved by 1% of the time
where the time goes in v6:
time: 229 us; the launch traced here: 228 us
  Pallas kernels  153 us (67%)
  blocking collectives  26.1 us (11%)
  waiting for transfers between devices  24.3 us (11%)
  starting transfers between devices  20.3 us (9%)
  local copies, waits for them, and re-layouts  4.58 us (2%)
    pallas_call x1, Pallas kernels, body(): pl.pallas_call(row_kernel, out_shape=jax.ShapeDtypeStruct((PEERS, 72, 128...  78.9 us
    pallas_call x1, Pallas kernels, body(): pl.pallas_call(column_kernel, out_shape=jax.ShapeDtypeStruct((4 * LENGTH,...  54.6 us
    all_to_all x1, blocking collectives, body(): lax.all_to_all(finished.reshape(128, 16, WIDTH), AXES, 0, 0, tiled=True)  26.1 us
    all_to_all x1, waiting for transfers between devices, body(): columns = lax.all_to_all(after_rows, PLANE, 0, 0, tiled=True)  16.9 us
    pallas_call x1, Pallas kernels, body(): pl.pallas_call(project_kernel, grid=(8,), out_shape=[jax.ShapeDtypeStruct...  15.9 us
    all_to_all x1, starting transfers between devices, body(): tiles = lax.all_to_all(payload, PLANE, 0, 0, tiled=True)  12.4 us
    all_to_all x1, waiting for transfers between devices, body(): tiles = lax.all_to_all(payload, PLANE, 0, 0, tiled=True)  7.1 us
    all_to_all x1, starting transfers between devices, body(): columns = lax.all_to_all(after_rows, PLANE, 0, 0, tiled=True)  6.81 us
  transfers between devices with their start and end apart: 4, of which 3 were waited for; matrix products, arithmetic and copies ran while one was open for 1% of the time, Pallas kernels for 7%

profile of v6, /device:TPU:1, one launch (start us, length us, event | category | flops | bytes accessed | tf_op | source)
XLA Modules:
  0.0 228.2 jit_solution(4965854591158525540)
XLA Ops:
  0.0 3.3 %shard_map.155 = bf16[64,64,256]{2,1,0:T(8,128)(2,1)} custom-call(bf16[2048,128]{1,0:T(8,128)(2,1)} %bitcast.20, f32[1,128]{1,0:T(1,128)} %bitcast.23, bf16[8,128]{1,0:T(8,128)(2,1)} %weight_ref.1, s32[1,512]{1,0:T(1,128)} %bitcast.22, f32[1,8]{1,0:T(1,128)} %bitcast.24), custom_call_target="tpu_custom_call" | custom-call | tf_op jit(solution)/shard_map/pallas_call | solution.py:474
  3.3 0.0 copy-start.9
  3.3 12.4 %all-to-all-start = ((bf16[64,64,256]{2,1,0:T(8,128)(2,1)}), bf16[64,64,256]{2,1,0:T(8,128)(2,1)}, u32[]{:S(2)}, u32[]{:S(2)}) async-start(bf16[64,64,256]{2,1,0:T(8,128)(2,1)} %shard_map.155), calls=%async_computation | async-start | bytes 4194304 | tf_op jit(solution)/shard_map/all_to_all | solution.py:489
  15.7 1.0 collective-permute-start
  16.7 0.1 collective-permute-start.1
  16.9 1.1 copy.17
  17.9 0.7 slice.6.wk_ref
  18.6 0.3 collective-permute-done.1.other_mask_ref
  18.9 0.8 copy.18.mask_ref
  19.7 15.9 %shard_map.154 = (bf16[8,512,384]{2,1,0:T(8,128)(2,1)}, bf16[8,256,512]{2,1,0:T(8,128)(2,1)}, bf16[8,256,256]{2,1,0:T(8,128)(2,1)}, bf16[8,256,256]{2,1,0:T(8,12...) custom-call(bf16[4,512,256]{2,1,0:T(8,128)(2,1)} %own_ref.1, ...), custom_call_target="tpu_custom_call" | custom-call | flops 6442450944 | bytes 26214400 | tf_op jit(solution)/shard_map/pallas_call | solution.py:494
  35.6 7.1 %all-to-all-done.tile_ref = bf16[64,64,256]{2,1,0:T(8,128)(2,1)} async-done(((bf16[64,64,256]{2,1,0:T(8,128)(2,1)}), bf16[64,64,256]{2,1,0:T(8,128)(2,1)}, u32[]{:S(2)}, u32[]{:S(2)}) %all-to-all-start) | async-done | bytes 2097184 | tf_op jit(solution)/shard_map/all_to_all | solution.py:489
  42.7 78.9 %shard_map.156 = bf16[64,72,128]{2,1,0:T(8,128)(2,1)} custom-call(f32[8,8,128]{2,1,0:T(8,128)} %get-tuple-element.13.safe_ref, bf16[256,256]{1,0:T(8,128)(2,1)} %wo_ref.2, bf16[8,256]{1,0:T(8,128)(2,1)} %get-tuple-element.14.mask_ref, bf16[64,64,256]{2,1,0:T(8,128)(2,1)} %all-to-all-done.tile_ref, bf16[8,8,512,256]{3,2,1,0:T(8,128)(2,1)} %get-tuple-element.15.powers_ref, ...), custom_call_target="tpu_custom_call" | custom-call | flops 4294967296 | bytes 20971520 | tf_op jit(solution)/shard_map/pallas_call | solution.py:542
  121.6 0.0 copy-start.6
  121.6 0.0 copy-start
  121.6 0.0 copy-start.2
  121.6 0.0 copy-start.3
  121.7 6.8 %all-to-all-start.1 = ((bf16[64,72,128]{2,1,0:T(8,128)(2,1)}), bf16[64,72,128]{2,1,0:T(8,128)(2,1)S(1)}, u32[]{:S(2)}, u32[]{:S(2)}) async-start(bf16[64,72,128]{2,1,0:T(8,128)(2,1)} %shard_map.156), calls=%async_computation.1 | async-start | bytes 2359296 | tf_op jit(solution)/shard_map/all_to_all | solution.py:569
  128.5 0.2 copy.19
  128.7 16.9 %all-to-all-done.1.x_ref = bf16[64,72,128]{2,1,0:T(8,128)(2,1)S(1)} async-done(((bf16[64,72,128]{2,1,0:T(8,128)(2,1)}), bf16[64,72,128]{2,1,0:T(8,128)(2,1)S(1)}, u32[]{:S(2)}, u32[]{:S(2)}) %all-to-all-start.1) | async-done | bytes 1179680 | tf_op jit(solution)/shard_map/all_to_all | solution.py:569
  145.7 54.6 %shard_map.157 = bf16[2048,256]{1,0:T(8,128)(2,1)S(1)} custom-call(bf16[64,72,128]{2,1,0:T(8,128)(2,1)S(1)} %all-to-all-done.1.x_ref, f32[1,256]{1,0:T(1,128)S(1)} %bitcast.17, bf16[256,256]{1,0:T(8,128)(2,1)S(1)} %slice.7.wk_ref, bf16[1024,256]{1,0:T(8,128)(2,1)S(1)} %bitcast.16, bf16[256,256]{1,0:T(8,128)(2,1)S(1)} %copy-done.2, f32[1,256]{1,0:T(1,128)S(1)} %bitcast.18, ...), custom_call_target="tpu_custom_call" | custom-call | flops 8589934592 | bytes 4194304 | tf_op jit(solution)/shard_map/pallas_call | solution.py:571
  200.3 26.1 %all_to_all.15 = bf16[128,16,256]{2,1,0:T(8,128)(2,1)S(1)} all-to-all(bf16[128,16,256]{2,1,0:T(8,128)(2,1)S(1)} %bitcast.15), channel_id=1, replica_groups=mesh['grp'=2,'z'=4,'x'=4,'yh'=2,'core'=2] {'grp','z','x','yh','core'}, dimensions={0} | all-to-all | bytes 2097152 | tf_op jit(solution)/shard_map/all_to_all | solution.py:604
  226.4 0.3 reshape.38
  226.7 0.4 copy.22
  227.1 1.1 reshape.39
  (20 shorter events, 0.1 us)
Async XLA Ops:
  3.3 12.4 %copy-start.9 = (bf16[4,512,256]{2,1,0:T(8,128)(2,1)S(1)}, bf16[4,512,256]{2,1,0:T(8,128)(2,1)}, u32[]{:S(2)}) copy-start(bf16[4,512,256]{2,1,0:T(8,128)(2,1)} %own_ref.1) | copy-start | bytes 3145732
  3.3 13.5 %copy-start.7 = (s32[4,512]{1,0:T(4,128)S(1)}, s32[4,512]{1,0:T(4,128)}, u32[]{:S(2)}) copy-start(s32[4,512]{1,0:T(4,128)} %own_mask_ref.1) | copy-start | bytes 24580
  3.3 13.5 %copy-start.5 = (bf16[256,1024]{1,0:T(8,128)(2,1)S(1)}, bf16[256,1024]{1,0:T(8,128)(2,1)}, u32[]{:S(2)}) copy-start(bf16[256,1024]{1,0:T(8,128)(2,1)} %param.24) | copy-start | bytes 1572868
  3.3 39.4 %all-to-all-start = ((bf16[64,64,256]{2,1,0:T(8,128)(2,1)}), bf16[64,64,256]{2,1,0:T(8,128)(2,1)}, u32[]{:S(2)}, u32[]{:S(2)}) async-start(bf16[64,64,256]{2,1,0:T(8,128)(2,1)} %shard_map.155), calls=%async_computation | async-start | bytes 4194304 | tf_op jit(solution)/shard_map/all_to_all | solution.py:489
  15.7 4.0 %collective-permute-start = (bf16[4,512,256]{2,1,0:T(8,128)(2,1)S(1)}, bf16[4,512,256]{2,1,0:T(8,128)(2,1)}, u32[]{:S(2)}, u32[]{:S(2)}) collective-permute-start(bf16[4,512,256]{2,1,0:T(8,128)(2,1)S(1)} %copy-done.9), channel_id=1, source_target_pairs={{0,1},{1,0},{2,3},{3,2},{4,5},{5,4},{6,7},{7,6},{8,9},{9,8},{10,11... | collective-permute-start | bytes 3145736 | tf_op jit(solution)/shard_map/ppermute | solution.py:472
  16.7 2.2 collective-permute-start.1
  18.9 0.8 copy-start.8
  121.6 6.9 %copy-start.6 = (bf16[256,1024]{1,0:T(8,128)(2,1)S(1)}, bf16[256,1024]{1,0:T(8,128)(2,1)}, u32[]{:S(2)}) copy-start(bf16[256,1024]{1,0:T(8,128)(2,1)} %param.27) | copy-start | bytes 1572868
  121.6 24.0 %copy-start = (bf16[256,1024]{1,0:T(8,128)(2,1)S(1)}, bf16[256,1024]{1,0:T(8,128)(2,1)}, u32[]{:S(2)}) copy-start(bf16[256,1024]{1,0:T(8,128)(2,1)} %w1_ref.1) | copy-start | bytes 1572868
  121.6 24.0 %copy-start.1 = (bf16[1024,256]{1,0:T(8,128)(2,1)S(1)}, bf16[1024,256]{1,0:T(8,128)(2,1)}, u32[]{:S(2)}) copy-start(bf16[1024,256]{1,0:T(8,128)(2,1)} %w2_ref.1) | copy-start | bytes 1572868
  121.6 24.0 %copy-start.2 = (bf16[256,256]{1,0:T(8,128)(2,1)S(1)}, bf16[256,256]{1,0:T(8,128)(2,1)}, u32[]{:S(2)}) copy-start(bf16[256,256]{1,0:T(8,128)(2,1)} %wo_ref.3) | copy-start | bytes 393220
  121.6 24.0 %copy-start.3 = (f32[256]{0:T(256)S(1)}, f32[256]{0:T(256)}, u32[]{:S(2)}) copy-start(f32[256]{0:T(256)} %param.26) | copy-start | bytes 3076
  121.7 24.0 %copy-start.4 = (f32[256]{0:T(256)S(1)}, f32[256]{0:T(256)}, u32[]{:S(2)}) copy-start(f32[256]{0:T(256)} %param.29) | copy-start | bytes 3076
  121.7 24.0 %all-to-all-start.1 = ((bf16[64,72,128]{2,1,0:T(8,128)(2,1)}), bf16[64,72,128]{2,1,0:T(8,128)(2,1)S(1)}, u32[]{:S(2)}, u32[]{:S(2)}) async-start(bf16[64,72,128]{2,1,0:T(8,128)(2,1)} %shard_map.156), calls=%async_computation.1 | async-start | bytes 2359296 | tf_op jit(solution)/shard_map/all_to_all | solution.py:569

commit v7 on v6

--- a/solution.py
+++ b/solution.py
@@ -17,6 +17,7 @@
 LENGTH = 512
 HALF = 256
 PEERS = 64
+ROWS = 2048
 LOG2E = math.log2(math.e)
 SCALE = HEAD**-0.5 * LOG2E
 F32 = jnp.float32
@@ -332,7 +333,7 @@
 
     lax.fori_loop(0, 8, sequence, 0)
     for j in range(2):
-        result_ref[:, j * 32 : (j + 1) * 32, :] = y_ref[j].astype(BF16).reshape(PEERS, 32, 128)
+        result_ref[:, j * 32 : (j + 1) * 32, :] = y_ref[j, :ROWS].astype(BF16).reshape(PEERS, 32, 128)
         result_ref[j * 32 : (j + 1) * 32, 64:, :] = jnp.broadcast_to(
             mask_ref[:, j * 128 : (j + 1) * 128][None], (32, 8, 128)
         )
@@ -435,7 +436,7 @@
     for call in finishing(3):
         call()
     for j in range(2):
-        out_ref[:, j * 128 : (j + 1) * 128] = y_ref[j].astype(BF16)
+        out_ref[:, j * 128 : (j + 1) * 128] = y_ref[j, :ROWS].astype(BF16)
 
 
 def whole(*shape):
@@ -553,7 +554,7 @@
             pltpu.VMEM((HEADS, LENGTH, HALF), F32),
             pltpu.VMEM((HEADS, LENGTH, HALF), BF16),
             pltpu.VMEM((WIDTH, HALF), F32),
-            pltpu.VMEM((2, 8 * HALF, 128), F32),
+            pltpu.VMEM((2, ROWS + 8, 128), F32),
             pltpu.VMEM((PEERS, 72, 128), BF16),
             pltpu.VMEM((LENGTH, WIDTH + 128), BF16),
             pltpu.VMEM((WIDTH, HALF), BF16),
@@ -584,7 +585,7 @@
             pltpu.VMEM((4, WIDTH, LENGTH), BF16),
             pltpu.VMEM((LENGTH, WIDTH), F32),
             pltpu.VMEM((LENGTH, WIDTH), BF16),
-            pltpu.VMEM((2, 4 * LENGTH, 128), F32),
+            pltpu.VMEM((2, ROWS + 8, 128), F32),
         ],
         compiler_params=params,
         cost_estimate=pl.CostEstimate(

time: 229 us -> 229 us (level)
  no operation moved by 1% of the time
where the time goes in v7:
time: 229 us; the launch traced here: 228 us
  Pallas kernels  153 us (67%)
  blocking collectives  26.1 us (11%)
  waiting for transfers between devices  24.3 us (11%)
  starting transfers between devices  20.3 us (9%)
  local copies, waits for them, and re-layouts  4.58 us (2%)
    pallas_call x1, Pallas kernels, body(): pl.pallas_call(row_kernel, out_shape=jax.ShapeDtypeStruct((PEERS, 72, 128...  78.9 us
    pallas_call x1, Pallas kernels, body(): pl.pallas_call(column_kernel, out_shape=jax.ShapeDtypeStruct((4 * LENGTH,...  54.6 us
    all_to_all x1, blocking collectives, body(): lax.all_to_all(finished.reshape(128, 16, WIDTH), AXES, 0, 0, tiled=True)  26.1 us
    all_to_all x1, waiting for transfers between devices, body(): columns = lax.all_to_all(after_rows, PLANE, 0, 0, tiled=True)  16.9 us
    pallas_call x1, Pallas kernels, body(): pl.pallas_call(project_kernel, grid=(8,), out_shape=[jax.ShapeDtypeStruct...  15.9 us
    all_to_all x1, starting transfers between devices, body(): tiles = lax.all_to_all(payload, PLANE, 0, 0, tiled=True)  12.4 us
    all_to_all x1, waiting for transfers between devices, body(): tiles = lax.all_to_all(payload, PLANE, 0, 0, tiled=True)  7.1 us
    all_to_all x1, starting transfers between devices, body(): columns = lax.all_to_all(after_rows, PLANE, 0, 0, tiled=True)  6.81 us
  transfers between devices with their start and end apart: 4, of which 3 were waited for; matrix products, arithmetic and copies ran while one was open for 1% of the time, Pallas kernels for 7%

profile of v7, /device:TPU:1, one launch (start us, length us, event | category | flops | bytes accessed | tf_op | source)
XLA Modules:
  0.0 228.2 jit_solution(14817862536276474511)
XLA Ops:
  0.0 3.3 %shard_map.155 = bf16[64,64,256]{2,1,0:T(8,128)(2,1)} custom-call(bf16[2048,128]{1,0:T(8,128)(2,1)} %bitcast.20, f32[1,128]{1,0:T(1,128)} %bitcast.23, bf16[8,128]{1,0:T(8,128)(2,1)} %weight_ref.1, s32[1,512]{1,0:T(1,128)} %bitcast.22, f32[1,8]{1,0:T(1,128)} %bitcast.24), custom_call_target="tpu_custom_call" | custom-call | tf_op jit(solution)/shard_map/pallas_call | solution.py:475
  3.3 0.0 copy-start.9
  3.3 12.4 %all-to-all-start = ((bf16[64,64,256]{2,1,0:T(8,128)(2,1)}), bf16[64,64,256]{2,1,0:T(8,128)(2,1)}, u32[]{:S(2)}, u32[]{:S(2)}) async-start(bf16[64,64,256]{2,1,0:T(8,128)(2,1)} %shard_map.155), calls=%async_computation | async-start | bytes 4194304 | tf_op jit(solution)/shard_map/all_to_all | solution.py:490
  15.7 1.0 collective-permute-start
  16.7 0.1 collective-permute-start.1
  16.9 1.1 copy.17
  17.9 0.7 slice.6.wk_ref
  18.6 0.3 collective-permute-done.1.other_mask_ref
  18.9 0.8 copy.18.mask_ref
  19.7 15.9 %shard_map.154 = (bf16[8,512,384]{2,1,0:T(8,128)(2,1)}, bf16[8,256,512]{2,1,0:T(8,128)(2,1)}, bf16[8,256,256]{2,1,0:T(8,128)(2,1)}, bf16[8,256,256]{2,1,0:T(8,12...) custom-call(bf16[4,512,256]{2,1,0:T(8,128)(2,1)} %own_ref.1, ...), custom_call_target="tpu_custom_call" | custom-call | flops 6442450944 | bytes 26214400 | tf_op jit(solution)/shard_map/pallas_call | solution.py:495
  35.6 7.1 %all-to-all-done.tile_ref = bf16[64,64,256]{2,1,0:T(8,128)(2,1)} async-done(((bf16[64,64,256]{2,1,0:T(8,128)(2,1)}), bf16[64,64,256]{2,1,0:T(8,128)(2,1)}, u32[]{:S(2)}, u32[]{:S(2)}) %all-to-all-start) | async-done | bytes 2097184 | tf_op jit(solution)/shard_map/all_to_all | solution.py:490
  42.7 78.9 %shard_map.156 = bf16[64,72,128]{2,1,0:T(8,128)(2,1)} custom-call(f32[8,8,128]{2,1,0:T(8,128)} %get-tuple-element.13.safe_ref, bf16[256,256]{1,0:T(8,128)(2,1)} %wo_ref.2, bf16[8,256]{1,0:T(8,128)(2,1)} %get-tuple-element.14.mask_ref, bf16[64,64,256]{2,1,0:T(8,128)(2,1)} %all-to-all-done.tile_ref, bf16[8,8,512,256]{3,2,1,0:T(8,128)(2,1)} %get-tuple-element.15.powers_ref, ...), custom_call_target="tpu_custom_call" | custom-call | flops 4294967296 | bytes 20971520 | tf_op jit(solution)/shard_map/pallas_call | solution.py:543
  121.6 0.0 copy-start
  121.6 0.0 copy-start.1
  121.6 0.0 copy-start.3
  121.7 0.0 copy-start.4
  121.7 6.8 %all-to-all-start.1 = ((bf16[64,72,128]{2,1,0:T(8,128)(2,1)}), bf16[64,72,128]{2,1,0:T(8,128)(2,1)S(1)}, u32[]{:S(2)}, u32[]{:S(2)}) async-start(bf16[64,72,128]{2,1,0:T(8,128)(2,1)} %shard_map.156), calls=%async_computation.1 | async-start | bytes 2359296 | tf_op jit(solution)/shard_map/all_to_all | solution.py:570
  128.5 0.2 copy.19
  128.7 16.9 %all-to-all-done.1.x_ref = bf16[64,72,128]{2,1,0:T(8,128)(2,1)S(1)} async-done(((bf16[64,72,128]{2,1,0:T(8,128)(2,1)}), bf16[64,72,128]{2,1,0:T(8,128)(2,1)S(1)}, u32[]{:S(2)}, u32[]{:S(2)}) %all-to-all-start.1) | async-done | bytes 1179680 | tf_op jit(solution)/shard_map/all_to_all | solution.py:570
  145.7 54.6 %shard_map.157 = bf16[2048,256]{1,0:T(8,128)(2,1)S(1)} custom-call(bf16[64,72,128]{2,1,0:T(8,128)(2,1)S(1)} %all-to-all-done.1.x_ref, f32[1,256]{1,0:T(1,128)S(1)} %bitcast.17, bf16[256,256]{1,0:T(8,128)(2,1)S(1)} %slice.7.wk_ref, bf16[1024,256]{1,0:T(8,128)(2,1)S(1)} %bitcast.16, bf16[256,256]{1,0:T(8,128)(2,1)S(1)} %copy-done.2, f32[1,256]{1,0:T(1,128)S(1)} %bitcast.18, ...), custom_call_target="tpu_custom_call" | custom-call | flops 8589934592 | bytes 4194304 | tf_op jit(solution)/shard_map/pallas_call | solution.py:572
  200.3 26.1 %all_to_all.15 = bf16[128,16,256]{2,1,0:T(8,128)(2,1)S(1)} all-to-all(bf16[128,16,256]{2,1,0:T(8,128)(2,1)S(1)} %bitcast.15), channel_id=1, replica_groups=mesh['grp'=2,'z'=4,'x'=4,'yh'=2,'core'=2] {'grp','z','x','yh','core'}, dimensions={0} | all-to-all | bytes 2097152 | tf_op jit(solution)/shard_map/all_to_all | solution.py:605
  226.4 0.3 reshape.38
  226.7 0.4 copy.22
  227.1 1.1 reshape.39
  (20 shorter events, 0.1 us)
Async XLA Ops:
  3.3 12.4 %copy-start.9 = (bf16[4,512,256]{2,1,0:T(8,128)(2,1)S(1)}, bf16[4,512,256]{2,1,0:T(8,128)(2,1)}, u32[]{:S(2)}) copy-start(bf16[4,512,256]{2,1,0:T(8,128)(2,1)} %own_ref.1) | copy-start | bytes 3145732
  3.3 13.5 %copy-start.7 = (s32[4,512]{1,0:T(4,128)S(1)}, s32[4,512]{1,0:T(4,128)}, u32[]{:S(2)}) copy-start(s32[4,512]{1,0:T(4,128)} %own_mask_ref.1) | copy-start | bytes 24580
  3.3 13.5 %copy-start.5 = (bf16[256,1024]{1,0:T(8,128)(2,1)S(1)}, bf16[256,1024]{1,0:T(8,128)(2,1)}, u32[]{:S(2)}) copy-start(bf16[256,1024]{1,0:T(8,128)(2,1)} %param.24) | copy-start | bytes 1572868
  3.3 39.4 %all-to-all-start = ((bf16[64,64,256]{2,1,0:T(8,128)(2,1)}), bf16[64,64,256]{2,1,0:T(8,128)(2,1)}, u32[]{:S(2)}, u32[]{:S(2)}) async-start(bf16[64,64,256]{2,1,0:T(8,128)(2,1)} %shard_map.155), calls=%async_computation | async-start | bytes 4194304 | tf_op jit(solution)/shard_map/all_to_all | solution.py:490
  15.7 4.0 %collective-permute-start = (bf16[4,512,256]{2,1,0:T(8,128)(2,1)S(1)}, bf16[4,512,256]{2,1,0:T(8,128)(2,1)}, u32[]{:S(2)}, u32[]{:S(2)}) collective-permute-start(bf16[4,512,256]{2,1,0:T(8,128)(2,1)S(1)} %copy-done.9), channel_id=1, source_target_pairs={{0,1},{1,0},{2,3},{3,2},{4,5},{5,4},{6,7},{7,6},{8,9},{9,8},{10,11... | collective-permute-start | bytes 3145736 | tf_op jit(solution)/shard_map/ppermute | solution.py:473
  16.7 2.2 collective-permute-start.1
  18.9 0.8 copy-start.8
  121.6 6.9 %copy-start.6 = (bf16[256,1024]{1,0:T(8,128)(2,1)S(1)}, bf16[256,1024]{1,0:T(8,128)(2,1)}, u32[]{:S(2)}) copy-start(bf16[256,1024]{1,0:T(8,128)(2,1)} %param.27) | copy-start | bytes 1572868
  121.6 24.0 %copy-start = (bf16[256,1024]{1,0:T(8,128)(2,1)S(1)}, bf16[256,1024]{1,0:T(8,128)(2,1)}, u32[]{:S(2)}) copy-start(bf16[256,1024]{1,0:T(8,128)(2,1)} %w1_ref.1) | copy-start | bytes 1572868
  121.6 24.0 %copy-start.1 = (bf16[1024,256]{1,0:T(8,128)(2,1)S(1)}, bf16[1024,256]{1,0:T(8,128)(2,1)}, u32[]{:S(2)}) copy-start(bf16[1024,256]{1,0:T(8,128)(2,1)} %w2_ref.1) | copy-start | bytes 1572868
  121.6 24.0 %copy-start.2 = (bf16[256,256]{1,0:T(8,128)(2,1)S(1)}, bf16[256,256]{1,0:T(8,128)(2,1)}, u32[]{:S(2)}) copy-start(bf16[256,256]{1,0:T(8,128)(2,1)} %wo_ref.3) | copy-start | bytes 393220
  121.6 24.0 %copy-start.3 = (f32[256]{0:T(256)S(1)}, f32[256]{0:T(256)}, u32[]{:S(2)}) copy-start(f32[256]{0:T(256)} %param.26) | copy-start | bytes 3076
  121.7 24.0 %copy-start.4 = (f32[256]{0:T(256)S(1)}, f32[256]{0:T(256)}, u32[]{:S(2)}) copy-start(f32[256]{0:T(256)} %param.29) | copy-start | bytes 3076
  121.7 24.0 %all-to-all-start.1 = ((bf16[64,72,128]{2,1,0:T(8,128)(2,1)}), bf16[64,72,128]{2,1,0:T(8,128)(2,1)S(1)}, u32[]{:S(2)}, u32[]{:S(2)}) async-start(bf16[64,72,128]{2,1,0:T(8,128)(2,1)} %shard_map.156), calls=%async_computation.1 | async-start | bytes 2359296 | tf_op jit(solution)/shard_map/all_to_all | solution.py:570

commit v8 on v7

--- a/solution.py
+++ b/solution.py
@@ -124,14 +124,18 @@
     feat_t = lax.broadcasted_iota(jnp.int32, (16, WIDTH), 1) // HEAD
     row_t = lax.broadcasted_iota(jnp.int32, (16, WIDTH), 0)
     ones_t = (feat_t == row_t).astype(F32).astype(BF16)
-    key_norm = jnp.max(nn(keys * keys, ones))
-    query_norm = jnp.max(nn(ones_t, qt * qt))
+    key_norm = most(nn(keys * keys, ones))
+    query_norm = most(nn(ones_t, qt * qt))
     return jnp.sqrt(key_norm * 1.02) * jnp.sqrt(query_norm * 1.02) * SCALE
+
+
+def most(a):
+    return jnp.max(jnp.max(a, axis=0, keepdims=True), axis=1, keepdims=True)
 
 
 def any_present(tile):
     lane = lax.broadcasted_iota(jnp.int32, tile.shape, 1)
-    return jnp.max(jnp.where(lane == 0, tile, -1e30)) > -1.0
+    return most(jnp.where(lane == 0, tile, -1e30)) > -1.0
 
 
 def score_powers(keys, mask_tile, qt):
@@ -344,11 +348,12 @@
 
 def column_kernel(
     x_ref, gain_ref, wk_ref, wt_ref, wo_ref, gain2_ref, w1_ref, w2_ref, out_ref,
-    x32_ref, keys_ref, tile_ref, vt_ref, qt_ref, gt_ref, o_ref, total_ref, normed_ref, y_ref,
+    x32_ref, absent_ref, bad_ref, entered_ref, keys_ref, tile_ref, vt_ref, qt_ref, gt_ref, o_ref,
+    total_ref, normed_ref, y_ref,
 ):
     _, q, _ = position()
     x32_ref[...] = x_ref[...].astype(F32).reshape(PEERS, 9, 8, 128)
-    absent = (x32_ref[:, 8].reshape(LENGTH, 128) - 1.0).astype(BF16)
+    absent_ref[...] = (x32_ref[:, 8].reshape(LENGTH, 128) - 1.0).astype(BF16)
     lane = lax.broadcasted_iota(jnp.int32, (128, 128), 1)
     row = lax.broadcasted_iota(jnp.int32, (128, 128), 0)
 
@@ -358,21 +363,36 @@
         ]
         return jnp.concatenate(halves, axis=1)
 
-    safe = jnp.bool_(True)
-    for r in range(4):
-        normed = norm(residue_rows(r, 0, PEERS), gain_ref[...])
-        keys = nn(normed, wk_ref[...]).astype(BF16)
-        keys_ref[r] = keys
+    bad_ref[...] = jnp.zeros((1, 128), F32)
+
+    def enter(r):
+        entered_ref[r] = norm(residue_rows(r, 0, PEERS), gain_ref[...])
+
+    def project_keys(r):
+        keys_ref[r] = nn(entered_ref[r], wk_ref[...]).astype(BF16)
+
+    def project_others(r, part, ref):
+        weight = wt_ref[part * WIDTH : (part + 1) * WIDTH]
+        ref[r] = nt(weight, entered_ref[r]).astype(BF16)
+
+    def check(r):
         pick = jnp.zeros((128, 128), F32)
         for at, value in enumerate(mask_parts()):
             pick = jnp.where((lane == at) & (row == 4 * q + r), value, pick)
-        tile = nn(absent, pick.astype(BF16))
+        tile = nn(absent_ref[...], pick.astype(BF16))
         tile_ref[r] = tile.astype(BF16)
-        vt_ref[r] = nt(wt_ref[2 * WIDTH : 3 * WIDTH], normed).astype(BF16)
-        qt = nt(wt_ref[:WIDTH], normed).astype(BF16)
-        qt_ref[r] = qt
-        gt_ref[r] = nt(wt_ref[3 * WIDTH :], normed).astype(BF16)
-        safe = safe & (score_bound(keys, qt) <= COLUMN_BOUND) & any_present(tile)
+        safe = (score_bound(keys_ref[r], qt_ref[r]) <= COLUMN_BOUND) & any_present(tile)
+        bad_ref[...] = jnp.maximum(bad_ref[...], jnp.where(safe, 0.0, 1.0))
+
+    def preparing(r):
+        return [
+            functools.partial(enter, r),
+            functools.partial(project_keys, r),
+            functools.partial(project_others, r, 0, qt_ref),
+            functools.partial(check, r),
+            functools.partial(project_others, r, 2, vt_ref),
+            functools.partial(project_others, r, 3, gt_ref),
+        ]
 
     def attention(r, between=()):
         parts = [
@@ -406,35 +426,27 @@
         blocks = [functools.partial(transition, part) for part in range(4)]
         return [functools.partial(project_out, r), normalize] + blocks + [functools.partial(keep, r)]
 
-    @pl.when(safe)
-    def _():
-        attention(0)
-
-        def residue(r, carry):
-            attention(r, finishing(r - 1))
-            return carry
-
-        lax.fori_loop(1, 4, residue, 0)
-
-    @pl.when(jnp.logical_not(safe))
+    for call in preparing(0):
+        call()
+    for r in range(4):
+        before = finishing(r - 1) if r else []
+        after = preparing(r + 1) if r < 3 else []
+        attention(r, before + after)
+    for call in finishing(3):
+        call()
+
+    @pl.when(jnp.max(bad_ref[...]) > 0.5)
     def _():
         def residue(r, carry):
             for n in range(2):
                 queries = qt_ref[r, :, n * HALF : (n + 1) * HALF]
                 gate(r, n, attend_exact(keys_ref[r], tile_ref[r], vt_ref[r], queries, None))
-            return carry
-
-        lax.fori_loop(0, 4, residue, 0)
-
-        def rest(r, carry):
             for call in finishing(r):
                 call()
             return carry
 
-        lax.fori_loop(0, 3, rest, 0)
-
-    for call in finishing(3):
-        call()
+        lax.fori_loop(0, 4, residue, 0)
+
     for j in range(2):
         out_ref[:, j * 128 : (j + 1) * 128] = y_ref[j, :ROWS].astype(BF16)
 
@@ -577,6 +589,9 @@
         out_specs=whole(4 * LENGTH, WIDTH),
         scratch_shapes=[
             pltpu.VMEM((PEERS, 9, 8, 128), F32),
+            pltpu.VMEM((LENGTH, 128), BF16),
+            pltpu.VMEM((1, 128), F32),
+            pltpu.VMEM((4, LENGTH, WIDTH), BF16),
             pltpu.VMEM((4, LENGTH, WIDTH), BF16),
             pltpu.VMEM((4, LENGTH, 128), BF16),
             pltpu.VMEM((4, WIDTH, LENGTH), BF16),

time: 229 us -> 240 us (1.048)
  Pallas kernels: 153 us -> 163 us
    pallas_call x1, Pallas kernels: 54.6 us -> 65.2 us  [body(): pl.pallas_call(column_kernel, out_shape=jax.ShapeDtypeStruct((4 * LENGTH,...]
  transfers between devices with their start and end apart: 4 -> 4, of which waited for: 3 -> 3; matrix products, arithmetic and copies ran while one was open for 1% -> 1% of each run, Pallas kernels for 7% -> 6%
where the time goes in v8:
time: 240 us; the launch traced here: 239 us
  Pallas kernels  163 us (68%)
  blocking collectives  26.1 us (11%)
  waiting for transfers between devices  24.6 us (10%)
  starting transfers between devices  20.5 us (9%)
  local copies, waits for them, and re-layouts  4.58 us (2%)
    pallas_call x1, Pallas kernels, body(): pl.pallas_call(row_kernel, out_shape=jax.ShapeDtypeStruct((PEERS, 72, 128...  78.9 us
    pallas_call x1, Pallas kernels, body(): pl.pallas_call(column_kernel, out_shape=jax.ShapeDtypeStruct((4 * LENGTH,...  65.2 us
    all_to_all x1, blocking collectives, body(): lax.all_to_all(finished.reshape(128, 16, WIDTH), AXES, 0, 0, tiled=True)  26.1 us
    all_to_all x1, waiting for transfers between devices, body(): columns = lax.all_to_all(after_rows, PLANE, 0, 0, tiled=True)  16.7 us
    pallas_call x1, Pallas kernels, body(): pl.pallas_call(project_kernel, grid=(8,), out_shape=[jax.ShapeDtypeStruct...  15.4 us
    all_to_all x1, starting transfers between devices, body(): tiles = lax.all_to_all(payload, PLANE, 0, 0, tiled=True)  12.4 us
    all_to_all x1, waiting for transfers between devices, body(): tiles = lax.all_to_all(payload, PLANE, 0, 0, tiled=True)  7.57 us
    all_to_all x1, starting transfers between devices, body(): columns = lax.all_to_all(after_rows, PLANE, 0, 0, tiled=True)  6.99 us
  transfers between devices with their start and end apart: 4, of which 3 were waited for; matrix products, arithmetic and copies ran while one was open for 1% of the time, Pallas kernels for 6%

profile of v8, /device:TPU:1, one launch (start us, length us, event | category | flops | bytes accessed | tf_op | source)
XLA Modules:
  0.0 238.7 jit_solution(16517307131286506660)
XLA Ops:
  0.0 3.3 %shard_map.155 = bf16[64,64,256]{2,1,0:T(8,128)(2,1)} custom-call(bf16[2048,128]{1,0:T(8,128)(2,1)} %bitcast.20, f32[1,128]{1,0:T(1,128)} %bitcast.23, bf16[8,128]{1,0:T(8,128)(2,1)} %weight_ref.1, s32[1,512]{1,0:T(1,128)} %bitcast.22, f32[1,8]{1,0:T(1,128)} %bitcast.24), custom_call_target="tpu_custom_call" | custom-call | tf_op jit(solution)/shard_map/pallas_call | solution.py:487
  3.3 0.0 copy-start.9
  3.3 12.4 %all-to-all-start = ((bf16[64,64,256]{2,1,0:T(8,128)(2,1)}), bf16[64,64,256]{2,1,0:T(8,128)(2,1)}, u32[]{:S(2)}, u32[]{:S(2)}) async-start(bf16[64,64,256]{2,1,0:T(8,128)(2,1)} %shard_map.155), calls=%async_computation | async-start | bytes 4194304 | tf_op jit(solution)/shard_map/all_to_all | solution.py:502
  15.7 1.0 collective-permute-start
  16.7 0.1 collective-permute-start.1
  16.9 1.1 copy.17
  17.9 0.7 slice.6.wk_ref
  18.6 0.3 collective-permute-done.1.other_mask_ref
  18.9 0.8 copy.18.mask_ref
  19.7 15.4 %shard_map.154 = (bf16[8,512,384]{2,1,0:T(8,128)(2,1)}, bf16[8,256,512]{2,1,0:T(8,128)(2,1)}, bf16[8,256,256]{2,1,0:T(8,128)(2,1)}, bf16[8,256,256]{2,1,0:T(8,12...) custom-call(bf16[4,512,256]{2,1,0:T(8,128)(2,1)} %own_ref.1, ...), custom_call_target="tpu_custom_call" | custom-call | flops 6442450944 | bytes 26214400 | tf_op jit(solution)/shard_map/pallas_call | solution.py:507
  35.2 7.6 %all-to-all-done.tile_ref = bf16[64,64,256]{2,1,0:T(8,128)(2,1)} async-done(((bf16[64,64,256]{2,1,0:T(8,128)(2,1)}), bf16[64,64,256]{2,1,0:T(8,128)(2,1)}, u32[]{:S(2)}, u32[]{:S(2)}) %all-to-all-start) | async-done | bytes 2097184 | tf_op jit(solution)/shard_map/all_to_all | solution.py:502
  42.7 78.9 %shard_map.156 = bf16[64,72,128]{2,1,0:T(8,128)(2,1)} custom-call(f32[8,8,128]{2,1,0:T(8,128)} %get-tuple-element.13.safe_ref, bf16[256,256]{1,0:T(8,128)(2,1)} %wo_ref.2, bf16[8,256]{1,0:T(8,128)(2,1)} %get-tuple-element.14.mask_ref, bf16[64,64,256]{2,1,0:T(8,128)(2,1)} %all-to-all-done.tile_ref, bf16[8,8,512,256]{3,2,1,0:T(8,128)(2,1)} %get-tuple-element.15.powers_ref, ...), custom_call_target="tpu_custom_call" | custom-call | flops 4294967296 | bytes 20971520 | tf_op jit(solution)/shard_map/pallas_call | solution.py:555
  121.6 0.0 copy-start
  121.6 0.0 copy-start.1
  121.6 0.0 copy-start.3
  121.7 0.0 copy-start.4
  121.7 7.0 %all-to-all-start.1 = ((bf16[64,72,128]{2,1,0:T(8,128)(2,1)}), bf16[64,72,128]{2,1,0:T(8,128)(2,1)S(1)}, u32[]{:S(2)}, u32[]{:S(2)}) async-start(bf16[64,72,128]{2,1,0:T(8,128)(2,1)} %shard_map.156), calls=%async_computation.1 | async-start | bytes 2359296 | tf_op jit(solution)/shard_map/all_to_all | solution.py:582
  128.7 0.2 copy.19
  128.9 16.7 %all-to-all-done.1.x_ref = bf16[64,72,128]{2,1,0:T(8,128)(2,1)S(1)} async-done(((bf16[64,72,128]{2,1,0:T(8,128)(2,1)}), bf16[64,72,128]{2,1,0:T(8,128)(2,1)S(1)}, u32[]{:S(2)}, u32[]{:S(2)}) %all-to-all-start.1) | async-done | bytes 1179680 | tf_op jit(solution)/shard_map/all_to_all | solution.py:582
  145.7 65.2 %shard_map.157 = bf16[2048,256]{1,0:T(8,128)(2,1)S(1)} custom-call(bf16[64,72,128]{2,1,0:T(8,128)(2,1)S(1)} %all-to-all-done.1.x_ref, f32[1,256]{1,0:T(1,128)S(1)} %bitcast.17, bf16[256,256]{1,0:T(8,128)(2,1)S(1)} %slice.7.wk_ref, bf16[1024,256]{1,0:T(8,128)(2,1)S(1)} %bitcast.16, bf16[256,256]{1,0:T(8,128)(2,1)S(1)} %copy-done.2, f32[1,256]{1,0:T(1,128)S(1)} %bitcast.18, ...), custom_call_target="tpu_custom_call" | custom-call | flops 8589934592 | bytes 4194304 | tf_op jit(solution)/shard_map/pallas_call | solution.py:584
  210.8 26.1 %all_to_all.15 = bf16[128,16,256]{2,1,0:T(8,128)(2,1)S(1)} all-to-all(bf16[128,16,256]{2,1,0:T(8,128)(2,1)S(1)} %bitcast.15), channel_id=1, replica_groups=mesh['grp'=2,'z'=4,'x'=4,'yh'=2,'core'=2] {'grp','z','x','yh','core'}, dimensions={0} | all-to-all | bytes 2097152 | tf_op jit(solution)/shard_map/all_to_all | solution.py:620
  237.0 0.3 reshape.38
  237.2 0.4 copy.22
  237.6 1.1 reshape.39
  (20 shorter events, 0.1 us)
Async XLA Ops:
  3.3 12.4 %copy-start.9 = (bf16[4,512,256]{2,1,0:T(8,128)(2,1)S(1)}, bf16[4,512,256]{2,1,0:T(8,128)(2,1)}, u32[]{:S(2)}) copy-start(bf16[4,512,256]{2,1,0:T(8,128)(2,1)} %own_ref.1) | copy-start | bytes 3145732
  3.3 13.5 %copy-start.7 = (s32[4,512]{1,0:T(4,128)S(1)}, s32[4,512]{1,0:T(4,128)}, u32[]{:S(2)}) copy-start(s32[4,512]{1,0:T(4,128)} %own_mask_ref.1) | copy-start | bytes 24580
  3.3 13.5 %copy-start.5 = (bf16[256,1024]{1,0:T(8,128)(2,1)S(1)}, bf16[256,1024]{1,0:T(8,128)(2,1)}, u32[]{:S(2)}) copy-start(bf16[256,1024]{1,0:T(8,128)(2,1)} %param.24) | copy-start | bytes 1572868
  3.3 39.4 %all-to-all-start = ((bf16[64,64,256]{2,1,0:T(8,128)(2,1)}), bf16[64,64,256]{2,1,0:T(8,128)(2,1)}, u32[]{:S(2)}, u32[]{:S(2)}) async-start(bf16[64,64,256]{2,1,0:T(8,128)(2,1)} %shard_map.155), calls=%async_computation | async-start | bytes 4194304 | tf_op jit(solution)/shard_map/all_to_all | solution.py:502
  15.7 4.0 %collective-permute-start = (bf16[4,512,256]{2,1,0:T(8,128)(2,1)S(1)}, bf16[4,512,256]{2,1,0:T(8,128)(2,1)}, u32[]{:S(2)}, u32[]{:S(2)}) collective-permute-start(bf16[4,512,256]{2,1,0:T(8,128)(2,1)S(1)} %copy-done.9), channel_id=1, source_target_pairs={{0,1},{1,0},{2,3},{3,2},{4,5},{5,4},{6,7},{7,6},{8,9},{9,8},{10,11... | collective-permute-start | bytes 3145736 | tf_op jit(solution)/shard_map/ppermute | solution.py:485
  16.7 2.2 collective-permute-start.1
  18.9 0.8 copy-start.8
  121.6 7.1 %copy-start.6 = (bf16[256,1024]{1,0:T(8,128)(2,1)S(1)}, bf16[256,1024]{1,0:T(8,128)(2,1)}, u32[]{:S(2)}) copy-start(bf16[256,1024]{1,0:T(8,128)(2,1)} %param.27) | copy-start | bytes 1572868
  121.6 24.0 %copy-start = (bf16[256,1024]{1,0:T(8,128)(2,1)S(1)}, bf16[256,1024]{1,0:T(8,128)(2,1)}, u32[]{:S(2)}) copy-start(bf16[256,1024]{1,0:T(8,128)(2,1)} %w1_ref.1) | copy-start | bytes 1572868
  121.6 24.0 %copy-start.1 = (bf16[1024,256]{1,0:T(8,128)(2,1)S(1)}, bf16[1024,256]{1,0:T(8,128)(2,1)}, u32[]{:S(2)}) copy-start(bf16[1024,256]{1,0:T(8,128)(2,1)} %w2_ref.1) | copy-start | bytes 1572868
  121.6 24.0 %copy-start.2 = (bf16[256,256]{1,0:T(8,128)(2,1)S(1)}, bf16[256,256]{1,0:T(8,128)(2,1)}, u32[]{:S(2)}) copy-start(bf16[256,256]{1,0:T(8,128)(2,1)} %wo_ref.3) | copy-start | bytes 393220
  121.6 24.0 %copy-start.3 = (f32[256]{0:T(256)S(1)}, f32[256]{0:T(256)}, u32[]{:S(2)}) copy-start(f32[256]{0:T(256)} %param.26) | copy-start | bytes 3076
  121.7 24.0 %copy-start.4 = (f32[256]{0:T(256)S(1)}, f32[256]{0:T(256)}, u32[]{:S(2)}) copy-start(f32[256]{0:T(256)} %param.29) | copy-start | bytes 3076
  121.7 24.0 %all-to-all-start.1 = ((bf16[64,72,128]{2,1,0:T(8,128)(2,1)}), bf16[64,72,128]{2,1,0:T(8,128)(2,1)S(1)}, u32[]{:S(2)}, u32[]{:S(2)}) async-start(bf16[64,72,128]{2,1,0:T(8,128)(2,1)} %shard_map.156), calls=%async_computation.1 | async-start | bytes 2359296 | tf_op jit(solution)/shard_map/all_to_all | solution.py:582
